TPU v7x, 32 devices: a whole 2x2x4 slice. The times are simulated.
32 devices in a mesh: dp: 8 (over z, y), tensor: 4 (over x, core).
Axes of the slice: x: 2, y: 2, z: 4, core: 2. Of those that a mesh axis runs over, the one named last changes fastest.
Arguments:
- tokens: bfloat16 [8192, 2048], P('dp'), may hold values from -6 to 6
- segments: int32 [8192], P('dp'), may hold values from 0 to 7, as said below
- pad_mask: int32 [8192], P('dp'), may hold values from 0 to 1, as said below
- w_query: bfloat16 [2048, 2048], P(None, 'tensor'), may hold values from -0.125 to 0.125
- w_key: bfloat16 [2048, 2048], P(None, 'tensor'), may hold values from -0.125 to 0.125
- w_value: bfloat16 [2048, 2048], P(None, 'tensor'), may hold values from -0.125 to 0.125
- w_out: bfloat16 [2048, 2048], P('tensor'), may hold values from -0.125 to 0.125
- gain_query: bfloat16 [16, 128], P('tensor'), may hold values from 0.25 to 1.75
- gain_key: bfloat16 [16, 128], P('tensor'), may hold values from 0.25 to 1.75
- gain_attn: bfloat16 [2048], replicated, may hold values from 0.25 to 1.75
- w_gate: bfloat16 [2048, 8192], P(None, 'tensor'), may hold values from -0.125 to 0.125
- w_up: bfloat16 [2048, 8192], P(None, 'tensor'), may hold values from -0.125 to 0.125
- w_down: bfloat16 [8192, 2048], P('tensor'), may hold values from -0.0625 to 0.0625
- gain_mlp: bfloat16 [2048], replicated, may hold values from 0.25 to 1.75
- cotangent: bfloat16 [8192, 2048], P('dp'), may hold values from -6 to 6
Outputs:
- output: bfloat16 [8192, 2048], P('dp')
- grad_tokens: bfloat16 [8192, 2048], P('dp')
- grad_query: float32 [2048, 2048], P('dp', 'tensor')
- grad_key: float32 [2048, 2048], P('dp', 'tensor')
- grad_value: float32 [2048, 2048], P('dp', 'tensor')
- grad_out: float32 [2048, 2048], P('tensor', 'dp')
- grad_gain_query: float32 [16, 128], P('tensor', 'dp')
- grad_gain_key: float32 [16, 128], P('tensor', 'dp')
- grad_gain_attn: float32 [2048], P('dp')
- grad_gate: float32 [2048, 8192], P('dp', 'tensor')
- grad_up: float32 [2048, 8192], P('dp', 'tensor')
- grad_down: float32 [8192, 2048], P('tensor', 'dp')
- grad_gain_mlp: float32 [2048], P('dp')
Inputs may be any that keep to these rules, and one draw needn't show every extreme that they name: `segments`: within each packed sequence of 1024 rows the numbers start at 0, never fall, and end at 7; a document is a run of one number. `pad_mask`: in each packed sequence of 1024 rows the ones come first, then 1 to 256 pad slots.
All inputs are finite; a program needn't handle non-finite values.
Results may differ from a plain program's by a relative error of at most 0.017.
Values sent between devices are 32-bit elements; how exact they have to be, the bound alone decides.
A program may use at most 320 MiB of HBM per device.

v0:
```python
import jax
import jax.numpy as jnp
from jax import lax
from jax.sharding import PartitionSpec as P

HEAD = 128
LENGTH = 1024


EPSILON = 1e-06
NEG_FILL = -1e30
ROPE_BASE = 500000.0


def outer_sum(left, right):
    return lax.dot_general(
        left, right, (((0,), (0,)), ((), ())), preferred_element_type=jnp.float32
    )


def back_product(left, right):
    return lax.dot_general(
        left, right, (((1,), (1,)), ((), ())), preferred_element_type=jnp.float32
    )


def rope_tables():
    half_size = HEAD // 2
    freq_row = ROPE_BASE ** (-(jnp.arange(half_size, dtype=jnp.float32) * 2.0) / HEAD)
    angle = jnp.arange(LENGTH, dtype=jnp.float32)[:, None] * freq_row[None, :]
    return (jnp.cos(angle), jnp.sin(angle))


def rotate(values, cosine, sine_part, direction):
    row_count, col_count = values.shape
    half_size = HEAD // 2
    split = values.reshape(row_count // LENGTH, LENGTH, col_count // HEAD, 2, half_size)
    first = split[:, :, :, 0]
    second = split[:, :, :, 1]
    cos_b = cosine[None, :, None, :]
    sin_b = direction * sine_part[None, :, None, :]
    turned = jnp.stack((first * cos_b - second * sin_b, second * cos_b + first * sin_b), axis=3)
    return turned.reshape(row_count, col_count)


def visible_keys(begin_at, block_rows, segment_ids, live_rows):
    seq_length = segment_ids.shape[0]
    key_index = jnp.arange(seq_length)
    query_index = begin_at + jnp.arange(block_rows)
    query_segs = segment_ids[begin_at : begin_at + block_rows]
    same_doc = query_segs[:, None] == segment_ids[None, :]
    causal = key_index[None, :] <= query_index[:, None]
    kept_key = (live_rows[None, :] > 0) | (key_index[None, :] == query_index[:, None])
    return same_doc & causal & kept_key


def block_scores(query_seq, key_heads, begin_at, block_rows, segment_ids, live_rows):
    local_heads = key_heads.shape[1]
    query_heads = query_seq[begin_at : begin_at + block_rows].reshape(block_rows, local_heads, HEAD)
    scores = jnp.einsum(
        "ihd,jhd->hij", query_heads, key_heads, preferred_element_type=jnp.float32
    ) * HEAD ** (-0.5)
    allowed = visible_keys(begin_at, block_rows, segment_ids, live_rows)
    return (query_heads, jnp.where(allowed[None], scores, NEG_FILL))


def attend_forward(query_seq, key_seq, value_seq, segment_ids, live_rows):
    seq_length = query_seq.shape[0]
    local_heads = query_seq.shape[1] // HEAD
    block_rows = min(512, seq_length)
    key_heads = key_seq.reshape(seq_length, local_heads, HEAD)
    value_heads = value_seq.reshape(seq_length, local_heads, HEAD)
    mixed_parts = []
    lse_parts = []
    for begin_at in range(0, seq_length, block_rows):
        query_heads, scores = block_scores(
            query_seq, key_heads, begin_at, block_rows, segment_ids, live_rows
        )
        row_max = jnp.max(scores, axis=-1, keepdims=True)
        exp_scores = jnp.exp(scores - row_max)
        row_total = jnp.sum(exp_scores, axis=-1, keepdims=True)
        attn_prob = (exp_scores / row_total).astype(jnp.bfloat16)
        mixed_block = jnp.einsum(
            "hij,jhd->ihd", attn_prob, value_heads, preferred_element_type=jnp.float32
        )
        mixed_parts.append(mixed_block.reshape(block_rows, -1).astype(jnp.bfloat16))
        lse_parts.append((row_max + jnp.log(row_total))[..., 0])
    return (jnp.concatenate(mixed_parts, 0), jnp.concatenate(lse_parts, 1))


def attend_backward(query_seq, key_seq, value_seq, grad_seq, log_totals, segment_ids, live_rows):
    seq_length = query_seq.shape[0]
    local_heads = query_seq.shape[1] // HEAD
    block_rows = min(512, seq_length)
    score_scale = HEAD ** (-0.5)
    key_heads = key_seq.reshape(seq_length, local_heads, HEAD)
    value_heads = value_seq.reshape(seq_length, local_heads, HEAD)
    key_total = jnp.zeros((seq_length, local_heads, HEAD), jnp.float32)
    value_total = jnp.zeros((seq_length, local_heads, HEAD), jnp.float32)
    query_parts = []
    for begin_at in range(0, seq_length, block_rows):
        query_heads, scores = block_scores(
            query_seq, key_heads, begin_at, block_rows, segment_ids, live_rows
        )
        attn_float = jnp.exp(scores - log_totals[:, begin_at : begin_at + block_rows, None])
        attn_prob = attn_float.astype(jnp.bfloat16)
        grad_heads = grad_seq[begin_at : begin_at + block_rows].reshape(
            block_rows, local_heads, HEAD
        )
        grad_prob = jnp.einsum(
            "ihd,jhd->hij", grad_heads, value_heads, preferred_element_type=jnp.float32
        )
        row_dot = jnp.sum(attn_float * grad_prob, axis=-1, keepdims=True)
        grad_scores = (attn_float * (grad_prob - row_dot)).astype(jnp.bfloat16)
        query_block = (
            jnp.einsum("hij,jhd->ihd", grad_scores, key_heads, preferred_element_type=jnp.float32)
            * score_scale
        )
        query_parts.append(query_block.reshape(block_rows, -1))
        key_total = (
            key_total
            + jnp.einsum(
                "hij,ihd->jhd", grad_scores, query_heads, preferred_element_type=jnp.float32
            )
            * score_scale
        )
        value_total = value_total + jnp.einsum(
            "hij,ihd->jhd", attn_prob, grad_heads, preferred_element_type=jnp.float32
        )
    return (
        jnp.concatenate(query_parts, 0),
        key_total.reshape(seq_length, -1),
        value_total.reshape(seq_length, -1).astype(jnp.bfloat16),
    )


def branch_total(partial_rows):
    return lax.psum(partial_rows, "tensor")


def input_total(partial_rows):
    return lax.psum(partial_rows, "tensor")


def norm_back(grad_rows, values, inv_rms, gain_row, model_width):
    scaled = grad_rows * gain_row
    inner_dot = jnp.sum(scaled * values, axis=1, keepdims=True)
    return inv_rms * scaled - values * inv_rms**3 * inner_dot / model_width


def shards(
    tokens,
    segments,
    pad_mask,
    w_query,
    w_key,
    w_value,
    w_out,
    gain_query,
    gain_key,
    gain_attn,
    w_gate,
    w_up,
    w_down,
    gain_mlp,
    cotangent,
):
    row_count, model_width = tokens.shape
    seq_count = row_count // LENGTH
    live_rows = pad_mask.astype(jnp.float32)
    cosine, sine_part = rope_tables()

    def split_seqs(values):
        return values.reshape((seq_count, LENGTH) + values.shape[1:])

    query_raw = jnp.dot(tokens, w_query, preferred_element_type=jnp.float32)
    key_raw = jnp.dot(tokens, w_key, preferred_element_type=jnp.float32)
    value_rows = jnp.dot(tokens, w_value, preferred_element_type=jnp.float32).astype(jnp.bfloat16)
    query_sq, key_sq = lax.psum(
        (jnp.sum(query_raw * query_raw, axis=1), jnp.sum(key_raw * key_raw, axis=1)), "tensor"
    )
    query_inv = lax.rsqrt(query_sq / model_width + EPSILON)[:, None]
    key_inv = lax.rsqrt(key_sq / model_width + EPSILON)[:, None]
    query_gain = gain_query.reshape(-1).astype(jnp.float32)
    key_gain = gain_key.reshape(-1).astype(jnp.float32)
    query_norm = rotate(query_raw * query_inv * query_gain, cosine, sine_part, 1.0).astype(
        jnp.bfloat16
    )
    key_norm = rotate(key_raw * key_inv * key_gain, cosine, sine_part, 1.0).astype(jnp.bfloat16)
    seg_split = split_seqs(segments)
    live_split = split_seqs(pad_mask)
    mixed, log_totals = lax.map(
        lambda packed: attend_forward(*packed),
        (
            split_seqs(query_norm),
            split_seqs(key_norm),
            split_seqs(value_rows),
            seg_split,
            live_split,
        ),
    )
    mixed = mixed.reshape(row_count, -1)
    branch = branch_total(jnp.dot(mixed, w_out, preferred_element_type=jnp.float32))
    branch_inv = lax.rsqrt(jnp.mean(branch * branch, axis=1, keepdims=True) + EPSILON)
    attn_gain = gain_attn.astype(jnp.float32)
    hidden_in = tokens.astype(jnp.float32) + branch * branch_inv * attn_gain
    hidden_low = hidden_in.astype(jnp.bfloat16)
    gate_rows = jnp.dot(hidden_low, w_gate, preferred_element_type=jnp.float32)
    up_rows = jnp.dot(hidden_low, w_up, preferred_element_type=jnp.float32)
    gate_sig = jax.nn.sigmoid(gate_rows)
    gate_act = gate_rows * gate_sig
    inner_rows = (gate_act * up_rows).astype(jnp.bfloat16)
    down_rows = branch_total(jnp.dot(inner_rows, w_down, preferred_element_type=jnp.float32))
    down_inv = lax.rsqrt(jnp.mean(down_rows * down_rows, axis=1, keepdims=True) + EPSILON)
    mlp_gain = gain_mlp.astype(jnp.float32)
    output = (hidden_in + down_rows * down_inv * mlp_gain).astype(jnp.bfloat16)
    seed = cotangent.astype(jnp.float32) * live_rows[:, None]
    grad_gain_mlp = jnp.sum(seed * down_rows * down_inv, axis=0)
    grad_down_rows = norm_back(seed, down_rows, down_inv, mlp_gain, model_width).astype(
        jnp.bfloat16
    )
    grad_down = outer_sum(inner_rows, grad_down_rows)
    grad_inner = back_product(grad_down_rows, w_down)
    grad_gate_rows = (
        grad_inner * up_rows * gate_sig * (1.0 + gate_rows * (1.0 - gate_sig))
    ).astype(jnp.bfloat16)
    grad_up_rows = (grad_inner * gate_act).astype(jnp.bfloat16)
    grad_gate = outer_sum(hidden_low, grad_gate_rows)
    grad_up = outer_sum(hidden_low, grad_up_rows)
    grad_hidden = seed + input_total(
        back_product(grad_gate_rows, w_gate) + back_product(grad_up_rows, w_up)
    )
    grad_gain_attn = jnp.sum(grad_hidden * branch * branch_inv, axis=0)
    grad_branch = norm_back(grad_hidden, branch, branch_inv, attn_gain, model_width).astype(
        jnp.bfloat16
    )
    grad_out = outer_sum(mixed, grad_branch)
    grad_mixed = back_product(grad_branch, w_out).astype(jnp.bfloat16)
    grad_query_rot, grad_key_rot, grad_value_rows = lax.map(
        lambda packed: attend_backward(*packed),
        (
            split_seqs(query_norm),
            split_seqs(key_norm),
            split_seqs(value_rows),
            split_seqs(grad_mixed),
            log_totals,
            seg_split,
            live_split,
        ),
    )
    grad_query_norm = rotate(grad_query_rot.reshape(row_count, -1), cosine, sine_part, -1.0)
    grad_key_norm = rotate(grad_key_rot.reshape(row_count, -1), cosine, sine_part, -1.0)
    grad_value_rows = grad_value_rows.reshape(row_count, -1)
    grad_gain_query = jnp.sum(grad_query_norm * query_raw * query_inv, axis=0).reshape(
        gain_query.shape
    )
    grad_gain_key = jnp.sum(grad_key_norm * key_raw * key_inv, axis=0).reshape(gain_key.shape)
    query_scaled = grad_query_norm * query_gain
    key_scaled = grad_key_norm * key_gain
    query_dot, key_dot = lax.psum(
        (jnp.sum(query_scaled * query_raw, axis=1), jnp.sum(key_scaled * key_raw, axis=1)), "tensor"
    )
    grad_query_raw = (
        query_inv * query_scaled - query_raw * query_inv**3 * query_dot[:, None] / model_width
    ).astype(jnp.bfloat16)
    grad_key_raw = (
        key_inv * key_scaled - key_raw * key_inv**3 * key_dot[:, None] / model_width
    ).astype(jnp.bfloat16)
    grad_query = outer_sum(tokens, grad_query_raw)
    grad_key = outer_sum(tokens, grad_key_raw)
    grad_value = outer_sum(tokens, grad_value_rows)
    input_part = (
        back_product(grad_query_raw, w_query)
        + back_product(grad_key_raw, w_key)
        + back_product(grad_value_rows, w_value)
    )
    grad_tokens = (grad_hidden + input_total(input_part)).astype(jnp.bfloat16)
    summed = tuple(
        (
            lax.psum_scatter(grad_query, "dp", scatter_dimension=0, tiled=True),
            lax.psum_scatter(grad_key, "dp", scatter_dimension=0, tiled=True),
            lax.psum_scatter(grad_value, "dp", scatter_dimension=0, tiled=True),
            lax.psum_scatter(grad_out, "dp", scatter_dimension=1, tiled=True),
            lax.psum_scatter(grad_gain_query, "dp", scatter_dimension=1, tiled=True),
            lax.psum_scatter(grad_gain_key, "dp", scatter_dimension=1, tiled=True),
            lax.psum_scatter(grad_gain_attn, "dp", scatter_dimension=0, tiled=True),
            lax.psum_scatter(grad_gate, "dp", scatter_dimension=0, tiled=True),
            lax.psum_scatter(grad_up, "dp", scatter_dimension=0, tiled=True),
            lax.psum_scatter(grad_down, "dp", scatter_dimension=1, tiled=True),
            lax.psum_scatter(grad_gain_mlp, "dp", scatter_dimension=0, tiled=True),
        )
    )
    return (output, grad_tokens) + summed


def solution(mesh):
    in_specs = (
        P("dp", None),
        P("dp"),
        P("dp"),
        P(None, "tensor"),
        P(None, "tensor"),
        P(None, "tensor"),
        P("tensor", None),
        P("tensor", None),
        P("tensor", None),
        P(),
        P(None, "tensor"),
        P(None, "tensor"),
        P("tensor", None),
        P(),
        P("dp", None),
    )
    out_specs = (
        P("dp", None),
        P("dp", None),
        P("dp", "tensor"),
        P("dp", "tensor"),
        P("dp", "tensor"),
        P("tensor", "dp"),
        P("tensor", "dp"),
        P("tensor", "dp"),
        P("dp"),
        P("dp", "tensor"),
        P("dp", "tensor"),
        P("tensor", "dp"),
        P("dp"),
    )
    return jax.shard_map(shards, mesh=mesh, in_specs=in_specs, out_specs=out_specs, check_vma=False)
```

profile of v0, /device:TPU:0, one launch (start us, length us, event | category | flops | bytes accessed | tf_op | source)
XLA Modules:
  0.0 2198.8 jit_solution(17051256779297361795)
XLA Ops:
  25.0 8.6 all-reduce.4
  61.6 152.7 %all-reduce.10.cloned.1.call-done = f32[1024,2048]{1,0:T(8,128)} async-done(((f32[1024,2048]{1,0:T(8,128)}), f32[1024,2048]{1,0:T(8,128)}) %all-reduce.10.cloned.1.call-update) | async-done | bytes 8388624 | tf_op jit(solution)/shard_map/psum | solution.py:138
  224.0 10.9 fusion.43
  234.9 15.2 multiply_convert_fusion.4
  252.1 10.9 fusion.44
  263.7 152.5 %all-reduce.12.cloned.1.call-done = f32[1024,2048]{1,0:T(8,128)} async-done(((f32[1024,2048]{1,0:T(8,128)}), f32[1024,2048]{1,0:T(8,128)}) %all-reduce.12.cloned.1.call-update) | async-done | bytes 8388624 | tf_op jit(solution)/shard_map/psum | solution.py:138
  427.3 21.0 multiply_convert_fusion.2
  448.3 12.7 fusion.45
  461.0 13.5 convolution_add_fusion
  475.2 152.5 %all-reduce.14.cloned.1.call-done = f32[1024,2048]{1,0:T(8,128)} async-done(((f32[1024,2048]{1,0:T(8,128)}), f32[1024,2048]{1,0:T(8,128)}) %all-reduce.14.cloned.1.call-update) | async-done | bytes 8388624 | tf_op jit(solution)/shard_map/psum | solution.py:142
  627.7 9.8 multiply_reduce_fusion.1
  639.5 10.9 subtract_convert_fusion
  687.2 5.9 all-reduce.3
  703.3 5.7 fusion.46
  710.0 12.1 add_add_fusion
  722.2 6.6 convolution_bitcast_fusion
  730.1 6.5 convolution_bitcast_fusion.2
  737.8 6.5 convolution_bitcast_fusion.1
  745.5 6.5 fusion.31
  752.7 17.4 fusion.42
  770.2 15.2 fusion.50
  785.7 15.2 fusion.49
  802.8 37.3 %all-reduce.2 = (f32[2048]{0:T(1024)S(1)}, f32[2048]{0:T(1024)S(1)}) all-reduce(f32[2048]{0:T(1024)S(1)} %copy-done.56, f32[2048]{0:T(1024)S(1)} %copy-done.55), channel_id=8, replica_groups=mesh['dp'=8,'tensor'=4] {'dp'}, use_global_device_ids=true, to_apply=%region_31.32.clone | all-reduce | flops 4096 | bytes 32768
  844.1 119.8 %all-reduce.16.cloned.1.call-done = f32[1024,2048]{1,0:T(8,128)} async-done(((f32[1024,2048]{1,0:T(8,128)}), f32[1024,2048]{1,0:T(8,128)}) %all-reduce.16.cloned.1.call-update) | async-done | bytes 8388624 | tf_op jit(solution)/shard_map/psum | solution.py:142
  964.0 10.6 add_convert_fusion
  974.6 81.7 %reduce-scatter.18.cloned.1.call-done = f32[256,512]{0,1:T(8,128)} async-done(((f32[2048,512]{0,1:T(8,128)}), f32[256,512]{0,1:T(8,128)}) %reduce-scatter.18.cloned.1.call-update) | async-done | bytes 524304 | tf_op jit(solution)/shard_map/reduce_scatter | solution.py:282
  1058.3 90.3 %reduce-scatter.14.cloned.1.call-done = f32[256,512]{0,1:T(8,128)} async-done(((f32[2048,512]{0,1:T(8,128)}), f32[256,512]{0,1:T(8,128)}) %reduce-scatter.14.cloned.1.call-update) | async-done | bytes 524304 | tf_op jit(solution)/shard_map/reduce_scatter | solution.py:280
  1150.7 89.9 %reduce-scatter.16.cloned.1.call-done = f32[256,512]{0,1:T(8,128)} async-done(((f32[2048,512]{0,1:T(8,128)}), f32[256,512]{0,1:T(8,128)}) %reduce-scatter.16.cloned.1.call-update) | async-done | bytes 524304 | tf_op jit(solution)/shard_map/reduce_scatter | solution.py:281
  1242.6 90.7 %reduce-scatter.20.cloned.1.call-done = f32[512,256]{1,0:T(8,128)} async-done(((f32[512,2048]{1,0:T(8,128)}), f32[512,256]{1,0:T(8,128)}) %reduce-scatter.20.cloned.1.call-update) | async-done | bytes 524304 | tf_op jit(solution)/shard_map/reduce_scatter | solution.py:283
  1333.3 286.8 %reduce-scatter.26.cloned.1.call-done = f32[2048,256]{1,0:T(8,128)} async-done(((f32[2048,2048]{1,0:T(8,128)}), f32[2048,256]{1,0:T(8,128)}) %reduce-scatter.26.cloned.1.call-update) | async-done | bytes 2097168 | tf_op jit(solution)/shard_map/reduce_scatter | solution.py:289
  1620.1 286.0 %reduce-scatter.24.cloned.1.call-done = f32[256,2048]{1,0:T(8,128)} async-done(((f32[2048,2048]{1,0:T(8,128)}), f32[256,2048]{1,0:T(8,128)}) %reduce-scatter.24.cloned.1.call-update) | async-done | bytes 2097168 | tf_op jit(solution)/shard_map/reduce_scatter | solution.py:288
  1906.1 285.9 %reduce-scatter.22.cloned.1.call-done = f32[256,2048]{1,0:T(8,128)} async-done(((f32[2048,2048]{1,0:T(8,128)}), f32[256,2048]{1,0:T(8,128)}) %reduce-scatter.22.cloned.1.call-update) | async-done | bytes 2097168 | tf_op jit(solution)/shard_map/reduce_scatter | solution.py:287
  (276 shorter events, 135.0 us)
Async XLA Ops:
  7.2 14.0 copy-start
  7.2 207.1 %all-reduce.10.cloned.1.call-start = ((), (), s32[]{:S(2)}) async-start(), calls=%async_computation.9 | async-start | bytes 16777216 | tf_op jit(solution)/shard_map/psum | solution.py:138
  8.8 27.4 %copy-start.51 = (f32[512]{0:T(512)}, f32[512]{0:T(512)S(1)}, u32[]{:S(2)}) copy-start(f32[512]{0:T(512)S(1)} %bitcast_convert_fusion.1) | copy-start | bytes 6148
  9.5 24.8 %copy-start.53 = (f32[512]{0:T(512)}, f32[512]{0:T(512)S(1)}, u32[]{:S(2)}) copy-start(f32[512]{0:T(512)S(1)} %bitcast_convert_fusion) | copy-start | bytes 6148
  12.0 24.4 %copy-start.31 = (f32[1024,64]{0,1:T(8,128)}, f32[1024,64]{0,1:T(8,128)S(1)}, u32[]{:S(2)}) copy-start(f32[1024,64]{0,1:T(8,128)S(1)} %get-tuple-element.157) | copy-start | bytes 786436
  17.4 33.2 %copy-start.29 = (bf16[1024,512]{0,1:T(8,128)(2,1)}, bf16[1024,512]{0,1:T(8,128)(2,1)S(1)}, u32[]{:S(2)}) copy-start(bf16[1024,512]{0,1:T(8,128)(2,1)S(1)} %convolution_convert_fusion.1) | copy-start | bytes 3145732
  37.3 9.5 copy-start.7
  37.4 9.4 copy-start.20
  61.0 355.3 %all-reduce.12.cloned.1.call-start = ((), (), s32[]{:S(2)}) async-start(), calls=%async_computation.10 | async-start | bytes 16777216 | tf_op jit(solution)/shard_map/psum | solution.py:138
  61.6 157.4 %copy-start.39 = (f32[2048]{0:T(1024)}, f32[2048]{0:T(1024)S(1)}, u32[]{:S(2)}) copy-start(f32[2048]{0:T(1024)S(1)} %convert_element_type.147) | copy-start | bytes 24580
  224.0 11.0 copy-start.28
  224.0 28.1 %slice-start.4 = ((s8[8388608]{0:T(1024)(128)(4,1)}), s8[4194304]{0:T(1024)(128)(4,1)S(1)}, s32[]{:S(2)}) async-start(s8[8388608]{0:T(1024)(128)(4,1)} %bitcast.158), calls=%async_computation.26 | async-start | bytes 8388608
  234.9 17.1 slice-start.5
  263.1 364.6 %all-reduce.14.cloned.1.call-start = ((), (), s32[]{:S(2)}) async-start(), calls=%async_computation.11 | async-start | bytes 16777216 | tf_op jit(solution)/shard_map/psum | solution.py:142
  427.3 21.0 copy-start.66
  448.2 12.7 copy-start.81
  474.5 153.2 %copy-start.40 = (f32[2048]{0:T(1024)S(1)}, f32[2048]{0:T(1024)}, u32[]{:S(2)}) copy-start(f32[2048]{0:T(1024)} %copy-done.39) | copy-start | bytes 24580
  474.5 153.2 %copy-start.46 = (f32[1024]{0:T(1024)S(1)}, f32[1024]{0:T(1024)}, u32[]{:S(2)}) copy-start(f32[1024]{0:T(1024)} %copy-done.45) | copy-start | bytes 12292
  474.5 366.9 %reduce-scatter.30.cloned.1.call-start = ((), (), s32[]{:S(2)}) async-start(), calls=%async_computation.21 | async-start | bytes 73728
  475.2 162.3 %copy-start.61 = (f32[1024]{0:T(1024)S(1)}, f32[1024]{0:T(1024)}, u32[]{:S(2)}) copy-start(f32[1024]{0:T(1024)} %get-tuple-element.149) | copy-start | bytes 12292
  627.7 9.8 copy-start.4
  627.7 10.6 copy-start.6
  627.7 11.8 copy-start.17
  684.0 158.8 %reduce-scatter.28.cloned.1.call-start = ((), (), s32[]{:S(2)}) async-start(), calls=%async_computation.20 | async-start | bytes 73728
  709.7 254.2 %all-reduce.16.cloned.1.call-start = ((), (), s32[]{:S(2)}) async-start(), calls=%async_computation.12 | async-start | bytes 16777216 | tf_op jit(solution)/shard_map/psum | solution.py:142
  722.1 334.1 %reduce-scatter.18.cloned.1.call-start = ((), (), s32[]{:S(2)}) async-start(), calls=%async_computation.15 | async-start | bytes 4718592 | tf_op jit(solution)/shard_map/reduce_scatter | solution.py:282
  728.9 419.8 %reduce-scatter.14.cloned.1.call-start = ((), (), s32[]{:S(2)}) async-start(), calls=%async_computation.13 | async-start | bytes 4718592 | tf_op jit(solution)/shard_map/reduce_scatter | solution.py:280
  736.6 503.9 %reduce-scatter.16.cloned.1.call-start = ((), (), s32[]{:S(2)}) async-start(), calls=%async_computation.14 | async-start | bytes 4718592 | tf_op jit(solution)/shard_map/reduce_scatter | solution.py:281
  744.3 589.0 %reduce-scatter.20.cloned.1.call-start = ((), (), s32[]{:S(2)}) async-start(), calls=%async_computation.16 | async-start | bytes 4718592 | tf_op jit(solution)/shard_map/reduce_scatter | solution.py:283
  752.0 868.1 %reduce-scatter.26.cloned.1.call-start = ((), (), s32[]{:S(2)}) async-start(), calls=%async_computation.19 | async-start | bytes 18874368 | tf_op jit(solution)/shard_map/reduce_scatter | solution.py:289
  770.1 1136.0 %reduce-scatter.24.cloned.1.call-start = ((), (), s32[]{:S(2)}) async-start(), calls=%async_computation.18 | async-start | bytes 18874368 | tf_op jit(solution)/shard_map/reduce_scatter | solution.py:288
  785.4 1406.6 %reduce-scatter.22.cloned.1.call-start = ((), (), s32[]{:S(2)}) async-start(), calls=%async_computation.17 | async-start | bytes 18874368 | tf_op jit(solution)/shard_map/reduce_scatter | solution.py:287
  (71 other events, 224.2 us)
Sparse Core Ops, SparseCore 0:
  61.1 153.1 all-reduce.9
  263.2 152.9 all-reduce.11
  474.6 153.0 all-reduce.13
  684.1 61.3 reduce-scatter.29
  749.3 60.2 reduce-scatter.27
  812.0 151.9 all-reduce.15
  967.6 88.6 reduce-scatter.17
  1060.3 88.2 reduce-scatter.13
  1152.3 88.2 reduce-scatter.15
  1245.0 88.2 reduce-scatter.19
  1337.7 282.3 reduce-scatter.25
  1624.8 281.2 reduce-scatter.23
  1910.5 281.4 reduce-scatter.21
where the time goes:
time: 2210 us; the launch traced here: 2200 us
  waiting for transfers between devices  1790 us (81%)
  matrix products  231 us (10%)
  other arithmetic  74 us (3%)
  blocking collectives  51.9 us (2%)
  local copies, waits for them, and re-layouts  35.1 us (2%)
    psum x2, waiting for transfers between devices, branch_total(): return lax.psum(partial_rows, 'tensor')  305 us
    reduce_scatter x1, waiting for transfers between devices, shards(): lax.psum_scatter(grad_down, 'dp', scatter_dimension=1, tiled=True)  287 us
    reduce_scatter x1, waiting for transfers between devices, shards(): lax.psum_scatter(grad_up, 'dp', scatter_dimension=0, tiled=True)  286 us
    reduce_scatter x1, waiting for transfers between devices, shards(): lax.psum_scatter(grad_gate, 'dp', scatter_dimension=0, tiled=True)  286 us
    psum x2, waiting for transfers between devices, input_total(): return lax.psum(partial_rows, 'tensor')  272 us
    reduce_scatter x1, waiting for transfers between devices, shards(): lax.psum_scatter(grad_out, 'dp', scatter_dimension=1, tiled=True)  90.7 us
    reduce_scatter x1, waiting for transfers between devices, shards(): lax.psum_scatter(grad_query, 'dp', scatter_dimension=0, tiled=True)  90.3 us
    reduce_scatter x1, waiting for transfers between devices, shards(): lax.psum_scatter(grad_key, 'dp', scatter_dimension=0, tiled=True)  89.9 us
  transfers between devices with their start and end apart: 13, of which 11 were waited for; matrix products, arithmetic and copies ran while one was open for 6% of the time, Pallas kernels for 0%

commit v1 on v0

v1 whole, which is shorter than its diff:
```python
import functools

import jax
import jax.numpy as jnp
from jax import lax
from jax.experimental import pallas as pl
from jax.experimental.pallas import tpu as pltpu
from jax.sharding import PartitionSpec as P

HEAD = 128
LENGTH = 1024
EPSILON = 1e-06
NEG_FILL = -1e30
ROPE_BASE = 500000.0
ROW_CHUNKS = 4
F32 = jnp.float32
BF16 = jnp.bfloat16


COLS = 512

def dp_kernel(dp_size, groups, *refs):
    n = len(groups)
    at_refs = refs[:n]
    b_refs = refs[n:2 * n]
    out_ref = refs[2 * n]
    (ysend, yrecv, zsend, zrecv, stage, ys_sem, yr_sem, zs_sem, zr_sem, out_sem,
     y_credit, up_credit, down_credit) = refs[2 * n + 1:]
    line = dp_size // 2
    block = at_refs[0].shape[0] // dp_size
    dp_at = lax.axis_index("dp")
    z, y = dp_at // 2, dp_at % 2
    total = sum(groups)
    partner = dp_at + 1 - 2 * y
    below, above = dp_at - 2, dp_at + 2
    has_below, has_above = z > 0, z < line - 1

    def dev(i):
        return {"dp": i}

    barrier = pltpu.get_barrier_semaphore()
    pl.semaphore_signal(barrier, inc=1, device_id=dev(partner), device_id_type=pl.DeviceIdType.MESH)

    @pl.when(has_below)
    def _():
        pl.semaphore_signal(barrier, inc=1, device_id=dev(below), device_id_type=pl.DeviceIdType.MESH)

    @pl.when(has_above)
    def _():
        pl.semaphore_signal(barrier, inc=1, device_id=dev(above), device_id_type=pl.DeviceIdType.MESH)

    pl.semaphore_wait(barrier, 1 + has_below.astype(jnp.int32) + has_above.astype(jnp.int32))

    def y_copy(p, b):
        return pltpu.make_async_remote_copy(
            src_ref=ysend.at[p, b], dst_ref=yrecv.at[p, b], send_sem=ys_sem.at[p, b],
            recv_sem=yr_sem.at[p, b], device_id=dev(partner), device_id_type=pl.DeviceIdType.MESH)

    def z_copy(p, b, slot, target):
        return pltpu.make_async_remote_copy(
            src_ref=zsend.at[p, b], dst_ref=zrecv.at[p, slot], send_sem=zs_sem.at[p, b],
            recv_sem=zr_sem.at[p, slot], device_id=dev(target), device_id_type=pl.DeviceIdType.MESH)

    def walk(fn, own):
        def body(i, carry):
            @pl.when(z <= i)
            def _():
                fn(z + line - 1 - i, True)

            @pl.when(z >= line - 1 - i)
            def _():
                fn(z - (line - 1 - i), False)
            return carry
        lax.fori_loop(0, line - 1, body, 0)
        own(z)

    def product(at_ref, b_ref, rows_at, col):
        return jnp.dot(
            at_ref[pl.ds(pl.multiple_of(rows_at * block, block), block), :],
            b_ref[:, pl.ds(pl.multiple_of(col * COLS, COLS), COLS)],
            preferred_element_type=F32)

    def send_stage(k, p, at_ref, b_ref, col):
        @pl.when(k >= 2)
        def _():
            for b in range(line):
                y_copy(p, b).wait_send()
            pl.semaphore_wait(y_credit, 1)

        def one(b, up=None):
            ysend[p, b] = product(at_ref, b_ref, 2 * b + 1 - y, col)
            y_copy(p, b).start()
        walk(one, one)

    def sum_stage(k, p, at_ref, b_ref, col):
        @pl.when(k >= 2)
        def _():
            for b in range(line):
                @pl.when(z != b)
                def _():
                    z_copy(p, b, b, below).wait_send()

            @pl.when(has_above)
            def _():
                pl.semaphore_wait(up_credit, 1)

            @pl.when(has_below)
            def _():
                pl.semaphore_wait(down_credit, 1)

        def mine(b):
            part = product(at_ref, b_ref, 2 * b + y, col)
            y_copy(p, b).wait_recv()
            return part + yrecv[p, b]

        def one(b, up):
            has_before, target = (has_below, above) if up else (has_above, below)
            zsend[p, b] = mine(b)

            @pl.when(has_before)
            def _():
                z_copy(p, b, b, target).wait_recv()
                zsend[p, b] += zrecv[p, b]
            if up:
                z_copy(p, b, b, target).start()
            else:
                @pl.when(b == z - 1)
                def _():
                    z_copy(p, b, line, target).start()

                @pl.when(b != z - 1)
                def _():
                    z_copy(p, b, b, target).start()

        def own(b):
            @pl.when(k >= 1)
            def _():
                pltpu.make_async_copy(stage, out_ref.at[k - 1], out_sem).wait()
            stage[...] = mine(b)

            @pl.when(has_below)
            def _():
                z_copy(p, b, b, below).wait_recv()
                stage[...] += zrecv[p, b]

            @pl.when(has_above)
            def _():
                z_copy(p, b, line, below).wait_recv()
                stage[...] += zrecv[p, line]
            pltpu.make_async_copy(stage, out_ref.at[k], out_sem).start()
        walk(one, own)

        @pl.when(k < total - 2)
        def _():
            pl.semaphore_signal(y_credit, inc=1, device_id=dev(partner), device_id_type=pl.DeviceIdType.MESH)

            @pl.when(has_below)
            def _():
                pl.semaphore_signal(up_credit, inc=1, device_id=dev(below), device_id_type=pl.DeviceIdType.MESH)

            @pl.when(has_above)
            def _():
                pl.semaphore_signal(down_credit, inc=1, device_id=dev(above), device_id_type=pl.DeviceIdType.MESH)

    send_stage(0, 0, at_refs[0], b_refs[0], 0)
    k0 = 0
    for g, count in enumerate(groups):
        at_ref, b_ref = at_refs[g], b_refs[g]

        def body(i, carry):
            k = k0 + i
            send_stage(k + 1, lax.rem(k + 1, 2), at_ref, b_ref, i + 1)
            sum_stage(k, lax.rem(k, 2), at_ref, b_ref, i)
            return carry
        lax.fori_loop(0, count - 1, body, 0)
        k = k0 + count - 1
        if g + 1 < n:
            send_stage(k + 1, (k + 1) % 2, at_refs[g + 1], b_refs[g + 1], 0)
        sum_stage(k, k % 2, at_ref, b_ref, count - 1)
        k0 += count
    pltpu.make_async_copy(stage, out_ref.at[total - 1], out_sem).wait()
    for p in range(2):
        for b in range(line):
            y_copy(p, b).wait_send()

            @pl.when(z != b)
            def _():
                z_copy(p, b, b, below).wait_send()

def dp_reduce(dp_size, pairs, collective_id=0):
    line = dp_size // 2
    depth = pairs[0][0].shape[0]
    block = depth // dp_size
    groups = [right.shape[1] // COLS for _, right in pairs]
    total = sum(groups)
    slot = (block, COLS)
    DMA = pltpu.SemaphoreType.DMA
    return pl.pallas_call(
        functools.partial(dp_kernel, dp_size, groups),
        out_shape=jax.ShapeDtypeStruct((total,) + slot, F32),
        in_specs=[pl.BlockSpec(memory_space=pltpu.VMEM)] * (2 * len(pairs)),
        out_specs=pl.BlockSpec(memory_space=pl.ANY),
        scratch_shapes=[
            pltpu.VMEM((2, line) + slot, F32),
            pltpu.VMEM((2, line) + slot, F32),
            pltpu.VMEM((2, line) + slot, F32),
            pltpu.VMEM((2, line + 1) + slot, F32),
            pltpu.VMEM(slot, F32),
            DMA((2, line)), DMA((2, line)), DMA((2, line)), DMA((2, line + 1)), DMA,
            pltpu.SemaphoreType.REGULAR, pltpu.SemaphoreType.REGULAR, pltpu.SemaphoreType.REGULAR,
        ],
        compiler_params=pltpu.CompilerParams(
            collective_id=collective_id, has_side_effects=True, vmem_limit_bytes=60 * 1024 * 1024),
    )(*[left for left, _ in pairs], *[right for _, right in pairs])


def times(left, right):
    return jnp.dot(left, right, preferred_element_type=F32)


def outer_sum(left, right):
    return lax.dot_general(left, right, (((0,), (0,)), ((), ())), preferred_element_type=F32)


def back_product(left, right):
    return lax.dot_general(left, right, (((1,), (1,)), ((), ())), preferred_element_type=F32)


def rope_tables():
    half_size = HEAD // 2
    freq_row = ROPE_BASE ** (-(jnp.arange(half_size, dtype=F32) * 2.0) / HEAD)
    angle = jnp.arange(LENGTH, dtype=F32)[:, None] * freq_row[None, :]
    return (jnp.cos(angle), jnp.sin(angle))


def rotate(values, cosine, sine_part, direction):
    row_count, col_count = values.shape
    half_size = HEAD // 2
    split = values.reshape(row_count // LENGTH, LENGTH, col_count // HEAD, 2, half_size)
    first = split[:, :, :, 0]
    second = split[:, :, :, 1]
    cos_b = cosine[None, :, None, :]
    sin_b = direction * sine_part[None, :, None, :]
    turned = jnp.stack((first * cos_b - second * sin_b, second * cos_b + first * sin_b), axis=3)
    return turned.reshape(row_count, col_count)


def visible_keys(begin_at, block_rows, segment_ids, live_rows):
    seq_length = segment_ids.shape[0]
    key_index = jnp.arange(seq_length)
    query_index = begin_at + jnp.arange(block_rows)
    query_segs = segment_ids[begin_at : begin_at + block_rows]
    same_doc = query_segs[:, None] == segment_ids[None, :]
    causal = key_index[None, :] <= query_index[:, None]
    kept_key = (live_rows[None, :] > 0) | (key_index[None, :] == query_index[:, None])
    return same_doc & causal & kept_key


def block_scores(query_seq, key_heads, begin_at, block_rows, segment_ids, live_rows):
    local_heads = key_heads.shape[1]
    query_heads = query_seq[begin_at : begin_at + block_rows].reshape(block_rows, local_heads, HEAD)
    scores = jnp.einsum(
        "ihd,jhd->hij", query_heads, key_heads, preferred_element_type=F32
    ) * HEAD ** (-0.5)
    allowed = visible_keys(begin_at, block_rows, segment_ids, live_rows)
    return (query_heads, jnp.where(allowed[None], scores, NEG_FILL))


def attend_forward(query_seq, key_seq, value_seq, segment_ids, live_rows):
    seq_length = query_seq.shape[0]
    local_heads = query_seq.shape[1] // HEAD
    block_rows = min(512, seq_length)
    key_heads = key_seq.reshape(seq_length, local_heads, HEAD)
    value_heads = value_seq.reshape(seq_length, local_heads, HEAD)
    mixed_parts = []
    lse_parts = []
    for begin_at in range(0, seq_length, block_rows):
        query_heads, scores = block_scores(
            query_seq, key_heads, begin_at, block_rows, segment_ids, live_rows
        )
        row_max = jnp.max(scores, axis=-1, keepdims=True)
        exp_scores = jnp.exp(scores - row_max)
        row_total = jnp.sum(exp_scores, axis=-1, keepdims=True)
        attn_prob = (exp_scores / row_total).astype(BF16)
        mixed_block = jnp.einsum(
            "hij,jhd->ihd", attn_prob, value_heads, preferred_element_type=F32
        )
        mixed_parts.append(mixed_block.reshape(block_rows, -1).astype(BF16))
        lse_parts.append((row_max + jnp.log(row_total))[..., 0])
    return (jnp.concatenate(mixed_parts, 0), jnp.concatenate(lse_parts, 1))


def attend_backward(query_seq, key_seq, value_seq, grad_seq, log_totals, segment_ids, live_rows):
    seq_length = query_seq.shape[0]
    local_heads = query_seq.shape[1] // HEAD
    block_rows = min(512, seq_length)
    score_scale = HEAD ** (-0.5)
    key_heads = key_seq.reshape(seq_length, local_heads, HEAD)
    value_heads = value_seq.reshape(seq_length, local_heads, HEAD)
    key_total = jnp.zeros((seq_length, local_heads, HEAD), F32)
    value_total = jnp.zeros((seq_length, local_heads, HEAD), F32)
    query_parts = []
    for begin_at in range(0, seq_length, block_rows):
        query_heads, scores = block_scores(
            query_seq, key_heads, begin_at, block_rows, segment_ids, live_rows
        )
        attn_float = jnp.exp(scores - log_totals[:, begin_at : begin_at + block_rows, None])
        attn_prob = attn_float.astype(BF16)
        grad_heads = grad_seq[begin_at : begin_at + block_rows].reshape(
            block_rows, local_heads, HEAD
        )
        grad_prob = jnp.einsum(
            "ihd,jhd->hij", grad_heads, value_heads, preferred_element_type=F32
        )
        row_dot = jnp.sum(attn_float * grad_prob, axis=-1, keepdims=True)
        grad_scores = (attn_float * (grad_prob - row_dot)).astype(BF16)
        query_block = (
            jnp.einsum("hij,jhd->ihd", grad_scores, key_heads, preferred_element_type=F32)
            * score_scale
        )
        query_parts.append(query_block.reshape(block_rows, -1))
        key_total = (
            key_total
            + jnp.einsum("hij,ihd->jhd", grad_scores, query_heads, preferred_element_type=F32)
            * score_scale
        )
        value_total = value_total + jnp.einsum(
            "hij,ihd->jhd", attn_prob, grad_heads, preferred_element_type=F32
        )
    return (
        jnp.concatenate(query_parts, 0),
        key_total.reshape(seq_length, -1),
        value_total.reshape(seq_length, -1).astype(BF16),
    )


def norm_back(grad_rows, values, inv_rms, gain_row, model_width):
    scaled = grad_rows * gain_row
    inner_dot = jnp.sum(scaled * values, axis=1, keepdims=True)
    return inv_rms * scaled - values * inv_rms**3 * inner_dot / model_width


def make_shards(dp_size, tensor_size):
    core_pairs = [(i, i ^ 1) for i in range(tensor_size)]
    tensor_bits = [1 << b for b in range(1, tensor_size.bit_length() - 1)]

    def to_core(values):
        return lax.ppermute(values, "tensor", core_pairs)

    def from_core(values):
        return to_core(values * 0.5) * 2.0

    def wide_sum(values):
        for bit in tensor_bits:
            values = values + lax.ppermute(
                values, "tensor", [(i, i ^ bit) for i in range(tensor_size)]
            )
        return values

    def own_rows_sum(own_part, other_part):
        return wide_sum(own_part + to_core(other_part))

    def shards(
        tokens,
        segments,
        pad_mask,
        w_query,
        w_key,
        w_value,
        w_out,
        gain_query,
        gain_key,
        gain_attn,
        w_gate,
        w_up,
        w_down,
        gain_mlp,
        cotangent,
    ):
        row_count, model_width = tokens.shape
        half_rows = row_count // 2
        chunk = half_rows // ROW_CHUNKS
        block = model_width // dp_size
        core_at = lax.axis_index("tensor") % 2
        cosine, sine_part = rope_tables()

        def split_rows(values):
            own = lax.dynamic_slice_in_dim(values, core_at * half_rows, half_rows, 0)
            other = lax.dynamic_slice_in_dim(values, (1 - core_at) * half_rows, half_rows, 0)
            return own, other

        def join_rows(own, other):
            return jnp.where(
                core_at == 0,
                jnp.concatenate((own, other), 0),
                jnp.concatenate((other, own), 0),
            )

        def cut(values):
            return [values[k * chunk : (k + 1) * chunk] for k in range(ROW_CHUNKS)]

        query_raw = times(tokens, w_query)
        key_raw = times(tokens, w_key)
        value_rows = times(tokens, w_value).astype(BF16)
        squares = jnp.stack(
            (jnp.sum(query_raw * query_raw, axis=1), jnp.sum(key_raw * key_raw, axis=1))
        )
        squares = wide_sum(squares + to_core(squares))
        query_inv = lax.rsqrt(squares[0] / model_width + EPSILON)[:, None]
        key_inv = lax.rsqrt(squares[1] / model_width + EPSILON)[:, None]
        query_gain = gain_query.reshape(-1).astype(F32)
        key_gain = gain_key.reshape(-1).astype(F32)
        query_norm = rotate(query_raw * query_inv * query_gain, cosine, sine_part, 1.0).astype(BF16)
        key_norm = rotate(key_raw * key_inv * key_gain, cosine, sine_part, 1.0).astype(BF16)
        mixed, log_totals = attend_forward(query_norm, key_norm, value_rows, segments, pad_mask)
        mixed_own, mixed_other = split_rows(mixed)
        mixed_rows = jnp.concatenate((mixed_own, mixed_other), 0)
        tokens_own, tokens_other = split_rows(tokens)
        cot_own, _ = split_rows(cotangent)
        live_own, _ = split_rows(pad_mask.astype(F32)[:, None])
        attn_gain = gain_attn.astype(F32)
        mlp_gain = gain_mlp.astype(F32)
        seed = cot_own.astype(F32) * live_own

        branch, branch_inv, hidden_in = [], [], []
        low_own, low_other = [], []
        gates, ups, sigs, inners = {}, {}, {}, {}
        down, down_inv = [], []
        for part, other, tok, tok_other in zip(
            cut(mixed_own), cut(mixed_other), cut(tokens_own), cut(tokens_other)
        ):
            total = own_rows_sum(times(part, w_out), times(other, w_out))
            inv = lax.rsqrt(jnp.mean(total * total, axis=1, keepdims=True) + EPSILON)
            step = total * inv * attn_gain
            branch.append(total)
            branch_inv.append(inv)
            hidden = tok.astype(F32) + step
            hidden_in.append(hidden)
            low_own.append(hidden.astype(BF16))
            low_other.append((tok_other.astype(F32) + to_core(step)).astype(BF16))
        for at in range(ROW_CHUNKS):
            parts = []
            for side, low in ((0, low_own[at]), (1, low_other[at])):
                gate = times(low, w_gate)
                up = times(low, w_up)
                sig = jax.nn.sigmoid(gate)
                inner = (gate * sig * up).astype(BF16)
                gates[side, at], ups[side, at], inners[side, at] = gate, up, inner
                parts.append(times(inner, w_down))
            total = own_rows_sum(*parts)
            down.append(total)
            down_inv.append(lax.rsqrt(jnp.mean(total * total, axis=1, keepdims=True) + EPSILON))

        seeds = cut(seed)
        gain_mlp_part = 0.0
        gdr_own, gdr_other, out_own = [], [], []
        for at in range(ROW_CHUNKS):
            gain_mlp_part = gain_mlp_part + jnp.sum(seeds[at] * down[at] * down_inv[at], axis=0)
            grad = norm_back(seeds[at], down[at], down_inv[at], mlp_gain, model_width)
            gdr_own.append(grad.astype(BF16))
            gdr_other.append(from_core(grad).astype(BF16))
            out_own.append(hidden_in[at] + down[at] * down_inv[at] * mlp_gain)
        out_own = jnp.concatenate(out_own, 0)
        out_other = from_core(out_own)
        output = join_rows(out_own.astype(BF16), out_other.astype(BF16))

        def all_rows(own, other):
            return jnp.concatenate(list(own) + list(other), 0)

        def all_sides(parts):
            return jnp.concatenate(
                [parts[side, at] for side in range(2) for at in range(ROW_CHUNKS)], 0
            )

        grad_down_rows = all_rows(gdr_own, gdr_other)
        inner_rows = all_sides(inners)
        gate_rows = all_sides(gates)
        up_rows = all_sides(ups)
        hidden_low = all_rows(low_own, low_other)
        grad_inner = back_product(grad_down_rows, w_down)
        gate_sig = jax.nn.sigmoid(gate_rows)
        grad_gate_rows = (
            grad_inner * up_rows * gate_sig * (1.0 + gate_rows * (1.0 - gate_sig))
        ).astype(BF16)
        grad_up_rows = (grad_inner * gate_rows * gate_sig).astype(BF16)
        gain_attn_part = 0.0
        gb_own, gb_other, grad_hidden = [], [], []
        for at in range(ROW_CHUNKS):
            parts = []
            for first in (0, half_rows):
                rows = slice(first + at * chunk, first + (at + 1) * chunk)
                parts.append(
                    back_product(grad_gate_rows[rows], w_gate)
                    + back_product(grad_up_rows[rows], w_up)
                )
            total = seeds[at] + own_rows_sum(*parts)
            grad_hidden.append(total)
            gain_attn_part = gain_attn_part + jnp.sum(total * branch[at] * branch_inv[at], axis=0)
            grad = norm_back(total, branch[at], branch_inv[at], attn_gain, model_width)
            gb_own.append(grad.astype(BF16))
            gb_other.append(from_core(grad).astype(BF16))
        grad_branch = all_rows(gb_own, gb_other)
        grad_mixed = back_product(grad_branch, w_out).astype(BF16)
        grad_mixed = join_rows(grad_mixed[:half_rows], grad_mixed[half_rows:])
        grad_query_rot, grad_key_rot, grad_value_rows = attend_backward(
            query_norm, key_norm, value_rows, grad_mixed, log_totals, segments, pad_mask
        )
        grad_query_norm = rotate(grad_query_rot, cosine, sine_part, -1.0)
        grad_key_norm = rotate(grad_key_rot, cosine, sine_part, -1.0)
        gain_query_part = jnp.sum(grad_query_norm * query_raw * query_inv, axis=0)
        gain_key_part = jnp.sum(grad_key_norm * key_raw * key_inv, axis=0)
        query_scaled = grad_query_norm * query_gain
        key_scaled = grad_key_norm * key_gain
        dots = jnp.stack(
            (jnp.sum(query_scaled * query_raw, axis=1), jnp.sum(key_scaled * key_raw, axis=1))
        )
        dots = wide_sum(dots + to_core(dots))
        grad_query_raw = (
            query_inv * query_scaled - query_raw * query_inv**3 * dots[0][:, None] / model_width
        ).astype(BF16)
        grad_key_raw = (
            key_inv * key_scaled - key_raw * key_inv**3 * dots[1][:, None] / model_width
        ).astype(BF16)
        grad_rows = jnp.concatenate((grad_query_raw, grad_key_raw, grad_value_rows), 1)
        w_all = jnp.concatenate((w_query, w_key, w_value), 1)
        rows_own, rows_other = split_rows(grad_rows)
        token_own = []
        for at, (part, other) in enumerate(zip(cut(rows_own), cut(rows_other))):
            token_own.append(
                grad_hidden[at]
                + own_rows_sum(back_product(part, w_all), back_product(other, w_all))
            )
        token_own = jnp.concatenate(token_own, 0)
        token_other = from_core(token_own)
        grad_tokens = join_rows(token_own.astype(BF16), token_other.astype(BF16))

        summed = dp_reduce(
            dp_size,
            [
                (grad_down_rows.T, inner_rows),
                (hidden_low.T, jnp.concatenate((grad_gate_rows, grad_up_rows), 1)),
                (grad_branch.T, mixed_rows),
                (tokens.T, grad_rows),
            ],
        )

        def side_by_side(first, count):
            return jnp.concatenate([summed[first + i] for i in range(count)], 1)

        hidden_chunks, head_chunks = w_gate.shape[1] // COLS, w_query.shape[1] // COLS
        starts = [0, hidden_chunks, 2 * hidden_chunks, 3 * hidden_chunks]
        grad_down, grad_gate, grad_up = (side_by_side(at, hidden_chunks) for at in starts[:3])
        grad_out, grad_query, grad_key, grad_value = (
            side_by_side(starts[3] + i * head_chunks, head_chunks) for i in range(4)
        )

        wide_gains = jnp.concatenate((gain_mlp_part, gain_attn_part))
        wide_gains = wide_gains + to_core(wide_gains)

        def by_block(values):
            heads = values.shape[0]
            return values.reshape(heads, dp_size, -1).transpose(1, 0, 2).reshape(dp_size, -1)

        gains = jnp.concatenate(
            (
                by_block(wide_gains[None, :model_width]),
                by_block(wide_gains[None, model_width:]),
                by_block(gain_query_part.reshape(gain_query.shape)),
                by_block(gain_key_part.reshape(gain_key.shape)),
            ),
            1,
        )
        gains = lax.psum_scatter(gains, "dp", scatter_dimension=0, tiled=True)[0]
        heads, head_block = gain_query.shape[0], HEAD // dp_size
        grad_gain_mlp = gains[:block]
        grad_gain_attn = gains[block : 2 * block]
        head_part = gains[2 * block :].reshape(2, heads, head_block)
        return (
            output,
            grad_tokens,
            grad_query,
            grad_key,
            grad_value,
            grad_out.T,
            head_part[0],
            head_part[1],
            grad_gain_attn,
            grad_gate,
            grad_up,
            grad_down.T,
            grad_gain_mlp,
        )

    return shards


def solution(mesh):
    in_specs = (
        P("dp", None),
        P("dp"),
        P("dp"),
        P(None, "tensor"),
        P(None, "tensor"),
        P(None, "tensor"),
        P("tensor", None),
        P("tensor", None),
        P("tensor", None),
        P(),
        P(None, "tensor"),
        P(None, "tensor"),
        P("tensor", None),
        P(),
        P("dp", None),
    )
    out_specs = (
        P("dp", None),
        P("dp", None),
        P("dp", "tensor"),
        P("dp", "tensor"),
        P("dp", "tensor"),
        P("tensor", "dp"),
        P("tensor", "dp"),
        P("tensor", "dp"),
        P("dp"),
        P("dp", "tensor"),
        P("dp", "tensor"),
        P("tensor", "dp"),
        P("dp"),
    )
    shards = make_shards(mesh.shape["dp"], mesh.shape["tensor"])
    return jax.shard_map(shards, mesh=mesh, in_specs=in_specs, out_specs=out_specs, check_vma=False)
```

time: 2210 us -> 1560 us (0.71)
  waiting for transfers between devices: 1790 us -> 322 us
  Pallas kernels: 0 us -> 730 us
  local copies, waits for them, and re-layouts: 35.1 us -> 98 us
  other arithmetic: 74 us -> 120 us
  starting transfers between devices: 1.75 us -> 29.3 us
    reduce_scatter x7 -> x0, waiting for transfers between devices: 1210 us -> none  [the longest x1 287 us: shards(): lax.psum_scatter(grad_down, 'dp', scatter_dimension=1, tiled=True)]
    pallas_call x0 -> x1, Pallas kernels: none -> 730 us  [dp_reduce(): pl.pallas_call(functools.partial(dp_kernel, dp_size, groups), out_shape=j...]
    psum x4 -> x0, waiting for transfers between devices: 577 us -> none  [the longest x2 305 us: branch_total(): return lax.psum(partial_rows, 'tensor')]
    ppermute x0 -> x51, waiting for transfers between devices: none -> 322 us  [the longest x18 319 us: wide_sum(): lax.ppermute(values, 'tensor', [(i, i ^ bit) for i in range(tensor_size)])]
    dot_general x14 -> x35, matrix products: 130 us -> 93.6 us  [times(): return jnp.dot(left, right, preferred_element_type=F32)]
    ppermute x0 -> x51, starting transfers between devices: none -> 29.3 us  [the longest x18 20.2 us: wide_sum(): lax.ppermute(values, 'tensor', [(i, i ^ bit) for i in range(tensor_size)])]
    unnamed x190 -> x266, local copies, waits for them, and re-layouts: 35 us -> 58.4 us
    dot_general x7 -> x26, matrix products: 76.3 us -> 83.5 us  [back_product(): lax.dot_general(left, right, (((1,), (1,)), ((), ())), preferred_element_...]
  transfers between devices with their start and end apart: 13 -> 51, of which waited for: 11 -> 18; matrix products, arithmetic and copies ran while one was open for 6% -> 22% of each run, Pallas kernels for 0% -> 47%
where the time goes in v1:
time: 1560 us; the launch traced here: 1550 us
  Pallas kernels  730 us (47%)
  waiting for transfers between devices  322 us (21%)
  matrix products  210 us (13%)
  other arithmetic  120 us (8%)
  local copies, waits for them, and re-layouts  98 us (6%)
  blocking collectives  37.6 us (2%)
  starting transfers between devices  29.3 us (2%)
    pallas_call x1, Pallas kernels, dp_reduce(): pl.pallas_call(functools.partial(dp_kernel, dp_size, groups), out_shape=j...  730 us
    ppermute x18, waiting for transfers between devices, wide_sum(): lax.ppermute(values, 'tensor', [(i, i ^ bit) for i in range(tensor_size)])  319 us
    dot_general x35, matrix products, times(): return jnp.dot(left, right, preferred_element_type=F32)  93.6 us
    dot_general x26, matrix products, back_product(): lax.dot_general(left, right, (((1,), (1,)), ((), ())), preferred_element_...  83.5 us
    unnamed x266, local copies, waits for them, and re-layouts  58.4 us
    unnamed x1, blocking collectives  37.6 us
  transfers between devices with their start and end apart: 51, of which 18 were waited for; matrix products, arithmetic and copies ran while one was open for 22% of the time, Pallas kernels for 47%

profile of v1, /device:TPU:0, one launch (start us, length us, event | category | flops | bytes accessed | tf_op | source)
XLA Modules:
  0.0 1550.3 jit_solution(5208944230121531105)
XLA Ops:
  0.7 6.7 multiply_reduce_fusion.6
  14.8 6.3 convolution_convert_fusion.1
  42.8 6.4 copy.250
  112.1 17.8 %collective-permute-done.3 = f32[128,2048]{0,1:T(8,128)S(1)} collective-permute-done((f32[128,2048]{0,1:T(8,128)S(1)}, f32[128,2048]{0,1:T(8,128)S(1)}, u32[]{:S(2)}, u32[]{:S(2)}) %collective-permute-start.3) | collective-permute-done | bytes 1048608 | tf_op jit(solution)/shard_map/ppermute | solution.py:355
  130.7 21.6 %collective-permute-done.8 = f32[128,2048]{0,1:T(8,128)S(1)} collective-permute-done((f32[128,2048]{0,1:T(8,128)S(1)}, f32[128,2048]{0,1:T(8,128)S(1)}, u32[]{:S(2)}, u32[]{:S(2)}) %collective-permute-start.8) | collective-permute-done | bytes 1048608 | tf_op jit(solution)/shard_map/ppermute | solution.py:355
  153.2 21.6 %collective-permute-done.13 = f32[128,2048]{0,1:T(8,128)S(1)} collective-permute-done((f32[128,2048]{0,1:T(8,128)S(1)}, f32[128,2048]{0,1:T(8,128)S(1)}, u32[]{:S(2)}, u32[]{:S(2)}) %collective-permute-start.13) | collective-permute-done | bytes 1048608 | tf_op jit(solution)/shard_map/ppermute | solution.py:355
  175.7 20.8 %collective-permute-done.18 = f32[128,2048]{0,1:T(8,128)S(1)} collective-permute-done((f32[128,2048]{0,1:T(8,128)S(1)}, f32[128,2048]{0,1:T(8,128)S(1)}, u32[]{:S(2)}, u32[]{:S(2)}) %collective-permute-start.18) | collective-permute-done | bytes 1048608 | tf_op jit(solution)/shard_map/ppermute | solution.py:355
  234.9 4.5 fusion.122
  246.7 4.9 fusion.123
  259.0 4.5 fusion.124
  299.4 9.7 collective-permute-done.6
  309.5 22.1 %collective-permute-done.11 = f32[128,2048]{0,1:T(8,128)S(1)} collective-permute-done((f32[128,2048]{0,1:T(8,128)S(1)}, f32[128,2048]{0,1:T(8,128)S(1)}, u32[]{:S(2)}, u32[]{:S(2)}) %collective-permute-start.11) | collective-permute-done | bytes 1048608 | tf_op jit(solution)/shard_map/ppermute | solution.py:355
  332.0 22.2 %collective-permute-done.16 = f32[128,2048]{0,1:T(8,128)S(1)} collective-permute-done((f32[128,2048]{0,1:T(8,128)S(1)}, f32[128,2048]{0,1:T(8,128)S(1)}, u32[]{:S(2)}, u32[]{:S(2)}) %collective-permute-start.16) | collective-permute-done | bytes 1048608 | tf_op jit(solution)/shard_map/ppermute | solution.py:355
  354.4 21.5 %collective-permute-done.21 = f32[128,2048]{0,1:T(8,128)S(1)} collective-permute-done((f32[128,2048]{0,1:T(8,128)S(1)}, f32[128,2048]{0,1:T(8,128)S(1)}, u32[]{:S(2)}, u32[]{:S(2)}) %collective-permute-start.21) | collective-permute-done | bytes 1048608 | tf_op jit(solution)/shard_map/ppermute | solution.py:355
  398.0 20.9 %multiply_convert_fusion.2 = (bf16[1024,2048]{1,0:T(8,128)(2,1)}, bf16[1024,2048]{1,0:T(8,128)(2,1)}) fusion(f32[1024,2048]{1,0:T(8,128)} %get-tuple-element.264, f32[1024,2048]{1,0:T(8,128)} %constant_dynamic-update-slice_fusion, bf16[1024,2048]{0,1:T(8,128)(2,1)} %fusion.38, bf16[2048,2048]{1,0:T(8,128)(2,1)} %param.27), kind=kOutput, calls=%fused_computation.7 | convolution fusion | flops 8617197568 | bytes 37748736 | tf_op jit(solution)/shard_map/dot_general | solution.py:226
  418.9 6.0 fusion.53
  425.0 5.9 fusion.56
  471.4 36.9 %collective-permute-done.28 = f32[128,2048]{0,1:T(8,128)S(1)} collective-permute-done((f32[128,2048]{0,1:T(8,128)S(1)}, f32[128,2048]{0,1:T(8,128)S(1)}, u32[]{:S(2)}, u32[]{:S(2)}) %collective-permute-start.28) | collective-permute-done | bytes 1048608 | tf_op jit(solution)/shard_map/ppermute | solution.py:355
  510.0 20.8 %collective-permute-done.34 = f32[128,2048]{0,1:T(8,128)S(1)} collective-permute-done((f32[128,2048]{0,1:T(8,128)S(1)}, f32[128,2048]{0,1:T(8,128)S(1)}, u32[]{:S(2)}, u32[]{:S(2)}) %collective-permute-start.34) | collective-permute-done | bytes 1048608 | tf_op jit(solution)/shard_map/ppermute | solution.py:355
  530.8 21.5 %collective-permute-done.30 = f32[128,2048]{0,1:T(8,128)S(1)} collective-permute-done((f32[128,2048]{0,1:T(8,128)S(1)}, f32[128,2048]{0,1:T(8,128)S(1)}, u32[]{:S(2)}, u32[]{:S(2)}) %collective-permute-start.30) | collective-permute-done | bytes 1048608 | tf_op jit(solution)/shard_map/ppermute | solution.py:355
  601.1 5.0 fusion.4
  606.6 6.1 add_convert_fusion
  641.0 16.3 %collective-permute-done.48 = f32[128,2048]{0,1:T(8,128)S(1)} collective-permute-done((f32[128,2048]{0,1:T(8,128)S(1)}, f32[128,2048]{0,1:T(8,128)S(1)}, u32[]{:S(2)}, u32[]{:S(2)}) %collective-permute-start.48) | collective-permute-done | bytes 1048608 | tf_op jit(solution)/shard_map/ppermute | solution.py:355
  657.7 22.1 %collective-permute-done.46 = f32[128,2048]{0,1:T(8,128)S(1)} collective-permute-done((f32[128,2048]{0,1:T(8,128)S(1)}, f32[128,2048]{0,1:T(8,128)S(1)}, u32[]{:S(2)}, u32[]{:S(2)}) %collective-permute-start.46) | collective-permute-done | bytes 1048608 | tf_op jit(solution)/shard_map/ppermute | solution.py:355
  680.0 22.3 %collective-permute-done.44 = f32[128,2048]{0,1:T(8,128)S(1)} collective-permute-done((f32[128,2048]{0,1:T(8,128)S(1)}, f32[128,2048]{0,1:T(8,128)S(1)}, u32[]{:S(2)}, u32[]{:S(2)}) %collective-permute-start.44) | collective-permute-done | bytes 1048608 | tf_op jit(solution)/shard_map/ppermute | solution.py:355
  702.4 21.4 %collective-permute-done.42 = f32[128,2048]{0,1:T(8,128)S(1)} collective-permute-done((f32[128,2048]{0,1:T(8,128)S(1)}, f32[128,2048]{0,1:T(8,128)S(1)}, u32[]{:S(2)}, u32[]{:S(2)}) %collective-permute-start.42) | collective-permute-done | bytes 1048608 | tf_op jit(solution)/shard_map/ppermute | solution.py:355
  727.2 7.9 pad_maximum_fusion.refs_5_
  735.6 37.6 %all-reduce = f32[8,640]{1,0:T(8,128)S(1)} all-reduce(f32[8,640]{1,0:T(8,128)S(1)} %pad_maximum_fusion.12), channel_id=2, replica_groups=mesh['dp'=8,'tensor'=4] {'dp'}, use_global_device_ids=true, to_apply=%region_36.37.clone | all-reduce | flops 5120 | bytes 40960
  782.1 6.4 copy.321
  788.5 730.0 %shard_map.246 = f32[16,256,512]{2,1,0:T(8,128)} custom-call(bf16[2048,1024]{1,0:T(8,128)(2,1)} %bitcast.33.refs_0_, bf16[2048,1024]{1,0:T(8,128)(2,1)} %bitcast.228, bf16[2048,1024]{1,0:T(8,128)(2,1)} %bitcast.227, bf16[2048,1024]{1,0:T(8,128)(2,1)} %bitcast.213, bf16[1024,2048]{1,0:T(8,128)(2,1)} %get-tuple-element.93.refs_4_, ...), custom_call_target="tpu_custom_call" | custom-call | tf_op jit(solution)/shard_map/pallas_call | solution.py:198
  1518.5 6.7 slice_bitcast_fusion.3
  1543.7 6.4 copy.322
  (560 shorter events, 356.7 us)
Async XLA Ops:
  11.2 29.0 %collective-permute-start = (f32[2,1024]{1,0:T(2,128)S(1)}, f32[2,1024]{1,0:T(2,128)S(1)}, u32[]{:S(2)}, u32[]{:S(2)}) collective-permute-start(f32[2,1024]{1,0:T(2,128)S(1)} %pad_maximum_fusion.14), channel_id=1, source_target_pairs={{0,1},{1,0},{2,3},{3,2},{4,5},{5,4},{6,7},{7,6},{8,9},{9,8},{10,11... | collective-permute-start | bytes 24584 | tf_op jit(solution)/shard_map/ppermute | solution.py:348
  40.2 16.0 %collective-permute-start.1 = (f32[2,1024]{1,0:T(2,128)S(1)}, f32[2,1024]{1,0:T(2,128)S(1)}, u32[]{:S(2)}, u32[]{:S(2)}) collective-permute-start(f32[2,1024]{1,0:T(2,128)S(1)} %fusion.110), channel_id=1, source_target_pairs={{0,2},{1,3},{2,0},{3,1},{4,6},{5,7},{6,4},{7,5},{8,10},{9,11},{10,... | collective-permute-start | bytes 24584 | tf_op jit(solution)/shard_map/ppermute | solution.py:355
  103.8 26.1 %collective-permute-start.3 = (f32[128,2048]{0,1:T(8,128)S(1)}, f32[128,2048]{0,1:T(8,128)S(1)}, u32[]{:S(2)}, u32[]{:S(2)}) collective-permute-start(f32[128,2048]{0,1:T(8,128)S(1)} %convolution_add_fusion.3), channel_id=1, source_target_pairs={{0,2},{1,3},{2,0},{3,1},{4,6},{5,7},{6,4},{7,5},{8,10},{9,11},{10,... | collective-permute-start | bytes 3145736 | tf_op jit(solution)/shard_map/ppermute | solution.py:355
  105.9 46.4 %collective-permute-start.8 = (f32[128,2048]{0,1:T(8,128)S(1)}, f32[128,2048]{0,1:T(8,128)S(1)}, u32[]{:S(2)}, u32[]{:S(2)}) collective-permute-start(f32[128,2048]{0,1:T(8,128)S(1)} %convolution_add_fusion.2), channel_id=1, source_target_pairs={{0,2},{1,3},{2,0},{3,1},{4,6},{5,7},{6,4},{7,5},{8,10},{9,11},{10,... | collective-permute-start | bytes 3145736 | tf_op jit(solution)/shard_map/ppermute | solution.py:355
  108.9 65.9 %collective-permute-start.13 = (f32[128,2048]{0,1:T(8,128)S(1)}, f32[128,2048]{0,1:T(8,128)S(1)}, u32[]{:S(2)}, u32[]{:S(2)}) collective-permute-start(f32[128,2048]{0,1:T(8,128)S(1)} %convolution_add_fusion.1), channel_id=1, source_target_pairs={{0,2},{1,3},{2,0},{3,1},{4,6},{5,7},{6,4},{7,5},{8,10},{9,11},{10,... | collective-permute-start | bytes 3145736 | tf_op jit(solution)/shard_map/ppermute | solution.py:355
  110.0 86.5 %collective-permute-start.18 = (f32[128,2048]{0,1:T(8,128)S(1)}, f32[128,2048]{0,1:T(8,128)S(1)}, u32[]{:S(2)}, u32[]{:S(2)}) collective-permute-start(f32[128,2048]{0,1:T(8,128)S(1)} %convolution_add_fusion), channel_id=1, source_target_pairs={{0,2},{1,3},{2,0},{3,1},{4,6},{5,7},{6,4},{7,5},{8,10},{9,11},{10,... | collective-permute-start | bytes 3145736 | tf_op jit(solution)/shard_map/ppermute | solution.py:355
  197.7 27.8 %collective-permute-start.4 = (f32[128,2048]{0,1:T(8,128)S(1)}, f32[128,2048]{0,1:T(8,128)}, u32[]{:S(2)}, u32[]{:S(2)}) collective-permute-start(f32[128,2048]{0,1:T(8,128)S(1)} %get-tuple-element.128), channel_id=1, source_target_pairs={{0,1},{1,0},{2,3},{3,2},{4,5},{5,4},{6,7},{7,6},{8,9},{9,8},{10,11... | collective-permute-start | bytes 3145736 | tf_op jit(solution)/shard_map/ppermute | solution.py:348
  199.3 40.3 %collective-permute-start.9 = (f32[128,2048]{0,1:T(8,128)}, f32[128,2048]{0,1:T(8,128)}, u32[]{:S(2)}, u32[]{:S(2)}) collective-permute-start(f32[128,2048]{0,1:T(8,128)} %get-tuple-element.125), channel_id=1, source_target_pairs={{0,1},{1,0},{2,3},{3,2},{4,5},{5,4},{6,7},{7,6},{8,9},{9,8},{10,11... | collective-permute-start | bytes 3145736 | tf_op jit(solution)/shard_map/ppermute | solution.py:348
  201.3 50.6 %collective-permute-start.14 = (f32[128,2048]{0,1:T(8,128)}, f32[128,2048]{0,1:T(8,128)}, u32[]{:S(2)}, u32[]{:S(2)}) collective-permute-start(f32[128,2048]{0,1:T(8,128)} %get-tuple-element.122), channel_id=1, source_target_pairs={{0,1},{1,0},{2,3},{3,2},{4,5},{5,4},{6,7},{7,6},{8,9},{9,8},{10,11... | collective-permute-start | bytes 3145736 | tf_op jit(solution)/shard_map/ppermute | solution.py:348
  202.8 60.9 %collective-permute-start.19 = (f32[128,2048]{0,1:T(8,128)}, f32[128,2048]{0,1:T(8,128)}, u32[]{:S(2)}, u32[]{:S(2)}) collective-permute-start(f32[128,2048]{0,1:T(8,128)} %get-tuple-element.119), channel_id=1, source_target_pairs={{0,1},{1,0},{2,3},{3,2},{4,5},{5,4},{6,7},{7,6},{8,9},{9,8},{10,11... | collective-permute-start | bytes 3145736 | tf_op jit(solution)/shard_map/ppermute | solution.py:348
  239.3 39.5 %collective-permute-start.5 = (f32[128,2048]{0,1:T(8,128)}, f32[128,2048]{0,1:T(8,128)}, u32[]{:S(2)}, u32[]{:S(2)}) collective-permute-start(f32[128,2048]{0,1:T(8,128)} %fusion.122), channel_id=1, source_target_pairs={{0,1},{1,0},{2,3},{3,2},{4,5},{5,4},{6,7},{7,6},{8,9},{9,8},{10,11... | collective-permute-start | bytes 3145736 | tf_op jit(solution)/shard_map/ppermute | solution.py:348
  251.6 31.9 %collective-permute-start.10 = (f32[128,2048]{0,1:T(8,128)}, f32[128,2048]{0,1:T(8,128)}, u32[]{:S(2)}, u32[]{:S(2)}) collective-permute-start(f32[128,2048]{0,1:T(8,128)} %fusion.123), channel_id=1, source_target_pairs={{0,1},{1,0},{2,3},{3,2},{4,5},{5,4},{6,7},{7,6},{8,9},{9,8},{10,11... | collective-permute-start | bytes 3145736 | tf_op jit(solution)/shard_map/ppermute | solution.py:348
  263.4 26.1 %collective-permute-start.15 = (f32[128,2048]{0,1:T(8,128)}, f32[128,2048]{0,1:T(8,128)}, u32[]{:S(2)}, u32[]{:S(2)}) collective-permute-start(f32[128,2048]{0,1:T(8,128)} %fusion.124), channel_id=1, source_target_pairs={{0,1},{1,0},{2,3},{3,2},{4,5},{5,4},{6,7},{7,6},{8,9},{9,8},{10,11... | collective-permute-start | bytes 3145736 | tf_op jit(solution)/shard_map/ppermute | solution.py:348
  274.2 20.1 %collective-permute-start.20 = (f32[128,2048]{0,1:T(8,128)S(1)}, f32[128,2048]{0,1:T(8,128)S(1)}, u32[]{:S(2)}, u32[]{:S(2)}) collective-permute-start(f32[128,2048]{0,1:T(8,128)S(1)} %fusion.125), channel_id=1, source_target_pairs={{0,1},{1,0},{2,3},{3,2},{4,5},{5,4},{6,7},{7,6},{8,9},{9,8},{10,11... | collective-permute-start | bytes 3145736 | tf_op jit(solution)/shard_map/ppermute | solution.py:348
  283.1 26.1 %collective-permute-start.6 = (f32[128,2048]{0,1:T(8,128)S(1)}, f32[128,2048]{0,1:T(8,128)S(1)}, u32[]{:S(2)}, u32[]{:S(2)}) collective-permute-start(f32[128,2048]{0,1:T(8,128)S(1)} %convolution_add_fusion.19), channel_id=1, source_target_pairs={{0,2},{1,3},{2,0},{3,1},{4,6},{5,7},{6,4},{7,5},{8,10},{9,11},{10,... | collective-permute-start | bytes 3145736 | tf_op jit(solution)/shard_map/ppermute | solution.py:355
  287.8 43.8 %collective-permute-start.11 = (f32[128,2048]{0,1:T(8,128)S(1)}, f32[128,2048]{0,1:T(8,128)S(1)}, u32[]{:S(2)}, u32[]{:S(2)}) collective-permute-start(f32[128,2048]{0,1:T(8,128)S(1)} %convolution_add_fusion.18), channel_id=1, source_target_pairs={{0,2},{1,3},{2,0},{3,1},{4,6},{5,7},{6,4},{7,5},{8,10},{9,11},{10,... | collective-permute-start | bytes 3145736 | tf_op jit(solution)/shard_map/ppermute | solution.py:355
  293.9 60.3 %collective-permute-start.16 = (f32[128,2048]{0,1:T(8,128)S(1)}, f32[128,2048]{0,1:T(8,128)S(1)}, u32[]{:S(2)}, u32[]{:S(2)}) collective-permute-start(f32[128,2048]{0,1:T(8,128)S(1)} %convolution_add_fusion.17), channel_id=1, source_target_pairs={{0,2},{1,3},{2,0},{3,1},{4,6},{5,7},{6,4},{7,5},{8,10},{9,11},{10,... | collective-permute-start | bytes 3145736 | tf_op jit(solution)/shard_map/ppermute | solution.py:355
  297.7 78.2 %collective-permute-start.21 = (f32[128,2048]{0,1:T(8,128)S(1)}, f32[128,2048]{0,1:T(8,128)S(1)}, u32[]{:S(2)}, u32[]{:S(2)}) collective-permute-start(f32[128,2048]{0,1:T(8,128)S(1)} %convolution_add_fusion.16), channel_id=1, source_target_pairs={{0,2},{1,3},{2,0},{3,1},{4,6},{5,7},{6,4},{7,5},{8,10},{9,11},{10,... | collective-permute-start | bytes 3145736 | tf_op jit(solution)/shard_map/ppermute | solution.py:355
  381.8 394.8 %collective-permute-start.22 = (f32[512,2048]{0,1:T(8,128)}, f32[512,2048]{0,1:T(8,128)}, u32[]{:S(2)}, u32[]{:S(2)}) collective-permute-start(f32[512,2048]{0,1:T(8,128)} %fusion.14), channel_id=1, source_target_pairs={{0,1},{1,0},{2,3},{3,2},{4,5},{5,4},{6,7},{7,6},{8,9},{9,8},{10,11... | collective-permute-start | bytes 12582920 | tf_op jit(solution)/shard_map/ppermute | solution.py:348
  443.9 13.5 collective-permute-start.31
  446.3 18.0 %collective-permute-start.33 = (f32[128,2048]{0,1:T(8,128)S(1)}, f32[128,2048]{0,1:T(8,128)S(1)}, u32[]{:S(2)}, u32[]{:S(2)}) collective-permute-start(f32[128,2048]{0,1:T(8,128)S(1)} %convolution_add_fusion.8), channel_id=1, source_target_pairs={{0,1},{1,0},{2,3},{3,2},{4,5},{5,4},{6,7},{7,6},{8,9},{9,8},{10,11... | collective-permute-start | bytes 3145736 | tf_op jit(solution)/shard_map/ppermute | solution.py:348
  449.3 17.8 %collective-permute-start.29 = (f32[128,2048]{0,1:T(8,128)S(1)}, f32[128,2048]{0,1:T(8,128)S(1)}, u32[]{:S(2)}, u32[]{:S(2)}) collective-permute-start(f32[128,2048]{0,1:T(8,128)S(1)} %convolution_add_fusion.12), channel_id=1, source_target_pairs={{0,1},{1,0},{2,3},{3,2},{4,5},{5,4},{6,7},{7,6},{8,9},{9,8},{10,11... | collective-permute-start | bytes 3145736 | tf_op jit(solution)/shard_map/ppermute | solution.py:348
  459.8 50.2 %collective-permute-start.32 = (f32[128,2048]{0,1:T(8,128)S(1)}, f32[128,2048]{0,1:T(8,128)S(1)}, u32[]{:S(2)}, u32[]{:S(2)}) collective-permute-start(f32[128,2048]{0,1:T(8,128)S(1)} %fusion.18), channel_id=1, source_target_pairs={{0,2},{1,3},{2,0},{3,1},{4,6},{5,7},{6,4},{7,5},{8,10},{9,11},{10,... | collective-permute-start | bytes 3145736 | tf_op jit(solution)/shard_map/ppermute | solution.py:355
  462.5 45.8 %collective-permute-start.28 = (f32[128,2048]{0,1:T(8,128)S(1)}, f32[128,2048]{0,1:T(8,128)S(1)}, u32[]{:S(2)}, u32[]{:S(2)}) collective-permute-start(f32[128,2048]{0,1:T(8,128)S(1)} %fusion.16), channel_id=1, source_target_pairs={{0,2},{1,3},{2,0},{3,1},{4,6},{5,7},{6,4},{7,5},{8,10},{9,11},{10,... | collective-permute-start | bytes 3145736 | tf_op jit(solution)/shard_map/ppermute | solution.py:355
  466.7 64.1 %collective-permute-start.34 = (f32[128,2048]{0,1:T(8,128)S(1)}, f32[128,2048]{0,1:T(8,128)S(1)}, u32[]{:S(2)}, u32[]{:S(2)}) collective-permute-start(f32[128,2048]{0,1:T(8,128)S(1)} %fusion.19), channel_id=1, source_target_pairs={{0,2},{1,3},{2,0},{3,1},{4,6},{5,7},{6,4},{7,5},{8,10},{9,11},{10,... | collective-permute-start | bytes 3145736 | tf_op jit(solution)/shard_map/ppermute | solution.py:355
  469.6 82.7 %collective-permute-start.30 = (f32[128,2048]{0,1:T(8,128)S(1)}, f32[128,2048]{0,1:T(8,128)S(1)}, u32[]{:S(2)}, u32[]{:S(2)}) collective-permute-start(f32[128,2048]{0,1:T(8,128)S(1)} %fusion.17), channel_id=1, source_target_pairs={{0,2},{1,3},{2,0},{3,1},{4,6},{5,7},{6,4},{7,5},{8,10},{9,11},{10,... | collective-permute-start | bytes 3145736 | tf_op jit(solution)/shard_map/ppermute | solution.py:355
  509.5 47.9 %collective-permute-start.35 = (f32[128,2048]{0,1:T(8,128)S(1)}, f32[128,2048]{0,1:T(8,128)S(1)}, u32[]{:S(2)}, u32[]{:S(2)}) collective-permute-start(f32[128,2048]{0,1:T(8,128)S(1)} %broadcast_multiply_fusion.3), channel_id=1, source_target_pairs={{0,1},{1,0},{2,3},{3,2},{4,5},{5,4},{6,7},{7,6},{8,9},{9,8},{10,11... | collective-permute-start | bytes 3145736 | tf_op jit(solution)/shard_map/ppermute | solution.py:348
  631.2 26.1 %collective-permute-start.48 = (f32[128,2048]{0,1:T(8,128)S(1)}, f32[128,2048]{0,1:T(8,128)S(1)}, u32[]{:S(2)}, u32[]{:S(2)}) collective-permute-start(f32[128,2048]{0,1:T(8,128)S(1)} %convolution_add_fusion.4), channel_id=1, source_target_pairs={{0,2},{1,3},{2,0},{3,1},{4,6},{5,7},{6,4},{7,5},{8,10},{9,11},{10,... | collective-permute-start | bytes 3145736 | tf_op jit(solution)/shard_map/ppermute | solution.py:355
  634.8 45.0 %collective-permute-start.46 = (f32[128,2048]{0,1:T(8,128)S(1)}, f32[128,2048]{0,1:T(8,128)S(1)}, u32[]{:S(2)}, u32[]{:S(2)}) collective-permute-start(f32[128,2048]{0,1:T(8,128)S(1)} %convolution_add_fusion.5), channel_id=1, source_target_pairs={{0,2},{1,3},{2,0},{3,1},{4,6},{5,7},{6,4},{7,5},{8,10},{9,11},{10,... | collective-permute-start | bytes 3145736 | tf_op jit(solution)/shard_map/ppermute | solution.py:355
  637.0 65.2 %collective-permute-start.44 = (f32[128,2048]{0,1:T(8,128)S(1)}, f32[128,2048]{0,1:T(8,128)S(1)}, u32[]{:S(2)}, u32[]{:S(2)}) collective-permute-start(f32[128,2048]{0,1:T(8,128)S(1)} %convolution_add_fusion.6), channel_id=1, source_target_pairs={{0,2},{1,3},{2,0},{3,1},{4,6},{5,7},{6,4},{7,5},{8,10},{9,11},{10,... | collective-permute-start | bytes 3145736 | tf_op jit(solution)/shard_map/ppermute | solution.py:355
  640.6 83.2 %collective-permute-start.42 = (f32[128,2048]{0,1:T(8,128)S(1)}, f32[128,2048]{0,1:T(8,128)S(1)}, u32[]{:S(2)}, u32[]{:S(2)}) collective-permute-start(f32[128,2048]{0,1:T(8,128)S(1)} %convolution_add_fusion.7), channel_id=1, source_target_pairs={{0,2},{1,3},{2,0},{3,1},{4,6},{5,7},{6,4},{7,5},{8,10},{9,11},{10,... | collective-permute-start | bytes 3145736 | tf_op jit(solution)/shard_map/ppermute | solution.py:355
  726.6 811.6 %collective-permute-start.49 = (f32[512,2048]{0,1:T(8,128)}, f32[512,2048]{0,1:T(8,128)}, u32[]{:S(2)}, u32[]{:S(2)}) collective-permute-start(f32[512,2048]{0,1:T(8,128)} %fusion.12), channel_id=1, source_target_pairs={{0,1},{1,0},{2,3},{3,2},{4,5},{5,4},{6,7},{7,6},{8,9},{9,8},{10,11... | collective-permute-start | bytes 12582920 | tf_op jit(solution)/shard_map/ppermute | solution.py:348
  (144 other events, 2353.9 us)

commit v2 on v1

v2 whole, which is shorter than its diff:
```python
import functools

import jax
import jax.numpy as jnp
from jax import lax
from jax.experimental import pallas as pl
from jax.experimental.pallas import tpu as pltpu
from jax.sharding import PartitionSpec as P

HEAD = 128
LENGTH = 1024
EPSILON = 1e-06
NEG_FILL = -1e30
ROPE_BASE = 500000.0
ROW_CHUNKS = 4
F32 = jnp.float32
BF16 = jnp.bfloat16


COLS = 256
SPAN = 6
Y_SLOTS = 3
B_SLOTS = 5
HBM_NAMES = (
    "gdrt", "hlt", "tokens", "inner", "mixed", "gdr", "gate", "up", "branch", "seed",
    "query", "key", "value", "query_raw", "key_raw",
    "w_out", "w_gate", "w_up", "w_down", "w_query", "w_key", "w_value",
)
TILE = 512
VMEM_LIMIT = 63 * 1024 * 1024
MESH = pl.DeviceIdType.MESH

def column_sum(values):
    return jnp.sum(values, axis=0, keepdims=True)


def mean_inverse(values):
    return lax.rsqrt(jnp.mean(values * values, axis=1, keepdims=True) + EPSILON)


def tensor_peers():
    at = lax.axis_index("tensor")
    core = lax.rem(at, 2)
    return core, at + 1 - 2 * core, lax.rem(at + 2, 4)


def greet(*peers):
    barrier = pltpu.get_barrier_semaphore()
    for peer in peers:
        pl.semaphore_signal(barrier, inc=1, device_id=peer, device_id_type=MESH)
    pl.semaphore_wait(barrier, len(peers))


def forward_kernel(
    mixed, w_out, attn_gain, mlp_gain, tok_hbm, seed_hbm, wg_hbm, wu_hbm, wd_hbm,
    gate_out, up_out, inner_out, hlt_out, gdr_out, gdrt_out, branch_out, out_out, gain_out,
    wg, wu, wd, cs, crecv, xs, xr, xr2, ag, gate_buf, up_buf, inner_buf, low_buf, hlt_buf,
    out_buf, tok, seed,
    w_sem, t_sem, s_sem, cs_sem, cr_sem, xs_sem, xr_sem, as_sem, ar_sem, cs2_sem, cr2_sem, xs2_sem, xr2_sem,
    gs_sem, gr_sem, os_sem, or_sem, g_sem, h_sem, b_sem, d_sem, o_sem,
):
    core, sibling, across = tensor_peers()
    chunk = xs.shape[1]
    half = chunk * ROW_CHUNKS
    tiles = wg.shape[1] // TILE
    wide_tiles = wd.shape[1] // TILE
    loads = [
        pltpu.make_async_copy(src, dst, w_sem.at[i])
        for i, (src, dst) in enumerate(((wg_hbm, wg), (wu_hbm, wu), (wd_hbm, wd)))
    ]
    for load in loads:
        load.start()

    def row_load(c, src, dst, sem):
        return pltpu.make_async_copy(
            src.at[pl.ds(c * chunk, chunk)], dst.at[c % 2], sem.at[c % 2])

    for c in range(2):
        row_load(c, tok_hbm, tok, t_sem).start()
        row_load(c, seed_hbm, seed, s_sem).start()
    greet({"tensor": sibling}, {"tensor": across})

    def remote(src, dst, send_sem, recv_sem, peer):
        return pltpu.make_async_remote_copy(
            src_ref=src, dst_ref=dst, send_sem=send_sem, recv_sem=recv_sem,
            device_id={"tensor": peer}, device_id_type=MESH)

    def core_copy(c):
        return remote(cs.at[c % 2], crecv.at[c], cs_sem.at[c], cr_sem.at[c], sibling)

    def x_copy(c):
        return remote(xs.at[c], xr.at[c], xs_sem.at[c], xr_sem.at[c], across)

    def hidden_copy(c):
        return remote(xr.at[c], ag.at[c % 2], as_sem.at[c], ar_sem.at[c], sibling)

    def core2_copy(c):
        return remote(cs.at[c % 2], crecv.at[c], cs2_sem.at[c], cr2_sem.at[c], sibling)

    def x2_copy(c):
        return remote(xs.at[c], xr2.at[c], xs2_sem.at[c], xr2_sem.at[c], across)

    def grad_copy(c):
        return remote(xr2.at[c], ag.at[c % 2], gs_sem.at[c], gr_sem.at[c], sibling)

    def out_copy(c):
        return remote(xr.at[c], crecv.at[c], os_sem.at[c], or_sem.at[c], sibling)

    def rows(first):
        return pl.ds(first, chunk)

    def side_copies(buf, dst, sem, c):
        return [
            pltpu.make_async_copy(
                buf.at[pl.ds(s * chunk, chunk)], dst.at[rows(s * half + c * chunk)], sem.at[s])
            for s in range(2)
        ]

    def turned_copies(buf, dst, sem, c):
        return [
            pltpu.make_async_copy(
                buf.at[:, pl.ds(s * chunk, chunk)], dst.at[:, rows(s * half + c * chunk)], sem.at[s])
            for s in range(2)
        ]

    for c in range(ROW_CHUNKS):
        if c >= 2:
            core_copy(c - 2).wait_send()
        cs[c % 2] = jnp.dot(mixed[rows(half + c * chunk), :], w_out[...], preferred_element_type=F32)
        core_copy(c).start()
        xs[c] = jnp.dot(mixed[rows(c * chunk), :], w_out[...], preferred_element_type=F32)
        if c >= 1:
            core_copy(c - 1).wait_recv()
            xs[c - 1] += crecv[c - 1]
            x_copy(c - 1).start()
    last = ROW_CHUNKS - 1
    core_copy(last).wait_recv()
    xs[last] += crecv[last]
    x_copy(last).start()
    core_copy(last - 1).wait_send()
    core_copy(last).wait_send()

    def feed(c):
        x_copy(c).wait()
        total = xs[c] + xr[c]
        xs[c] = total
        branch_copy = pltpu.make_async_copy(xs.at[c], branch_out.at[rows(c * chunk)], b_sem)
        branch_copy.start()
        row_load(c, tok_hbm, tok, t_sem).wait()
        hidden = tok[c % 2].astype(F32) + total * mean_inverse(total) * attn_gain[...]
        if c + 2 < ROW_CHUNKS:
            row_load(c + 2, tok_hbm, tok, t_sem).start()
        xr[c] = hidden
        hidden_copy(c).start()
        low_buf[0:chunk, :] = hidden.astype(BF16)
        if c >= 1:
            for copy in turned_copies(hlt_buf, hlt_out, h_sem, c - 1):
                copy.wait()
            for buf, dst, i in ((gate_buf, gate_out, 0), (up_buf, up_out, 1), (inner_buf, inner_out, 2)):
                for copy in side_copies(buf, dst, g_sem.at[i], c - 1):
                    copy.wait()
        hlt_buf[:, 0:chunk] = hidden.astype(BF16).T
        hidden_copy(c).wait_recv()
        low_buf[chunk : 2 * chunk, :] = ag[c % 2].astype(BF16)
        hlt_buf[:, chunk : 2 * chunk] = ag[c % 2].astype(BF16).T
        for copy in turned_copies(hlt_buf, hlt_out, h_sem, c):
            copy.start()
        if c == 0:
            loads[0].wait()
            loads[1].wait()

        def tile(n, carry):
            at = pl.ds(pl.multiple_of(n * TILE, TILE), TILE)
            gate = jnp.dot(low_buf[...], wg[:, at], preferred_element_type=F32)
            up = jnp.dot(low_buf[...], wu[:, at], preferred_element_type=F32)
            gate_buf[:, at] = gate
            up_buf[:, at] = up
            inner_buf[:, at] = (gate * jax.nn.sigmoid(gate) * up).astype(BF16)
            return carry
        lax.fori_loop(0, tiles, tile, 0)
        for buf, dst, i in ((gate_buf, gate_out, 0), (up_buf, up_out, 1), (inner_buf, inner_out, 2)):
            for copy in side_copies(buf, dst, g_sem.at[i], c):
                copy.start()
        if c == 0:
            loads[2].wait()
        if c >= 2:
            core2_copy(c - 2).wait_send()
        branch_copy.wait()

        def down_tile(n, carry):
            at = pl.ds(pl.multiple_of(n * TILE, TILE), TILE)
            part = jnp.dot(inner_buf[...], wd[:, at], preferred_element_type=F32)
            xs[c, :, at] = part[0:chunk]
            cs[c % 2, :, at] = part[chunk : 2 * chunk]
            return carry
        lax.fori_loop(0, wide_tiles, down_tile, 0)
        core2_copy(c).start()
        core2_copy(c).wait_recv()
        xs[c] += crecv[c]
        x2_copy(c).start()

    def finish(c, gain_total):
        x2_copy(c).wait()
        down = xs[c] + xr2[c]
        inv = mean_inverse(down)
        row_load(c, seed_hbm, seed, s_sem).wait()
        seed_rows = seed[c % 2].astype(F32)
        if c + 2 < ROW_CHUNKS:
            row_load(c + 2, seed_hbm, seed, s_sem).start()
        normed = down * inv
        gain_total = gain_total + column_sum(seed_rows * normed)
        scaled = seed_rows * mlp_gain[...]
        dot = jnp.sum(scaled * down, axis=1, keepdims=True)
        grad = inv * scaled - down * (inv * inv * inv * dot / down.shape[1])
        hidden_copy(c).wait_send()
        xr2[c] = grad
        grad_copy(c).start()
        xr[c] = xr[c] + normed * mlp_gain[...]
        if c == 0:
            for copy in turned_copies(hlt_buf, hlt_out, h_sem, last):
                copy.wait()
        if c >= 1:
            for copy in turned_copies(hlt_buf, gdrt_out, d_sem.at[0], c - 1):
                copy.wait()
            for copy in side_copies(low_buf, gdr_out, d_sem.at[1], c - 1):
                copy.wait()
        low_buf[0:chunk, :] = grad.astype(BF16)
        hlt_buf[:, 0:chunk] = grad.astype(BF16).T
        grad_copy(c).wait_recv()
        out_copy(c).start()
        low_buf[chunk : 2 * chunk, :] = ag[c % 2].astype(BF16)
        hlt_buf[:, chunk : 2 * chunk] = ag[c % 2].astype(BF16).T
        for copy in turned_copies(hlt_buf, gdrt_out, d_sem.at[0], c):
            copy.start()
        for copy in side_copies(low_buf, gdr_out, d_sem.at[1], c):
            copy.start()
        return gain_total

    def out_copies(c):
        return [
            pltpu.make_async_copy(
                out_buf.at[pl.ds(s * chunk, chunk)],
                out_out.at[pl.ds(pl.multiple_of(at * half + c * chunk, chunk), chunk)], o_sem.at[s])
            for s, at in ((0, core), (1, 1 - core))
        ]

    def place(c):
        if c >= 1:
            for copy in out_copies(c - 1):
                copy.wait()
        out_buf[0:chunk, :] = xr[c].astype(BF16)
        out_copy(c).wait_recv()
        out_buf[chunk : 2 * chunk, :] = crecv[c].astype(BF16)
        for copy in out_copies(c):
            copy.start()

    for c in range(ROW_CHUNKS):
        feed(c)
    gain_total = jnp.zeros(mlp_gain.shape, F32)
    for c in range(ROW_CHUNKS):
        gain_total = finish(c, gain_total)
        if c >= 1:
            place(c - 1)
    place(last)
    gain_out[...] = gain_total
    for buf, dst, i in ((gate_buf, gate_out, 0), (up_buf, up_out, 1), (inner_buf, inner_out, 2)):
        for copy in side_copies(buf, dst, g_sem.at[i], last):
            copy.wait()
    for copy in turned_copies(hlt_buf, gdrt_out, d_sem.at[0], last):
        copy.wait()
    for copy in side_copies(low_buf, gdr_out, d_sem.at[1], last):
        copy.wait()
    for copy in out_copies(last):
        copy.wait()
    core2_copy(last - 1).wait_send()
    core2_copy(last).wait_send()
    for c in range(ROW_CHUNKS):
        grad_copy(c).wait_send()
        out_copy(c).wait_send()


def forward_layer(mixed, w_out, attn_gain, mlp_gain, tok, seed, w_gate, w_up, w_down):
    row_count, width = mixed.shape[0], w_out.shape[1]
    hidden = w_gate.shape[1]
    chunk = row_count // 2 // ROW_CHUNKS
    DMA = pltpu.SemaphoreType.DMA
    vmem, any_space = pl.BlockSpec(memory_space=pltpu.VMEM), pl.BlockSpec(memory_space=pl.ANY)

    def shape(*dims, kind=F32):
        return jax.ShapeDtypeStruct(dims, kind)

    per_chunk = DMA((ROW_CHUNKS,))
    return pl.pallas_call(
        forward_kernel,
        out_shape=(
            shape(row_count, hidden),
            shape(row_count, hidden),
            shape(row_count, hidden, kind=BF16),
            shape(width, row_count, kind=BF16),
            shape(row_count, width, kind=BF16),
            shape(width, row_count, kind=BF16),
            shape(row_count // 2, width),
            shape(row_count, width, kind=BF16),
            shape(1, width),
        ),
        in_specs=[vmem] * 4 + [any_space] * 5,
        out_specs=(any_space,) * 8 + (vmem,),
        scratch_shapes=[
            pltpu.VMEM(w_gate.shape, BF16),
            pltpu.VMEM(w_up.shape, BF16),
            pltpu.VMEM(w_down.shape, BF16),
            pltpu.VMEM((2, chunk, width), F32),
            pltpu.VMEM((ROW_CHUNKS, chunk, width), F32),
            pltpu.VMEM((ROW_CHUNKS, chunk, width), F32),
            pltpu.VMEM((ROW_CHUNKS, chunk, width), F32),
            pltpu.VMEM((ROW_CHUNKS, chunk, width), F32),
            pltpu.VMEM((2, chunk, width), F32),
            pltpu.VMEM((2 * chunk, hidden), F32),
            pltpu.VMEM((2 * chunk, hidden), F32),
            pltpu.VMEM((2 * chunk, hidden), BF16),
            pltpu.VMEM((2 * chunk, width), BF16),
            pltpu.VMEM((width, 2 * chunk), BF16),
            pltpu.VMEM((2 * chunk, width), BF16),
            pltpu.VMEM((2, chunk, width), BF16),
            pltpu.VMEM((2, chunk, width), BF16),
            DMA((3,)),
            DMA((2,)),
            DMA((2,)),
        ]
        + [per_chunk] * 14
        + [DMA((3, 2)), DMA((2,)), DMA, DMA((2, 2)), DMA((2,))],
        compiler_params=pltpu.CompilerParams(
            collective_id=1, has_side_effects=True, vmem_limit_bytes=VMEM_LIMIT),
    )(mixed, w_out, attn_gain, mlp_gain, tok, seed, w_gate, w_up, w_down)


def backward_kernel(
    dp_size, counts,
    gdrt_hbm, hlt_hbm, tok_hbm, inner_hbm, mixed_hbm, gdr_hbm, gate_hbm, up_hbm, branch_hbm, seed_hbm,
    query_hbm, key_hbm, value_hbm, query_raw_hbm, key_raw_hbm,
    w_out_hbm, wg_hbm, wu_hbm, wd_hbm, wq_hbm, wk_hbm, wv_hbm,
    query_inv, key_inv, log_totals, seg_col, seg_row, live_col, cosine, sine,
    query_gain, key_gain, attn_gain, gain_mlp_part,
    turned_out, straight_out, token_out, gains_out,
    ggr_hbm, gur_hbm, gbt_hbm, gh_hbm, gqkv_hbm,
    at, bbuf, ysend, yrecv, zsend, zrecv, stage, stage_t, cs, crecv, xs, xr, ag, dots, dots_in,
    vec, vec_in,
    at_sem, b_sem, ys_sem, yr_sem, zs_sem, zr_sem, out_sem,
    cs_sem, cr_sem, xs_sem, xr_sem, as_sem, ar_sem, cs2_sem, cr2_sem, xs2_sem, xr2_sem, as2_sem,
    ar2_sem, ds_sem, dr_sem, vs_sem, vr_sem, w_sem,
    y_credit, up_credit, down_credit,
):
    n_down, n_hidden, n_heads, n_out = counts
    first_heads = n_down + n_hidden
    first_out = first_heads + n_heads
    total = first_out + n_out
    line = dp_size // 2
    width = at.shape[1]
    block = width // dp_size
    chunk = xs.shape[1]
    half = chunk * ROW_CHUNKS
    full = 2 * half
    head_cols = query_hbm.shape[1]
    passes = total + total // SPAN
    dp_at = lax.axis_index("dp")
    z, y = dp_at // 2, dp_at % 2
    partner = dp_at + 1 - 2 * y
    below, above = dp_at - 2, dp_at + 2
    has_below, has_above = z > 0, z < line - 1
    core, sibling, across = tensor_peers()
    steps = [1 << s for s in range(dp_size.bit_length() - 1)]
    vec_peers = [dp_at + bit * (1 - 2 * ((dp_at // bit) % 2)) for bit in steps]

    def at_dp(i):
        return {"dp": i}

    def at_tensor(i):
        return {"tensor": i}

    barrier = pltpu.get_barrier_semaphore()

    def greet_one(peer):
        pl.semaphore_signal(barrier, inc=1, device_id=peer, device_id_type=MESH)

    other_z = z - 1 + 2 * lax.rem(z, 2)
    has_other = (other_z >= 0) & (other_z < line)
    for peer in vec_peers:
        greet_one(at_dp(peer))
    greet_one(at_tensor(sibling))
    greet_one(at_tensor(across))

    @pl.when(has_other)
    def _():
        greet_one(at_dp(2 * other_z + y))
    pl.semaphore_wait(barrier, len(steps) + 2 + has_other.astype(jnp.int32))

    def remote(src, dst, send_sem, recv_sem, peer):
        return pltpu.make_async_remote_copy(
            src_ref=src, dst_ref=dst, send_sem=send_sem, recv_sem=recv_sem,
            device_id=peer, device_id_type=MESH)

    def y_copy(p, b):
        return remote(ysend.at[p, b], yrecv.at[p, b], ys_sem.at[p, b], yr_sem.at[p, b], at_dp(partner))

    def z_copy(p, b, slot, target):
        return remote(zsend.at[p, b], zrecv.at[p, slot], zs_sem.at[p, b], zr_sem.at[p, slot], at_dp(target))

    def group_of(k):
        return (
            (k >= n_down).astype(jnp.int32)
            + (k >= first_heads).astype(jnp.int32)
            + (k >= first_out).astype(jnp.int32))

    def product(k, rows_at):
        return jnp.dot(
            at[lax.rem(group_of(k), 2), pl.ds(pl.multiple_of(rows_at * block, block), block), :],
            bbuf[lax.rem(k, B_SLOTS)], preferred_element_type=F32)

    def at_load(i):
        src = (gdrt_hbm, hlt_hbm, None, gbt_hbm)[i]
        return pltpu.make_async_copy(src, at.at[i % 2], at_sem.at[i % 2])

    def b_load(k, act):
        def columns(src, at_chunk):
            act(pltpu.make_async_copy(
                src.at[:, pl.ds(pl.multiple_of(at_chunk * COLS, COLS), COLS)],
                bbuf.at[lax.rem(k, B_SLOTS)], b_sem.at[lax.rem(k, B_SLOTS)]))
        per = n_hidden // 2

        @pl.when(k < n_down)
        def _():
            columns(inner_hbm, k)

        @pl.when((k >= n_down) & (k < n_down + per))
        def _():
            columns(ggr_hbm, k - n_down)

        @pl.when((k >= n_down + per) & (k < first_heads))
        def _():
            columns(gur_hbm, k - n_down - per)

        @pl.when((k >= first_heads) & (k < first_out))
        def _():
            columns(gqkv_hbm, k - first_heads)

        @pl.when((k >= first_out) & (k < total))
        def _():
            columns(mixed_hbm, k - first_out)

    def line_first(k):
        return lax.rem(k, SPAN) == SPAN - 1

    def walk(fn):
        def body(i, carry):
            @pl.when(z <= i)
            def _():
                fn(z + line - 1 - i, True)

            @pl.when(z >= line - 1 - i)
            def _():
                fn(z - (line - 1 - i), False)
            return carry
        lax.fori_loop(0, line - 1, body, 0)

    def pair_send(k):
        p = lax.rem(k, Y_SLOTS)

        @pl.when(k >= Y_SLOTS)
        def _():
            pl.semaphore_wait(y_credit, 1)
        b_load(k, lambda copy: copy.wait())

        @pl.when(jnp.logical_not(line_first(k)))
        def _():
            def one(b, up=None):
                ysend[p, b] = product(k, 2 * b + 1 - y)
                y_copy(p, b).start()
            walk(one)
            one(z)

    def line_send(q, k, source):
        p = lax.rem(q, 2)

        @pl.when(q >= 2)
        def _():
            @pl.when(has_above)
            def _():
                pl.semaphore_wait(up_credit, 1)

            @pl.when(has_below)
            def _():
                pl.semaphore_wait(down_credit, 1)

        def one(b, up):
            has_before, target = (has_below, above) if up else (has_above, below)
            zsend[p, b] = source(b)

            @pl.when(has_before)
            def _():
                z_copy(p, b, b, target).wait_recv()
                zsend[p, b] += zrecv[p, b]
            if up:
                z_copy(p, b, b, target).start()
            else:
                @pl.when(b == z - 1)
                def _():
                    z_copy(p, b, line, target).start()

                @pl.when(b != z - 1)
                def _():
                    z_copy(p, b, b, target).start()
        walk(one)

    def line_own(q, dst):
        p = lax.rem(q, 2)

        @pl.when(has_below)
        def _():
            z_copy(p, z, z, below).wait_recv()
            dst[...] += zrecv[p, z]

        @pl.when(has_above)
        def _():
            z_copy(p, z, line, below).wait_recv()
            dst[...] += zrecv[p, line]

        def drain(b, up):
            z_copy(p, b, b, below).wait_send()
        walk(drain)

        @pl.when(q < passes - 2)
        def _():
            @pl.when(has_below)
            def _():
                pl.semaphore_signal(up_credit, inc=1, device_id=at_dp(below), device_id_type=MESH)

            @pl.when(has_above)
            def _():
                pl.semaphore_signal(down_credit, inc=1, device_id=at_dp(above), device_id_type=MESH)

    def is_turned(k):
        return (k < n_down) | (k >= first_out)

    def out_act(k, act):
        @pl.when(is_turned(k))
        def _():
            first = jnp.where(k < n_down, k, k - first_out + n_down) * COLS
            act(pltpu.make_async_copy(
                stage_t, turned_out.at[pl.ds(pl.multiple_of(first, COLS), COLS)], out_sem))

        @pl.when(jnp.logical_not(is_turned(k)))
        def _():
            cols = pl.ds(pl.multiple_of((k - n_down) * COLS, COLS), COLS)
            act(pltpu.make_async_copy(stage, straight_out.at[:, cols], out_sem))

    def finish_chunk(k, q):
        p = lax.rem(k, Y_SLOTS)

        @pl.when(k >= 1)
        def _():
            out_act(k - 1, lambda copy: copy.wait())
        stage[...] = product(k, 2 * z + y)
        y_copy(p, z).wait_recv()
        stage[...] += yrecv[p, z]
        line_own(q, stage)

        @pl.when(is_turned(k))
        def _():
            stage_t[...] = stage[...].T
        out_act(k, lambda copy: copy.start())

        @pl.when(line_first(k))
        def _():
            y_copy(p, z).wait_send()

        @pl.when(jnp.logical_not(line_first(k)))
        def _():
            for b in range(line):
                y_copy(p, b).wait_send()

        @pl.when(k < total - Y_SLOTS)
        def _():
            pl.semaphore_signal(y_credit, inc=1, device_id=at_dp(partner), device_id_type=MESH)

    def tick(k):
        p = lax.rem(k, Y_SLOTS)
        q = k + k // SPAN
        is_line_first = line_first(k)

        @pl.when(jnp.logical_not(is_line_first))
        def _():
            def mine(b):
                part = product(k, 2 * b + y)
                y_copy(p, b).wait_recv()
                return part + yrecv[p, b]
            line_send(q, k, mine)

        @pl.when(is_line_first)
        def _():
            line_send(q, k, lambda b: product(k, 2 * b + 1 - y))

        @pl.when(k >= 1)
        def _():
            finish_chunk(k - 1, q - 1)

        @pl.when(is_line_first)
        def _():
            line_send(q + 1, k, lambda b: product(k, 2 * b + y))
            ysend[p, z] = product(k, 2 * z + 1 - y)
            line_own(q, ysend.at[p, z])
            y_copy(p, z).start()

        @pl.when(k + 2 < total)
        def _():
            pair_send(k + 2)

        @pl.when(k + 3 < total)
        def _():
            b_load(k + 3, lambda copy: copy.start())

    def fetch(*pairs):
        copies = [pltpu.make_async_copy(src, dst, w_sem.at[i]) for i, (src, dst) in enumerate(pairs)]
        for copy in copies:
            copy.start()
        for copy in copies:
            copy.wait()

    def side(hbm, s, c):
        return hbm.at[pl.ds(s * half + c * chunk, chunk)]

    def core_copy(c, again):
        ss, rs = (cs2_sem, cr2_sem) if again else (cs_sem, cr_sem)
        return remote(cs.at[c % 2], crecv.at[c], ss.at[c], rs.at[c], at_tensor(sibling))

    def x_copy(c, again):
        ss, rs = (xs2_sem, xr2_sem) if again else (xs_sem, xr_sem)
        return remote(xs.at[c], xr.at[c], ss.at[c], rs.at[c], at_tensor(across))

    def to_sibling(c, again):
        ss, rs = (as2_sem, ar2_sem) if again else (as_sem, ar_sem)
        return remote(xr.at[c], ag.at[c % 2], ss.at[c], rs.at[c], at_tensor(sibling))

    def send_partial(c, again):
        core_copy(c, again).start()
        core_copy(c, again).wait_recv()
        xs[c] += crecv[c]
        x_copy(c, again).start()
        core_copy(c, again).wait_send()

    def feed_back():
        def scoped(wd, grads, gates, ups, ggr, gur):
            fetch((wd_hbm, wd))
            for c in range(2 * ROW_CHUNKS):
                rows = pl.ds(c * chunk, chunk)
                fetch((gdr_hbm.at[rows], grads), (gate_hbm.at[rows], gates), (up_hbm.at[rows], ups))

                def tile(n, carry):
                    cols = pl.ds(pl.multiple_of(n * TILE, TILE), 512)
                    grad = lax.dot_general(
                        grads[...], wd[cols, :], (((1,), (1,)), ((), ())), preferred_element_type=F32)
                    gate, up = gates[:, cols], ups[:, cols]
                    sig = jax.nn.sigmoid(gate)
                    ggr[:, cols] = (grad * up * sig * (1.0 + gate * (1.0 - sig))).astype(BF16)
                    gur[:, cols] = (grad * gate * sig).astype(BF16)
                    return carry
                lax.fori_loop(0, wd.shape[0] // TILE, tile, 0)
                fetch((ggr, ggr_hbm.at[rows]), (gur, gur_hbm.at[rows]))
        hidden = wd_hbm.shape[0]
        pl.run_scoped(
            scoped, pltpu.VMEM(wd_hbm.shape, BF16), pltpu.VMEM((chunk, width), BF16),
            pltpu.VMEM((chunk, hidden), F32), pltpu.VMEM((chunk, hidden), F32),
            pltpu.VMEM((chunk, hidden), BF16), pltpu.VMEM((chunk, hidden), BF16))

    def hidden_partial():
        def scoped(wg, wu, ggr, gur):
            fetch((wg_hbm, wg), (wu_hbm, wu))
            for c in range(ROW_CHUNKS):
                for s in range(2):
                    fetch((side(ggr_hbm, s, c), ggr), (side(gur_hbm, s, c), gur))

                    def tile(n, carry):
                        rows = pl.ds(pl.multiple_of(n * TILE, TILE), 512)
                        part = lax.dot_general(
                            ggr[...], wg[rows, :], (((1,), (1,)), ((), ())), preferred_element_type=F32)
                        part = part + lax.dot_general(
                            gur[...], wu[rows, :], (((1,), (1,)), ((), ())), preferred_element_type=F32)
                        if s == 0:
                            xs[c, :, rows] = part
                        else:
                            cs[c % 2, :, rows] = part
                        return carry
                    lax.fori_loop(0, width // TILE, tile, 0)
                send_partial(c, False)
        hidden = wg_hbm.shape[1]
        pl.run_scoped(
            scoped, pltpu.VMEM(wg_hbm.shape, BF16), pltpu.VMEM(wu_hbm.shape, BF16),
            pltpu.VMEM((chunk, hidden), BF16), pltpu.VMEM((chunk, hidden), BF16))

    def branch_back(c):
        def scoped(branch, seed, low, turned):
            rows = pl.ds(c * chunk, chunk)
            fetch((branch_hbm.at[rows], branch), (seed_hbm.at[rows], seed))
            x_copy(c, False).wait()
            grad_hidden = xs[c] + xr[c] + seed[...].astype(F32)
            xs[c] = grad_hidden
            values = branch[...]
            inv = mean_inverse(values)
            vec[1:2, :] += column_sum(grad_hidden * values * inv)
            scaled = grad_hidden * attn_gain[...]
            dot = jnp.sum(scaled * values, axis=1, keepdims=True)
            grad = inv * scaled - values * (inv * inv * inv * dot / width)
            xr[c] = grad
            to_sibling(c, False).start()
            low[0:chunk, :] = grad.astype(BF16)
            turned[:, 0:chunk] = grad.astype(BF16).T
            fetch((xs.at[c], gh_hbm.at[rows]))
            to_sibling(c, False).wait_recv()
            low[chunk : 2 * chunk, :] = ag[c % 2].astype(BF16)
            turned[:, chunk : 2 * chunk] = ag[c % 2].astype(BF16).T
            fetch(
                (turned.at[:, pl.ds(0, chunk)], gbt_hbm.at[:, rows]),
                (turned.at[:, pl.ds(chunk, chunk)], gbt_hbm.at[:, pl.ds(half + c * chunk, chunk)]),
                (low.at[pl.ds(0, chunk)], gb_at(0, c)),
                (low.at[pl.ds(chunk, chunk)], gb_at(1, c)))
            to_sibling(c, False).wait_send()

        def gb_at(s, c):
            first = jnp.where(core == s, 0, half) + c * chunk
            return token_out.at[pl.ds(pl.multiple_of(first, chunk), chunk)]
        pl.run_scoped(
            scoped, pltpu.VMEM((chunk, width), F32), pltpu.VMEM((chunk, width), BF16),
            pltpu.VMEM((2 * chunk, width), BF16), pltpu.VMEM((width, 2 * chunk), BF16))

    def attention_back():
        heads = head_cols // HEAD
        q_rows = min(256, full)
        scale = HEAD ** (-0.5)

        def scoped(query, key, value, mixed_grad, dq, dk, dv, raw):
            def products(w_out, rows_buf):
                fetch((w_out_hbm, w_out), (query_hbm, query), (key_hbm, key), (value_hbm, value))
                for c in range(full // q_rows):
                    rows = pl.ds(c * q_rows, q_rows)
                    fetch((token_out.at[rows], rows_buf))
                    mixed_grad[rows, :] = lax.dot_general(
                        rows_buf[...], w_out[...], (((1,), (1,)), ((), ())),
                        preferred_element_type=F32).astype(BF16)
            pl.run_scoped(
                products, pltpu.VMEM(w_out_hbm.shape, BF16), pltpu.VMEM((q_rows, width), BF16))

            def head(h, carry):
                cols = pl.ds(pl.multiple_of(h * HEAD, HEAD), HEAD)
                dk[:, cols] = jnp.zeros((full, HEAD), F32)
                dv[...] = jnp.zeros((full, HEAD), F32)
                for i in range(full // q_rows):
                    rows, keys = slice(i * q_rows, (i + 1) * q_rows), (i + 1) * q_rows
                    q_block, grad_block = query[rows, cols], mixed_grad[rows, cols]
                    key_block, value_block = key[0:keys, cols], value[0:keys, cols]
                    nt = (((1,), (1,)), ((), ()))
                    scores = lax.dot_general(key_block, q_block, nt, preferred_element_type=F32) * scale
                    key_at = lax.broadcasted_iota(jnp.int32, (keys, q_rows), 0)
                    query_at = lax.broadcasted_iota(jnp.int32, (keys, q_rows), 1) + i * q_rows
                    allowed = (
                        (seg_col[0:keys, :] == seg_row[:, rows])
                        & (key_at <= query_at)
                        & ((live_col[0:keys, :] > 0) | (key_at == query_at)))
                    scores = jnp.where(allowed, scores, NEG_FILL)
                    prob = jnp.exp(scores - log_totals[pl.ds(h, 1), rows])
                    grad_prob = lax.dot_general(value_block, grad_block, nt, preferred_element_type=F32)
                    row_dot = jnp.sum(prob * grad_prob, axis=0, keepdims=True)
                    grad_scores = (prob * (grad_prob - row_dot)).astype(BF16)
                    dq[rows, cols] = lax.dot_general(
                        grad_scores, key_block, (((0,), (0,)), ((), ())), preferred_element_type=F32) * scale
                    dk[0:keys, cols] += jnp.dot(grad_scores, q_block, preferred_element_type=F32) * scale
                    dv[0:keys, :] += jnp.dot(prob.astype(BF16), grad_block, preferred_element_type=F32)
                mixed_grad[:, cols] = dv[...].astype(BF16)
                return carry
            lax.fori_loop(0, heads, head, 0)
            fetch((mixed_grad, gqkv_hbm.at[:, pl.ds(2 * head_cols, head_cols)]))

            lanes = lax.broadcasted_iota(jnp.int32, (q_rows, HEAD), 1)
            vec[2:3, :] = jnp.zeros((1, width), F32)
            for which, (grads, raw_hbm, inv, gain) in enumerate((
                (dq, query_raw_hbm, query_inv, query_gain), (dk, key_raw_hbm, key_inv, key_gain))):
                fetch((raw_hbm, raw))

                def back(i, carry):
                    rows = pl.ds(pl.multiple_of(i * q_rows, q_rows), q_rows)
                    dot = jnp.zeros((q_rows, 1), F32)
                    for h in range(heads):
                        cols = slice(h * HEAD, (h + 1) * HEAD)
                        grad = grads[rows, cols]
                        grad = grad * cosine[rows, :] + pltpu.roll(grad, HEAD // 2, 1) * sine[rows, :]
                        raw_rows = raw[rows, cols]
                        gain_cols = slice(which * head_cols + h * HEAD, which * head_cols + (h + 1) * HEAD)
                        vec[2:3, gain_cols] += column_sum(grad * raw_rows * inv[rows, :])
                        scaled = grad * gain[:, cols]
                        grads[rows, cols] = scaled
                        dot = dot + jnp.sum(scaled * raw_rows, axis=1, keepdims=True)
                    if which == 0:
                        dots[rows, :] = jnp.broadcast_to(dot, (q_rows, HEAD))
                    else:
                        dots[rows, :] = jnp.where(lanes == 0, dots[rows, :], dot)
                    return carry
                lax.fori_loop(0, full // q_rows, back, 0)
            for i, peer in enumerate((sibling, across)):
                copy = remote(dots, dots_in.at[i], ds_sem.at[i], dr_sem.at[i], at_tensor(peer))
                copy.start()
                copy.wait()
                dots[...] += dots_in[i]
            for which, (grads, raw_hbm, inv) in enumerate((
                (dq, query_raw_hbm, query_inv), (dk, key_raw_hbm, key_inv))):
                fetch((raw_hbm, raw))
                for i in range(full // q_rows):
                    rows = slice(i * q_rows, (i + 1) * q_rows)
                    inv_rows = inv[rows, :]
                    dot = dots[rows, which : which + 1]
                    mixed_grad[rows, :] = (
                        inv_rows * grads[rows, :]
                        - raw[rows, :] * (inv_rows * inv_rows * inv_rows * dot / width)
                    ).astype(BF16)
                fetch((mixed_grad, gqkv_hbm.at[:, pl.ds(which * head_cols, head_cols)]))
        rows_of = (full, head_cols)
        pl.run_scoped(
            scoped, pltpu.VMEM(rows_of, BF16), pltpu.VMEM(rows_of, BF16), pltpu.VMEM(rows_of, BF16),
            pltpu.VMEM(rows_of, BF16), pltpu.VMEM(rows_of, F32), pltpu.VMEM(rows_of, F32),
            pltpu.VMEM((full, HEAD), F32), pltpu.VMEM(rows_of, F32))

    def gains_sum():
        copy = remote(vec, vec_in.at[0], vs_sem.at[0], vr_sem.at[0], at_tensor(sibling))
        copy.start()
        copy.wait()
        vec[0:2, :] += vec_in[0, 0:2, :]
        for i, peer in enumerate(vec_peers):
            copy = remote(vec, vec_in.at[i + 1], vs_sem.at[i + 1], vr_sem.at[i + 1], at_dp(peer))
            copy.start()
            copy.wait()
            vec[...] += vec_in[i + 1]

    def turn_tokens():
        def scoped(rows_buf):
            for i in range(full // 256):
                rows = pl.ds(i * 256, 256)
                fetch((tok_hbm.at[rows], rows_buf))
                at[0, :, rows] = rows_buf[...].T
        pl.run_scoped(scoped, pltpu.VMEM((256, width), BF16))

    def input_partial():
        def scoped(weights, grads):
            fetch(*[(w, weights.at[i]) for i, w in enumerate((wq_hbm, wk_hbm, wv_hbm))], (gqkv_hbm, grads))
            for c in range(ROW_CHUNKS):
                for s in range(2):
                    first = jnp.where(core == s, 0, half) + c * chunk
                    rows = pl.ds(pl.multiple_of(first, chunk), chunk)

                    def tile(n, carry):
                        cols = pl.ds(pl.multiple_of(n * TILE, TILE), 512)
                        part = jnp.zeros((chunk, TILE), F32)
                        for i in range(3):
                            part = part + lax.dot_general(
                                grads[rows, i * head_cols : (i + 1) * head_cols], weights[i, cols, :],
                                (((1,), (1,)), ((), ())), preferred_element_type=F32)
                        if s == 0:
                            xs[c, :, cols] = part
                        else:
                            cs[c % 2, :, cols] = part
                        return carry
                    lax.fori_loop(0, width // TILE, tile, 0)
                send_partial(c, True)
        pl.run_scoped(
            scoped, pltpu.VMEM((3,) + wq_hbm.shape, BF16), pltpu.VMEM((full, 3 * head_cols), BF16))

    def token_grads(c):
        def scoped(grad_hidden, low):
            fetch((gh_hbm.at[pl.ds(c * chunk, chunk)], grad_hidden))
            x_copy(c, True).wait()
            total_rows = xs[c] + xr[c] + grad_hidden[...]
            xr[c] = total_rows
            to_sibling(c, True).start()
            low[0] = total_rows.astype(BF16)
            to_sibling(c, True).wait_recv()
            low[1] = ag[c % 2].astype(BF16)
            copies = []
            for s in range(2):
                first = jnp.where(core == s, 0, half) + c * chunk
                copies.append((low.at[s], token_out.at[pl.ds(pl.multiple_of(first, chunk), chunk)]))
            fetch(*copies)
            to_sibling(c, True).wait_send()
        pl.run_scoped(scoped, pltpu.VMEM((chunk, width), F32), pltpu.VMEM((2, chunk, width), BF16))

    vec[...] = jnp.zeros(vec.shape, F32)
    vec[0:1, :] = gain_mlp_part[...]
    at_load(0).start()
    at_load(1).start()
    for k in range(3):
        b_load(jnp.int32(k), lambda copy: copy.start())
    at_load(0).wait()
    pair_send(jnp.int32(0))
    pair_send(jnp.int32(1))
    feed_back()
    at_load(1).wait()

    work = {0: hidden_partial, 8: attention_back, 9: turn_tokens, 10: input_partial, 11: gains_sum}
    for c in range(ROW_CHUNKS):
        work[3 + c] = functools.partial(branch_back, c)
        work[13 + c] = functools.partial(token_grads, c)

    def body(k, carry):
        tick(k)
        for when, fn in work.items():
            @pl.when(k == when)
            def _(fn=fn):
                fn()

        @pl.when(k == first_heads + 1)
        def _():
            at_load(3).start()

        @pl.when(k == first_heads + 2)
        def _():
            at_load(3).wait()
        return carry
    lax.fori_loop(0, total, body, 0)
    finish_chunk(jnp.int32(total - 1), jnp.int32(passes - 1))
    out_act(jnp.int32(total - 1), lambda copy: copy.wait())
    gains_out[...] = vec[...]


def backward_layer(dp_size, hbm, vmem_args):
    names = dict(zip(HBM_NAMES, hbm, strict=True))
    width, row_count = names["gdrt"].shape
    hidden, head_cols = names["inner"].shape[1], names["query"].shape[1]
    line, block = dp_size // 2, width // dp_size
    chunk = row_count // 2 // ROW_CHUNKS
    counts = (hidden // COLS, 2 * hidden // COLS, 3 * head_cols // COLS, head_cols // COLS)
    DMA, REG = pltpu.SemaphoreType.DMA, pltpu.SemaphoreType.REGULAR
    vmem, any_space = pl.BlockSpec(memory_space=pltpu.VMEM), pl.BlockSpec(memory_space=pl.ANY)

    def shape(*dims, kind=F32):
        return jax.ShapeDtypeStruct(dims, kind)

    slot = (block, COLS)
    per_chunk = DMA((ROW_CHUNKS,))
    steps = dp_size.bit_length() - 1
    results = pl.pallas_call(
        functools.partial(backward_kernel, dp_size, counts),
        out_shape=(
            shape((counts[0] + counts[3]) * COLS, block),
            shape(block, (counts[1] + counts[2]) * COLS),
            shape(row_count, width, kind=BF16),
            shape(8, width),
            shape(row_count, hidden, kind=BF16),
            shape(row_count, hidden, kind=BF16),
            shape(width, row_count, kind=BF16),
            shape(row_count // 2, width),
            shape(row_count, 3 * head_cols, kind=BF16),
        ),
        in_specs=[any_space] * len(hbm) + [vmem] * len(vmem_args),
        out_specs=(any_space,) * 3 + (vmem,) + (any_space,) * 5,
        scratch_shapes=[
            pltpu.VMEM((2, width, row_count), BF16),
            pltpu.VMEM((B_SLOTS, row_count, COLS), BF16),
            pltpu.VMEM((Y_SLOTS, line) + slot, F32),
            pltpu.VMEM((Y_SLOTS, line) + slot, F32),
            pltpu.VMEM((2, line) + slot, F32),
            pltpu.VMEM((2, line + 1) + slot, F32),
            pltpu.VMEM(slot, F32),
            pltpu.VMEM((COLS, block), F32),
            pltpu.VMEM((2, chunk, width), F32),
            pltpu.VMEM((ROW_CHUNKS, chunk, width), F32),
            pltpu.VMEM((ROW_CHUNKS, chunk, width), F32),
            pltpu.VMEM((ROW_CHUNKS, chunk, width), F32),
            pltpu.VMEM((2, chunk, width), F32),
            pltpu.VMEM((row_count, HEAD), F32),
            pltpu.VMEM((2, row_count, HEAD), F32),
            pltpu.VMEM((8, width), F32),
            pltpu.VMEM((steps + 1, 8, width), F32),
            DMA((2,)),
            DMA((B_SLOTS,)),
            DMA((Y_SLOTS, line)),
            DMA((Y_SLOTS, line)),
            DMA((2, line)),
            DMA((2, line + 1)),
            DMA,
        ]
        + [per_chunk] * 12
        + [DMA((2,)), DMA((2,)), DMA((steps + 1,)), DMA((steps + 1,)), DMA((4,)), REG, REG, REG],
        compiler_params=pltpu.CompilerParams(
            collective_id=2, has_side_effects=True, vmem_limit_bytes=VMEM_LIMIT),
    )(*hbm, *vmem_args)
    return results[:4]


def times(left, right):
    return jnp.dot(left, right, preferred_element_type=F32)


def rope_tables():
    half_size = HEAD // 2
    freq_row = ROPE_BASE ** (-(jnp.arange(half_size, dtype=F32) * 2.0) / HEAD)
    angle = jnp.arange(LENGTH, dtype=F32)[:, None] * freq_row[None, :]
    return (jnp.cos(angle), jnp.sin(angle))


def rotate(values, cosine, sine_part, direction):
    row_count, col_count = values.shape
    half_size = HEAD // 2
    split = values.reshape(row_count // LENGTH, LENGTH, col_count // HEAD, 2, half_size)
    first = split[:, :, :, 0]
    second = split[:, :, :, 1]
    cos_b = cosine[None, :, None, :]
    sin_b = direction * sine_part[None, :, None, :]
    turned = jnp.stack((first * cos_b - second * sin_b, second * cos_b + first * sin_b), axis=3)
    return turned.reshape(row_count, col_count)


def visible_keys(begin_at, block_rows, segment_ids, live_rows):
    seq_length = segment_ids.shape[0]
    key_index = jnp.arange(seq_length)
    query_index = begin_at + jnp.arange(block_rows)
    query_segs = segment_ids[begin_at : begin_at + block_rows]
    same_doc = query_segs[:, None] == segment_ids[None, :]
    causal = key_index[None, :] <= query_index[:, None]
    kept_key = (live_rows[None, :] > 0) | (key_index[None, :] == query_index[:, None])
    return same_doc & causal & kept_key


def block_scores(query_seq, key_heads, begin_at, block_rows, segment_ids, live_rows):
    local_heads = key_heads.shape[1]
    query_heads = query_seq[begin_at : begin_at + block_rows].reshape(block_rows, local_heads, HEAD)
    scores = jnp.einsum(
        "ihd,jhd->hij", query_heads, key_heads, preferred_element_type=F32
    ) * HEAD ** (-0.5)
    allowed = visible_keys(begin_at, block_rows, segment_ids, live_rows)
    return (query_heads, jnp.where(allowed[None], scores, NEG_FILL))


def attend_forward(query_seq, key_seq, value_seq, segment_ids, live_rows):
    seq_length = query_seq.shape[0]
    local_heads = query_seq.shape[1] // HEAD
    block_rows = min(512, seq_length)
    key_heads = key_seq.reshape(seq_length, local_heads, HEAD)
    value_heads = value_seq.reshape(seq_length, local_heads, HEAD)
    mixed_parts = []
    lse_parts = []
    for begin_at in range(0, seq_length, block_rows):
        query_heads, scores = block_scores(
            query_seq, key_heads, begin_at, block_rows, segment_ids, live_rows
        )
        row_max = jnp.max(scores, axis=-1, keepdims=True)
        exp_scores = jnp.exp(scores - row_max)
        row_total = jnp.sum(exp_scores, axis=-1, keepdims=True)
        attn_prob = (exp_scores / row_total).astype(BF16)
        mixed_block = jnp.einsum(
            "hij,jhd->ihd", attn_prob, value_heads, preferred_element_type=F32
        )
        mixed_parts.append(mixed_block.reshape(block_rows, -1).astype(BF16))
        lse_parts.append((row_max + jnp.log(row_total))[..., 0])
    return (jnp.concatenate(mixed_parts, 0), jnp.concatenate(lse_parts, 1))


def make_shards(dp_size, tensor_size):
    core_pairs = [(i, i ^ 1) for i in range(tensor_size)]
    tensor_bits = [1 << b for b in range(1, tensor_size.bit_length() - 1)]

    def to_core(values):
        return lax.ppermute(values, "tensor", core_pairs)

    def wide_sum(values):
        for bit in tensor_bits:
            values = values + lax.ppermute(
                values, "tensor", [(i, i ^ bit) for i in range(tensor_size)]
            )
        return values

    def shards(
        tokens,
        segments,
        pad_mask,
        w_query,
        w_key,
        w_value,
        w_out,
        gain_query,
        gain_key,
        gain_attn,
        w_gate,
        w_up,
        w_down,
        gain_mlp,
        cotangent,
    ):
        row_count, model_width = tokens.shape
        half_rows = row_count // 2
        block = model_width // dp_size
        core_at = lax.axis_index("tensor") % 2
        cosine, sine_part = rope_tables()

        def split_rows(values):
            own = lax.dynamic_slice_in_dim(values, core_at * half_rows, half_rows, 0)
            other = lax.dynamic_slice_in_dim(values, (1 - core_at) * half_rows, half_rows, 0)
            return own, other

        query_raw = times(tokens, w_query)
        key_raw = times(tokens, w_key)
        value_rows = times(tokens, w_value).astype(BF16)
        squares = jnp.stack(
            (jnp.sum(query_raw * query_raw, axis=1), jnp.sum(key_raw * key_raw, axis=1))
        )
        squares = wide_sum(squares + to_core(squares))
        query_inv = lax.rsqrt(squares[0] / model_width + EPSILON)[:, None]
        key_inv = lax.rsqrt(squares[1] / model_width + EPSILON)[:, None]
        query_gain = gain_query.reshape(-1).astype(F32)
        key_gain = gain_key.reshape(-1).astype(F32)
        query_norm = rotate(query_raw * query_inv * query_gain, cosine, sine_part, 1.0).astype(BF16)
        key_norm = rotate(key_raw * key_inv * key_gain, cosine, sine_part, 1.0).astype(BF16)
        mixed, log_totals = attend_forward(query_norm, key_norm, value_rows, segments, pad_mask)
        mixed_own, mixed_other = split_rows(mixed)
        mixed_rows = jnp.concatenate((mixed_own, mixed_other), 0)
        tokens_own, tokens_other = split_rows(tokens)
        cot_own, _ = split_rows(cotangent)
        live_own, _ = split_rows(pad_mask[:, None])
        attn_gain = gain_attn.astype(F32)
        mlp_gain = gain_mlp.astype(F32)
        seed = jnp.where(live_own > 0, cot_own, jnp.zeros_like(cot_own))

        (
            gate_rows,
            up_rows,
            inner_rows,
            hidden_turned,
            grad_down_rows,
            grad_down_turned,
            branch_rows,
            output,
            gain_mlp_part,
        ) = forward_layer(
            mixed_rows,
            w_out,
            attn_gain[None, :],
            mlp_gain[None, :],
            tokens_own,
            seed,
            w_gate,
            w_up,
            w_down,
        )
        turned, straight, grad_tokens, gains = backward_layer(
            dp_size,
            (
                grad_down_turned, hidden_turned, tokens, inner_rows, mixed_rows, grad_down_rows,
                gate_rows, up_rows, branch_rows, seed,
                query_norm, key_norm, value_rows, query_raw, key_raw,
                w_out, w_gate, w_up, w_down, w_query, w_key, w_value,
            ),
            (
                query_inv, key_inv, log_totals, segments[:, None], segments[None, :],
                pad_mask[:, None], jnp.concatenate((cosine, cosine), 1),
                jnp.concatenate((sine_part, -sine_part), 1),
                query_gain[None, :], key_gain[None, :], attn_gain[None, :], gain_mlp_part,
            ),
        )
        hidden, head_cols = w_gate.shape[1], w_query.shape[1]
        grad_gate, grad_up = straight[:, :hidden], straight[:, hidden : 2 * hidden]
        grad_query, grad_key, grad_value = (
            straight[:, 2 * hidden + i * head_cols : 2 * hidden + (i + 1) * head_cols]
            for i in range(3)
        )
        dp_at = lax.axis_index("dp")
        wide = lax.dynamic_slice_in_dim(gains[:2], dp_at * block, block, 1)
        head_gains = gains[2, : 2 * head_cols].reshape(2 * gain_query.shape[0], HEAD)
        head_gains = lax.dynamic_slice_in_dim(head_gains, dp_at * (HEAD // dp_size), HEAD // dp_size, 1)
        return (
            output,
            grad_tokens,
            grad_query,
            grad_key,
            grad_value,
            turned[hidden:],
            head_gains[: gain_query.shape[0]],
            head_gains[gain_query.shape[0] :],
            wide[1],
            grad_gate,
            grad_up,
            turned[:hidden],
            wide[0],
        )

    return shards


def solution(mesh):
    in_specs = (
        P("dp", None),
        P("dp"),
        P("dp"),
        P(None, "tensor"),
        P(None, "tensor"),
        P(None, "tensor"),
        P("tensor", None),
        P("tensor", None),
        P("tensor", None),
        P(),
        P(None, "tensor"),
        P(None, "tensor"),
        P("tensor", None),
        P(),
        P("dp", None),
    )
    out_specs = (
        P("dp", None),
        P("dp", None),
        P("dp", "tensor"),
        P("dp", "tensor"),
        P("dp", "tensor"),
        P("tensor", "dp"),
        P("tensor", "dp"),
        P("tensor", "dp"),
        P("dp"),
        P("dp", "tensor"),
        P("dp", "tensor"),
        P("tensor", "dp"),
        P("dp"),
    )
    shards = make_shards(mesh.shape["dp"], mesh.shape["tensor"])
    return jax.shard_map(shards, mesh=mesh, in_specs=in_specs, out_specs=out_specs, check_vma=False)
```

time: 1560 us -> 1180 us (0.76)
  Pallas kernels: 730 us -> 1080 us
  waiting for transfers between devices: 322 us -> 0.01 us
  matrix products: 210 us -> 27.3 us
  other arithmetic: 120 us -> 25.9 us
  local copies, waits for them, and re-layouts: 98 us -> 36.8 us
  blocking collectives: 37.6 us -> 0 us
  starting transfers between devices: 29.3 us -> 3.1 us
    pallas_call x1 -> x2, Pallas kernels: 730 us -> 1080 us  [the longest x1 883 us: backward_layer(): pl.pallas_call(functools.partial(backward_kernel, dp_size, counts), out_s...]
    ppermute x18 -> x1, waiting for transfers between devices: 319 us -> 0.01 us  [wide_sum(): lax.ppermute(values, 'tensor', [(i, i ^ bit) for i in range(tensor_size)])]
    dot_general x34 -> x0, matrix products: 105 us -> none  [the longest x26 83.5 us: back_product(): lax.dot_general(left, right, (((1,), (1,)), ((), ())), preferred_element_...]
    dot_general x35 -> x3, matrix products: 93.6 us -> 15.4 us  [times(): return jnp.dot(left, right, preferred_element_type=F32)]
    unnamed x266 -> x36, local copies, waits for them, and re-layouts: 58.4 us -> 5.79 us
    unnamed x1 -> x0, blocking collectives: 37.6 us -> none
    unnamed x29 -> x0, other arithmetic: 21.2 us -> none
    ppermute x18 -> x1, starting transfers between devices: 20.2 us -> 2.58 us  [wide_sum(): lax.ppermute(values, 'tensor', [(i, i ^ bit) for i in range(tensor_size)])]
  transfers between devices with their start and end apart: 51 -> 2, of which waited for: 18 -> 0; matrix products, arithmetic and copies ran while one was open for 22% -> 3% of each run, Pallas kernels for 47% -> 0%
where the time goes in v2:
time: 1180 us; the launch traced here: 1170 us
  Pallas kernels  1080 us (92%)
  local copies, waits for them, and re-layouts  36.8 us (3%)
  matrix products  27.3 us (2%)
  other arithmetic  25.9 us (2%)
    pallas_call x1, Pallas kernels, backward_layer(): pl.pallas_call(functools.partial(backward_kernel, dp_size, counts), out_s...  883 us
    pallas_call x1, Pallas kernels, forward_layer(): pl.pallas_call(forward_kernel, out_shape=(shape(row_count, hidden), shape...  196 us
  transfers between devices with their start and end apart: 2, of which 0 were waited for; matrix products, arithmetic and copies ran while one was open for 3% of the time, Pallas kernels for 0%

profile of v2, /device:TPU:0, one launch (start us, length us, event | category | flops | bytes accessed | tf_op | source)
XLA Modules:
  0.0 1172.7 jit_solution(2971351608080536495)
XLA Ops:
  0.7 6.7 multiply_reduce_fusion.1
  7.4 2.4 multiply_reduce_fusion
  10.4 6.2 convolution_convert_fusion.value_hbm
  17.3 3.1 fusion.20
  20.5 4.9 dynamic-slice_select_fusion
  25.4 1.7 fusion.10
  27.8 2.6 collective-permute-start.1
  30.4 1.3 pad_maximum_fusion.2
  31.7 1.2 copy.64
  33.0 1.9 copy.63
  34.9 2.3 copy.88
  38.4 2.9 copy.75.query_raw_hbm
  41.3 1.8 copy.76.key_raw_hbm
  45.2 1.9 multiply_multiply_fusion.1
  47.5 1.1 pad_maximum_fusion
  49.3 1.9 fusion
  51.2 1.9 fusion.1
  53.1 4.7 fusion.2
  57.9 4.6 fusion.12
  62.4 3.5 fusion.13
  66.2 1.3 copy.87
  67.5 1.3 copy.73.query_hbm
  68.8 1.3 copy.74.key_hbm
  72.2 1.7 fusion.15
  75.6 195.8 %shard_map.246 = (f32[1024,2048]{1,0:T(8,128)}, f32[1024,2048]{1,0:T(8,128)}, bf16[1024,2048]{1,0:T(8,128)(2,1)}, bf16[2048,1024]{1,0:T(8,128)(2,1)}, bf16[1024,...) custom-call(bf16[1024,512]{1,0:T(8,128)(2,1)} %pad_maximum_fusion.1., ...), custom_call_target="tpu_custom_call" | custom-call | tf_op jit(solution)/shard_map/pallas_call | solution.py:293
  271.4 882.8 %shard_map.247 = (f32[2560,256]{1,0:T(8,128)}, f32[256,5632]{1,0:T(8,128)}, bf16[1024,2048]{1,0:T(8,128)(2,1)}, f32[8,2048]{1,0:T(8,128)}, bf16[1024,2048]{1,0:T...) custom-call(bf16[2048,1024]{1,0:T(8,128)(2,1)} %get-tuple-element.27, ...), custom_call_target="tpu_custom_call" | custom-call | tf_op jit(solution)/shard_map/pallas_call | solution.py:945
  1155.8 2.5 fusion.31
  1158.3 4.9 fusion.30
  1164.0 1.5 slice.92
  1166.8 2.1 copy.91
  1168.9 1.6 copy-done.4
  1170.5 2.0 copy.92
  (69 shorter events, 14.0 us)
Async XLA Ops:
  0.6 6.7 copy-start
  0.7 6.7 copy-start.8
  9.8 17.9 %collective-permute-start = (f32[2,1024]{1,0:T(2,128)S(1)}, f32[2,1024]{1,0:T(2,128)S(1)}, u32[]{:S(2)}, u32[]{:S(2)}) collective-permute-start(f32[2,1024]{1,0:T(2,128)S(1)} %pad_maximum_fusion.5), channel_id=1, source_target_pairs={{0,1},{1,0},{2,3},{3,2},{4,5},{5,4},{6,7},{7,6},{8,9},{9,8},{10,11... | collective-permute-start | bytes 24584 | tf_op jit(solution)/shard_map/ppermute | solution.py:1067
  10.4 6.3 copy-start.11
  10.4 6.3 copy-start.12
  10.4 6.3 copy-start.15
  20.5 6.7 copy-start.16
  20.5 9.9 copy-start.1
  20.5 9.9 copy-start.2
  20.5 9.9 copy-start.9
  25.4 11.7 %copy-start.13 = (bf16[2048]{0:T(1024)(128)(2,1)S(1)}, bf16[2048]{0:T(1024)(128)(2,1)}, u32[]{:S(2)}) copy-start(bf16[2048]{0:T(1024)(128)(2,1)} %param.24) | copy-start | bytes 12292
  25.4 12.3 %copy-start.14 = (bf16[2048]{0:T(1024)(128)(2,1)S(1)}, bf16[2048]{0:T(1024)(128)(2,1)}, u32[]{:S(2)}) copy-start(bf16[2048]{0:T(1024)(128)(2,1)} %param.28) | copy-start | bytes 12292
  27.8 17.3 %collective-permute-start.1 = (f32[2,1024]{1,0:T(2,128)S(1)}, f32[2,1024]{1,0:T(2,128)S(1)}, u32[]{:S(2)}, u32[]{:S(2)}) collective-permute-start(f32[2,1024]{1,0:T(2,128)S(1)} %fusion.29), channel_id=1, source_target_pairs={{0,2},{1,3},{2,0},{3,1},{4,6},{5,7},{6,4},{7,5},{8,10},{9,11},{10,... | collective-permute-start | bytes 24584 | tf_op jit(solution)/shard_map/ppermute | solution.py:1071
  45.1 1.9 copy-start.7
  53.1 4.7 copy-start.10
  62.4 5.0 copy-start.5
  1158.3 4.9 copy-start.6
  1163.2 3.6 copy-start.3
  1166.8 3.7 copy-start.4

commit v3 on v2

--- a/solution.py
+++ b/solution.py
@@ -21,6 +21,11 @@
 SPAN = 6
 Y_SLOTS = 3
 B_SLOTS = 5
+FEED_TICK = 3
+HIDDEN_TICK = 7
+BRANCH_TICK = 12
+INPUT_TICK = 21
+TOKEN_TICK = 26
 HBM_NAMES = (
     "gdrt", "hlt", "tokens", "inner", "mixed", "gdr", "gate", "up", "branch", "seed",
     "query", "key", "value", "query_raw", "key_raw",
@@ -347,7 +352,7 @@
     vec, vec_in,
     at_sem, b_sem, ys_sem, yr_sem, zs_sem, zr_sem, out_sem,
     cs_sem, cr_sem, xs_sem, xr_sem, as_sem, ar_sem, cs2_sem, cr2_sem, xs2_sem, xr2_sem, as2_sem,
-    ar2_sem, ds_sem, dr_sem, vs_sem, vr_sem, w_sem,
+    ar2_sem, ds_sem, dr_sem, vs_sem, vr_sem, w_sem, pre_sem, st_sem, gh_sem, tok_sem,
     y_credit, up_credit, down_credit,
 ):
     n_down, n_hidden, n_heads, n_out = counts
@@ -618,15 +623,49 @@
         def _():
             b_load(k + 3, lambda copy: copy.start())
 
-    def fetch(*pairs):
-        copies = [pltpu.make_async_copy(src, dst, w_sem.at[i]) for i, (src, dst) in enumerate(pairs)]
+    nt = (((1,), (1,)), ((), ()))
+
+    def copies_of(sem, *pairs):
+        return [pltpu.make_async_copy(src, dst, sem.at[i]) for i, (src, dst) in enumerate(pairs)]
+
+    def start(copies):
         for copy in copies:
             copy.start()
+
+    def finish(copies):
         for copy in copies:
             copy.wait()
 
-    def side(hbm, s, c):
-        return hbm.at[pl.ds(s * half + c * chunk, chunk)]
+    def run_ticks(first, last, work):
+        def body(k, carry):
+            tick(k)
+            for when, fn in work.items():
+                low, high = when if isinstance(when, tuple) else (when, when + 1)
+
+                @pl.when((k >= low) & (k < high))
+                def _(fn=fn, low=low):
+                    if isinstance(fn, list):
+                        for one in fn:
+                            one()
+                    elif low + 1 == high:
+                        fn()
+                    else:
+                        fn(k - low)
+            return carry
+        lax.fori_loop(first, last, body, 0)
+
+    def part(fn, *args):
+        return functools.partial(fn, *args)
+
+    def side_rows(s, c):
+        return pl.ds(s * half + c * chunk, chunk)
+
+    def both_sides(hbm, buf, c, out=False):
+        pairs = [(hbm.at[side_rows(s, c)], buf.at[pl.ds(s * chunk, chunk)]) for s in range(2)]
+        return [(b, a) for a, b in pairs] if out else pairs
+
+    def sequence_rows(s, c):
+        return pl.ds(pl.multiple_of(jnp.where(core == s, 0, half) + c * chunk, chunk), chunk)
 
     def core_copy(c, again):
         ss, rs = (cs2_sem, cr2_sem) if again else (cs_sem, cr_sem)
@@ -640,69 +679,117 @@
         ss, rs = (as2_sem, ar2_sem) if again else (as_sem, ar_sem)
         return remote(xr.at[c], ag.at[c % 2], ss.at[c], rs.at[c], at_tensor(sibling))
 
-    def send_partial(c, again):
-        core_copy(c, again).start()
+    def pass_on(c, again):
         core_copy(c, again).wait_recv()
         xs[c] += crecv[c]
         x_copy(c, again).start()
         core_copy(c, again).wait_send()
 
-    def feed_back():
-        def scoped(wd, grads, gates, ups, ggr, gur):
-            fetch((wd_hbm, wd))
-            for c in range(2 * ROW_CHUNKS):
-                rows = pl.ds(c * chunk, chunk)
-                fetch((gdr_hbm.at[rows], grads), (gate_hbm.at[rows], gates), (up_hbm.at[rows], ups))
-
-                def tile(n, carry):
-                    cols = pl.ds(pl.multiple_of(n * TILE, TILE), 512)
-                    grad = lax.dot_general(
-                        grads[...], wd[cols, :], (((1,), (1,)), ((), ())), preferred_element_type=F32)
-                    gate, up = gates[:, cols], ups[:, cols]
-                    sig = jax.nn.sigmoid(gate)
-                    ggr[:, cols] = (grad * up * sig * (1.0 + gate * (1.0 - sig))).astype(BF16)
-                    gur[:, cols] = (grad * gate * sig).astype(BF16)
-                    return carry
-                lax.fori_loop(0, wd.shape[0] // TILE, tile, 0)
-                fetch((ggr, ggr_hbm.at[rows]), (gur, gur_hbm.at[rows]))
-        hidden = wd_hbm.shape[0]
-        pl.run_scoped(
-            scoped, pltpu.VMEM(wd_hbm.shape, BF16), pltpu.VMEM((chunk, width), BF16),
-            pltpu.VMEM((chunk, hidden), F32), pltpu.VMEM((chunk, hidden), F32),
-            pltpu.VMEM((chunk, hidden), BF16), pltpu.VMEM((chunk, hidden), BF16))
-
-    def hidden_partial():
-        def scoped(wg, wu, ggr, gur):
-            fetch((wg_hbm, wg), (wu_hbm, wu))
-            for c in range(ROW_CHUNKS):
-                for s in range(2):
-                    fetch((side(ggr_hbm, s, c), ggr), (side(gur_hbm, s, c), gur))
-
-                    def tile(n, carry):
-                        rows = pl.ds(pl.multiple_of(n * TILE, TILE), 512)
-                        part = lax.dot_general(
-                            ggr[...], wg[rows, :], (((1,), (1,)), ((), ())), preferred_element_type=F32)
-                        part = part + lax.dot_general(
-                            gur[...], wu[rows, :], (((1,), (1,)), ((), ())), preferred_element_type=F32)
-                        if s == 0:
-                            xs[c, :, rows] = part
-                        else:
-                            cs[c % 2, :, rows] = part
-                        return carry
-                    lax.fori_loop(0, width // TILE, tile, 0)
-                send_partial(c, False)
-        hidden = wg_hbm.shape[1]
-        pl.run_scoped(
-            scoped, pltpu.VMEM(wg_hbm.shape, BF16), pltpu.VMEM(wu_hbm.shape, BF16),
-            pltpu.VMEM((chunk, hidden), BF16), pltpu.VMEM((chunk, hidden), BF16))
-
-    def branch_back(c):
-        def scoped(branch, seed, low, turned):
+    hidden = wd_hbm.shape[0]
+
+    def feed_phase(wd, grads, gates, ups, ggr, gur):
+        def loads(c):
+            return copies_of(
+                pre_sem, *both_sides(gdr_hbm, grads, c), *both_sides(gate_hbm, gates, c),
+                *both_sides(up_hbm, ups, c))
+
+        def stores(c):
+            return copies_of(
+                st_sem, *both_sides(ggr_hbm, ggr, c, True), *both_sides(gur_hbm, gur, c, True))
+
+        def piece(c):
+            finish(loads(c))
+            if c >= 1:
+                finish(stores(c - 1))
+
+            def tile(n, carry):
+                cols = pl.ds(pl.multiple_of(n * TILE, TILE), TILE)
+                grad = lax.dot_general(grads[...], wd[cols, :], nt, preferred_element_type=F32)
+                gate = gates[:, cols]
+                sig = jax.nn.sigmoid(gate)
+                act = gate * sig
+                ggr[:, cols] = (grad * ups[:, cols] * (sig + act * (1.0 - sig))).astype(BF16)
+                gur[:, cols] = (grad * act).astype(BF16)
+                return carry
+            lax.fori_loop(0, hidden // TILE, tile, 0)
+            start(stores(c))
+            if c + 1 < ROW_CHUNKS:
+                start(loads(c + 1))
+
+        load_weight = copies_of(w_sem, (wd_hbm, wd))
+        start(load_weight)
+        start(loads(0))
+        at_load(0).wait()
+        pair_send(jnp.int32(0))
+        pair_send(jnp.int32(1))
+        finish(load_weight)
+        piece(0)
+        run_ticks(0, FEED_TICK, {c - 1: part(piece, c) for c in range(1, ROW_CHUNKS)})
+        finish(stores(ROW_CHUNKS - 1))
+
+    def hidden_phase(weights, ggr, gur):
+        load_weights = copies_of(w_sem, (wg_hbm, weights.at[0]), (wu_hbm, weights.at[1]))
+
+        def loads(c):
+            return copies_of(pre_sem, *both_sides(ggr_hbm, ggr, c), *both_sides(gur_hbm, gur, c))
+
+        def piece(c):
+            if c == 0:
+                finish(load_weights)
+            else:
+                pass_on(c - 1, False)
+            finish(loads(c))
+
+            def tile(n, carry):
+                rows = pl.ds(pl.multiple_of(n * TILE, TILE), TILE)
+                total_part = lax.dot_general(ggr[...], weights[0, rows, :], nt, preferred_element_type=F32)
+                total_part = total_part + lax.dot_general(
+                    gur[...], weights[1, rows, :], nt, preferred_element_type=F32)
+                xs[c, :, rows] = total_part[0:chunk]
+                cs[c % 2, :, rows] = total_part[chunk : 2 * chunk]
+                return carry
+            lax.fori_loop(0, width // TILE, tile, 0)
+            core_copy(c, False).start()
+            if c + 1 < ROW_CHUNKS:
+                start(loads(c + 1))
+
+        start(load_weights)
+        start(loads(0))
+        run_ticks(
+            FEED_TICK, HIDDEN_TICK, {FEED_TICK + c: part(piece, c) for c in range(ROW_CHUNKS)})
+
+    def branch_phase(branch, seed, low, turned, w_out, mixed_grad, token_rows):
+        load_weight = copies_of(w_sem, (w_out_hbm, w_out))
+        token_piece = full // ROW_CHUNKS
+
+        def loads(c):
             rows = pl.ds(c * chunk, chunk)
-            fetch((branch_hbm.at[rows], branch), (seed_hbm.at[rows], seed))
+            return copies_of(pre_sem, (branch_hbm.at[rows], branch), (seed_hbm.at[rows], seed))
+
+        def stores(c):
+            i = c % 2
+            return copies_of(
+                st_sem.at[pl.ds(4 * i, 4)],
+                (turned.at[i, :, pl.ds(0, chunk)], gbt_hbm.at[:, side_rows(0, c)]),
+                (turned.at[i, :, pl.ds(chunk, chunk)], gbt_hbm.at[:, side_rows(1, c)]),
+                *[(
+                    mixed_grad.at[i, pl.ds(s * chunk, chunk)],
+                    gqkv_hbm.at[sequence_rows(s, c), pl.ds(2 * head_cols, head_cols)],
+                ) for s in range(2)])
+
+        def hidden_store(c):
+            return copies_of(gh_sem, (xs.at[c], gh_hbm.at[pl.ds(c * chunk, chunk)]))
+
+        def token_load(c):
+            return copies_of(tok_sem, (tok_hbm.at[pl.ds(c * token_piece, token_piece)], token_rows))
+
+        def first(c):
+            i = c % 2
+            finish(loads(c))
             x_copy(c, False).wait()
             grad_hidden = xs[c] + xr[c] + seed[...].astype(F32)
             xs[c] = grad_hidden
+            start(hidden_store(c))
             values = branch[...]
             inv = mean_inverse(values)
             vec[1:2, :] += column_sum(grad_hidden * values * inv)
@@ -711,182 +798,264 @@
             grad = inv * scaled - values * (inv * inv * inv * dot / width)
             xr[c] = grad
             to_sibling(c, False).start()
-            low[0:chunk, :] = grad.astype(BF16)
-            turned[:, 0:chunk] = grad.astype(BF16).T
-            fetch((xs.at[c], gh_hbm.at[rows]))
+            if c >= 2:
+                finish(stores(c - 2))
+            low[i, 0:chunk, :] = grad.astype(BF16)
+            turned[i, :, 0:chunk] = grad.astype(BF16).T
+            if c + 1 < ROW_CHUNKS:
+                start(loads(c + 1))
+
+        def second(c):
+            i = c % 2
             to_sibling(c, False).wait_recv()
-            low[chunk : 2 * chunk, :] = ag[c % 2].astype(BF16)
-            turned[:, chunk : 2 * chunk] = ag[c % 2].astype(BF16).T
-            fetch(
-                (turned.at[:, pl.ds(0, chunk)], gbt_hbm.at[:, rows]),
-                (turned.at[:, pl.ds(chunk, chunk)], gbt_hbm.at[:, pl.ds(half + c * chunk, chunk)]),
-                (low.at[pl.ds(0, chunk)], gb_at(0, c)),
-                (low.at[pl.ds(chunk, chunk)], gb_at(1, c)))
+            if c == 0:
+                finish(load_weight)
+            other = ag[i].astype(BF16)
+            low[i, chunk : 2 * chunk, :] = other
+            turned[i, :, chunk : 2 * chunk] = other.T
+            mixed_grad[i] = lax.dot_general(
+                low[i], w_out[...], nt, preferred_element_type=F32).astype(BF16)
+            start(stores(c))
+            finish(hidden_store(c))
             to_sibling(c, False).wait_send()
 
-        def gb_at(s, c):
-            first = jnp.where(core == s, 0, half) + c * chunk
-            return token_out.at[pl.ds(pl.multiple_of(first, chunk), chunk)]
-        pl.run_scoped(
-            scoped, pltpu.VMEM((chunk, width), F32), pltpu.VMEM((chunk, width), BF16),
-            pltpu.VMEM((2 * chunk, width), BF16), pltpu.VMEM((width, 2 * chunk), BF16))
-
-    def attention_back():
+        def turn(c):
+            finish(token_load(c))
+            at[0, :, pl.ds(c * token_piece, token_piece)] = token_rows[...].T
+            if c + 1 < ROW_CHUNKS:
+                start(token_load(c + 1))
+
+        start(load_weight)
+        start(loads(0))
+        start(token_load(0))
+        work = {HIDDEN_TICK + c: [] for c in range(ROW_CHUNKS + 1)}
+        work[HIDDEN_TICK].append(part(pass_on, ROW_CHUNKS - 1, False))
+        for c in range(ROW_CHUNKS):
+            work[HIDDEN_TICK + c].append(part(first, c))
+            work[HIDDEN_TICK + c + 1].append(part(second, c))
+        work[HIDDEN_TICK + 3] += [part(turn, 0)]
+        work[HIDDEN_TICK + 4] += [part(turn, c) for c in range(1, ROW_CHUNKS)]
+        run_ticks(HIDDEN_TICK, BRANCH_TICK, work)
+        for c in range(ROW_CHUNKS - 2, ROW_CHUNKS):
+            finish(stores(c))
+
+    def attention_phase(query, key, value, mixed_grad, dq, dk, dv, raw, bias):
         heads = head_cols // HEAD
         q_rows = min(256, full)
         scale = HEAD ** (-0.5)
-
-        def scoped(query, key, value, mixed_grad, dq, dk, dv, raw):
-            def products(w_out, rows_buf):
-                fetch((w_out_hbm, w_out), (query_hbm, query), (key_hbm, key), (value_hbm, value))
-                for c in range(full // q_rows):
-                    rows = pl.ds(c * q_rows, q_rows)
-                    fetch((token_out.at[rows], rows_buf))
-                    mixed_grad[rows, :] = lax.dot_general(
-                        rows_buf[...], w_out[...], (((1,), (1,)), ((), ())),
-                        preferred_element_type=F32).astype(BF16)
-            pl.run_scoped(
-                products, pltpu.VMEM(w_out_hbm.shape, BF16), pltpu.VMEM((q_rows, width), BF16))
-
-            def head(h, carry):
-                cols = pl.ds(pl.multiple_of(h * HEAD, HEAD), HEAD)
-                dk[:, cols] = jnp.zeros((full, HEAD), F32)
-                dv[...] = jnp.zeros((full, HEAD), F32)
-                for i in range(full // q_rows):
-                    rows, keys = slice(i * q_rows, (i + 1) * q_rows), (i + 1) * q_rows
-                    q_block, grad_block = query[rows, cols], mixed_grad[rows, cols]
-                    key_block, value_block = key[0:keys, cols], value[0:keys, cols]
-                    nt = (((1,), (1,)), ((), ()))
-                    scores = lax.dot_general(key_block, q_block, nt, preferred_element_type=F32) * scale
-                    key_at = lax.broadcasted_iota(jnp.int32, (keys, q_rows), 0)
-                    query_at = lax.broadcasted_iota(jnp.int32, (keys, q_rows), 1) + i * q_rows
-                    allowed = (
-                        (seg_col[0:keys, :] == seg_row[:, rows])
-                        & (key_at <= query_at)
-                        & ((live_col[0:keys, :] > 0) | (key_at == query_at)))
-                    scores = jnp.where(allowed, scores, NEG_FILL)
-                    prob = jnp.exp(scores - log_totals[pl.ds(h, 1), rows])
-                    grad_prob = lax.dot_general(value_block, grad_block, nt, preferred_element_type=F32)
-                    row_dot = jnp.sum(prob * grad_prob, axis=0, keepdims=True)
-                    grad_scores = (prob * (grad_prob - row_dot)).astype(BF16)
-                    dq[rows, cols] = lax.dot_general(
-                        grad_scores, key_block, (((0,), (0,)), ((), ())), preferred_element_type=F32) * scale
-                    dk[0:keys, cols] += jnp.dot(grad_scores, q_block, preferred_element_type=F32) * scale
-                    dv[0:keys, :] += jnp.dot(prob.astype(BF16), grad_block, preferred_element_type=F32)
-                mixed_grad[:, cols] = dv[...].astype(BF16)
+        value_cols = pl.ds(2 * head_cols, head_cols)
+        loads = copies_of(
+            pre_sem, (query_hbm, query), (key_hbm, key), (value_hbm, value),
+            (gqkv_hbm.at[:, value_cols], mixed_grad))
+
+        def masks():
+            for i in range(full // q_rows):
+                rows, keys = slice(i * q_rows, (i + 1) * q_rows), (i + 1) * q_rows
+                key_at = lax.broadcasted_iota(jnp.int32, (keys, q_rows), 0)
+                query_at = lax.broadcasted_iota(jnp.int32, (keys, q_rows), 1) + i * q_rows
+                allowed = (
+                    (seg_col[0:keys, :] == seg_row[:, rows])
+                    & (key_at <= query_at)
+                    & ((live_col[0:keys, :] > 0) | (key_at == query_at)))
+                bias[0:keys, rows] = jnp.where(allowed, 0.0, NEG_FILL)
+            finish(loads)
+
+        def head(h):
+            cols = pl.ds(pl.multiple_of(h * HEAD, HEAD), HEAD)
+            dk[:, cols] = jnp.zeros((full, HEAD), F32)
+            dv[...] = jnp.zeros((full, HEAD), F32)
+            for i in range(full // q_rows):
+                rows, keys = slice(i * q_rows, (i + 1) * q_rows), (i + 1) * q_rows
+                q_block, grad_block = query[rows, cols], mixed_grad[rows, cols]
+                key_block, value_block = key[0:keys, cols], value[0:keys, cols]
+                scores = lax.dot_general(key_block, q_block, nt, preferred_element_type=F32) * scale
+                prob = jnp.exp(scores + bias[0:keys, rows] - log_totals[pl.ds(h, 1), rows])
+                grad_prob = lax.dot_general(value_block, grad_block, nt, preferred_element_type=F32)
+                row_dot = jnp.sum(prob * grad_prob, axis=0, keepdims=True)
+                grad_scores = (prob * (grad_prob - row_dot)).astype(BF16)
+                dq[rows, cols] = lax.dot_general(
+                    grad_scores, key_block, (((0,), (0,)), ((), ())), preferred_element_type=F32) * scale
+                dk[0:keys, cols] += jnp.dot(grad_scores, q_block, preferred_element_type=F32) * scale
+                dv[0:keys, :] += jnp.dot(prob.astype(BF16), grad_block, preferred_element_type=F32)
+            mixed_grad[:, cols] = dv[...].astype(BF16)
+
+        store_value = copies_of(st_sem, (mixed_grad, gqkv_hbm.at[:, value_cols]))
+        sides = ((dq, query_raw_hbm, query_inv, query_gain), (dk, key_raw_hbm, key_inv, key_gain))
+
+        def load_raw(which):
+            return copies_of(pre_sem, (sides[which][1], raw))
+
+        def back(which):
+            grads, _, inv, gain = sides[which]
+            finish(load_raw(which))
+            lanes = lax.broadcasted_iota(jnp.int32, (q_rows, HEAD), 1)
+
+            def block_back(i, carry):
+                rows = pl.ds(pl.multiple_of(i * q_rows, q_rows), q_rows)
+                dot = jnp.zeros((q_rows, 1), F32)
+                for h in range(heads):
+                    cols = slice(h * HEAD, (h + 1) * HEAD)
+                    grad = grads[rows, cols]
+                    grad = grad * cosine[rows, :] + pltpu.roll(grad, HEAD // 2, 1) * sine[rows, :]
+                    raw_rows = raw[rows, cols]
+                    gain_cols = slice(which * head_cols + h * HEAD, which * head_cols + (h + 1) * HEAD)
+                    vec[2:3, gain_cols] += column_sum(grad * raw_rows * inv[rows, :])
+                    scaled = grad * gain[:, cols]
+                    grads[rows, cols] = scaled
+                    dot = dot + jnp.sum(scaled * raw_rows, axis=1, keepdims=True)
+                if which == 0:
+                    dots[rows, :] = jnp.broadcast_to(dot, (q_rows, HEAD))
+                else:
+                    dots[rows, :] = jnp.where(lanes == 0, dots[rows, :], dot)
                 return carry
-            lax.fori_loop(0, heads, head, 0)
-            fetch((mixed_grad, gqkv_hbm.at[:, pl.ds(2 * head_cols, head_cols)]))
-
-            lanes = lax.broadcasted_iota(jnp.int32, (q_rows, HEAD), 1)
-            vec[2:3, :] = jnp.zeros((1, width), F32)
-            for which, (grads, raw_hbm, inv, gain) in enumerate((
-                (dq, query_raw_hbm, query_inv, query_gain), (dk, key_raw_hbm, key_inv, key_gain))):
-                fetch((raw_hbm, raw))
-
-                def back(i, carry):
-                    rows = pl.ds(pl.multiple_of(i * q_rows, q_rows), q_rows)
-                    dot = jnp.zeros((q_rows, 1), F32)
-                    for h in range(heads):
-                        cols = slice(h * HEAD, (h + 1) * HEAD)
-                        grad = grads[rows, cols]
-                        grad = grad * cosine[rows, :] + pltpu.roll(grad, HEAD // 2, 1) * sine[rows, :]
-                        raw_rows = raw[rows, cols]
-                        gain_cols = slice(which * head_cols + h * HEAD, which * head_cols + (h + 1) * HEAD)
-                        vec[2:3, gain_cols] += column_sum(grad * raw_rows * inv[rows, :])
-                        scaled = grad * gain[:, cols]
-                        grads[rows, cols] = scaled
-                        dot = dot + jnp.sum(scaled * raw_rows, axis=1, keepdims=True)
-                    if which == 0:
-                        dots[rows, :] = jnp.broadcast_to(dot, (q_rows, HEAD))
+            lax.fori_loop(0, full // q_rows, block_back, 0)
+
+        def dots_copy(i):
+            return remote(
+                dots, dots_in.at[i], ds_sem.at[i], dr_sem.at[i], at_tensor((sibling, across)[i]))
+
+        def dots_add(i):
+            dots_copy(i).wait()
+            dots[...] += dots_in[i]
+
+        def combine(which):
+            grads, _, inv, _ = sides[which]
+            for i in range(full // q_rows):
+                rows = slice(i * q_rows, (i + 1) * q_rows)
+                inv_rows = inv[rows, :]
+                dot = dots[rows, which : which + 1]
+                mixed_grad[rows, :] = (
+                    inv_rows * grads[rows, :]
+                    - raw[rows, :] * (inv_rows * inv_rows * inv_rows * dot / width)
+                ).astype(BF16)
+
+        def store_grads(which):
+            return copies_of(
+                st_sem, (mixed_grad, gqkv_hbm.at[:, pl.ds(which * head_cols, head_cols)]))
+
+        def after_heads():
+            start(store_value)
+            start(load_raw(0))
+
+        def back_query():
+            back(0)
+            start(load_raw(1))
+
+        def back_key():
+            back(1)
+            dots_copy(0).start()
+            finish(store_value)
+
+        def first_sum():
+            dots_add(0)
+            dots_copy(1).start()
+
+        def second_sum():
+            dots_add(1)
+            combine(1)
+            start(store_grads(1))
+            start(load_raw(0))
+
+        def last_part():
+            finish(store_grads(1))
+            finish(load_raw(0))
+            combine(0)
+            start(store_grads(0))
+
+        start(loads)
+        t = BRANCH_TICK
+        run_ticks(t, INPUT_TICK, {
+            t: masks,
+            (t + 1, t + 1 + heads): head,
+            t + heads: after_heads,
+            t + heads + 1: back_query,
+            t + heads + 2: back_key,
+            t + heads + 3: first_sum,
+            t + heads + 4: [second_sum, last_part],
+        })
+        finish(store_grads(0))
+
+    def input_phase(weights, grads, grad_hidden, low):
+        loads = copies_of(
+            w_sem, *[(w, weights.at[i]) for i, w in enumerate((wq_hbm, wk_hbm, wv_hbm))],
+            (gqkv_hbm, grads))
+
+        def piece(c):
+            if c == 0:
+                finish(loads)
+            else:
+                pass_on(c - 1, True)
+            for s in range(2):
+                rows = sequence_rows(s, c)
+
+                def tile(n, carry):
+                    cols = pl.ds(pl.multiple_of(n * TILE, TILE), TILE)
+                    total_part = jnp.zeros((chunk, TILE), F32)
+                    for i in range(3):
+                        total_part = total_part + lax.dot_general(
+                            grads[rows, i * head_cols : (i + 1) * head_cols], weights[i, cols, :],
+                            nt, preferred_element_type=F32)
+                    if s == 0:
+                        xs[c, :, cols] = total_part
                     else:
-                        dots[rows, :] = jnp.where(lanes == 0, dots[rows, :], dot)
+                        cs[c % 2, :, cols] = total_part
                     return carry
-                lax.fori_loop(0, full // q_rows, back, 0)
-            for i, peer in enumerate((sibling, across)):
-                copy = remote(dots, dots_in.at[i], ds_sem.at[i], dr_sem.at[i], at_tensor(peer))
-                copy.start()
-                copy.wait()
-                dots[...] += dots_in[i]
-            for which, (grads, raw_hbm, inv) in enumerate((
-                (dq, query_raw_hbm, query_inv), (dk, key_raw_hbm, key_inv))):
-                fetch((raw_hbm, raw))
-                for i in range(full // q_rows):
-                    rows = slice(i * q_rows, (i + 1) * q_rows)
-                    inv_rows = inv[rows, :]
-                    dot = dots[rows, which : which + 1]
-                    mixed_grad[rows, :] = (
-                        inv_rows * grads[rows, :]
-                        - raw[rows, :] * (inv_rows * inv_rows * inv_rows * dot / width)
-                    ).astype(BF16)
-                fetch((mixed_grad, gqkv_hbm.at[:, pl.ds(which * head_cols, head_cols)]))
-        rows_of = (full, head_cols)
-        pl.run_scoped(
-            scoped, pltpu.VMEM(rows_of, BF16), pltpu.VMEM(rows_of, BF16), pltpu.VMEM(rows_of, BF16),
-            pltpu.VMEM(rows_of, BF16), pltpu.VMEM(rows_of, F32), pltpu.VMEM(rows_of, F32),
-            pltpu.VMEM((full, HEAD), F32), pltpu.VMEM(rows_of, F32))
-
-    def gains_sum():
-        copy = remote(vec, vec_in.at[0], vs_sem.at[0], vr_sem.at[0], at_tensor(sibling))
-        copy.start()
-        copy.wait()
-        vec[0:2, :] += vec_in[0, 0:2, :]
-        for i, peer in enumerate(vec_peers):
-            copy = remote(vec, vec_in.at[i + 1], vs_sem.at[i + 1], vr_sem.at[i + 1], at_dp(peer))
-            copy.start()
-            copy.wait()
-            vec[...] += vec_in[i + 1]
-
-    def turn_tokens():
-        def scoped(rows_buf):
-            for i in range(full // 256):
-                rows = pl.ds(i * 256, 256)
-                fetch((tok_hbm.at[rows], rows_buf))
-                at[0, :, rows] = rows_buf[...].T
-        pl.run_scoped(scoped, pltpu.VMEM((256, width), BF16))
-
-    def input_partial():
-        def scoped(weights, grads):
-            fetch(*[(w, weights.at[i]) for i, w in enumerate((wq_hbm, wk_hbm, wv_hbm))], (gqkv_hbm, grads))
-            for c in range(ROW_CHUNKS):
-                for s in range(2):
-                    first = jnp.where(core == s, 0, half) + c * chunk
-                    rows = pl.ds(pl.multiple_of(first, chunk), chunk)
-
-                    def tile(n, carry):
-                        cols = pl.ds(pl.multiple_of(n * TILE, TILE), 512)
-                        part = jnp.zeros((chunk, TILE), F32)
-                        for i in range(3):
-                            part = part + lax.dot_general(
-                                grads[rows, i * head_cols : (i + 1) * head_cols], weights[i, cols, :],
-                                (((1,), (1,)), ((), ())), preferred_element_type=F32)
-                        if s == 0:
-                            xs[c, :, cols] = part
-                        else:
-                            cs[c % 2, :, cols] = part
-                        return carry
-                    lax.fori_loop(0, width // TILE, tile, 0)
-                send_partial(c, True)
-        pl.run_scoped(
-            scoped, pltpu.VMEM((3,) + wq_hbm.shape, BF16), pltpu.VMEM((full, 3 * head_cols), BF16))
-
-    def token_grads(c):
-        def scoped(grad_hidden, low):
-            fetch((gh_hbm.at[pl.ds(c * chunk, chunk)], grad_hidden))
+                lax.fori_loop(0, width // TILE, tile, 0)
+            core_copy(c, True).start()
+
+        def hidden_load(c):
+            return copies_of(gh_sem, (gh_hbm.at[pl.ds(c * chunk, chunk)], grad_hidden))
+
+        def stores(c):
+            return copies_of(
+                st_sem, *[(low.at[s], token_out.at[sequence_rows(s, c)]) for s in range(2)])
+
+        def first(c):
+            finish(hidden_load(c))
             x_copy(c, True).wait()
-            total_rows = xs[c] + xr[c] + grad_hidden[...]
-            xr[c] = total_rows
+            xr[c] = xs[c] + xr[c] + grad_hidden[...]
             to_sibling(c, True).start()
-            low[0] = total_rows.astype(BF16)
+            if c + 1 < ROW_CHUNKS:
+                start(hidden_load(c + 1))
+
+        def second(c):
+            if c >= 1:
+                finish(stores(c - 1))
+            low[0] = xr[c].astype(BF16)
             to_sibling(c, True).wait_recv()
             low[1] = ag[c % 2].astype(BF16)
-            copies = []
-            for s in range(2):
-                first = jnp.where(core == s, 0, half) + c * chunk
-                copies.append((low.at[s], token_out.at[pl.ds(pl.multiple_of(first, chunk), chunk)]))
-            fetch(*copies)
+            start(stores(c))
             to_sibling(c, True).wait_send()
-        pl.run_scoped(scoped, pltpu.VMEM((chunk, width), F32), pltpu.VMEM((2, chunk, width), BF16))
+
+        vec_peer_ids = [at_tensor(sibling)] + [at_dp(peer) for peer in vec_peers]
+
+        def vec_copy(i):
+            return remote(vec, vec_in.at[i], vs_sem.at[i], vr_sem.at[i], vec_peer_ids[i])
+
+        def vec_step(i):
+            if i >= 1:
+                vec_copy(i - 1).wait()
+                if i == 1:
+                    vec[0:2, :] += vec_in[0, 0:2, :]
+                else:
+                    vec[...] += vec_in[i - 1]
+            if i < len(vec_peer_ids):
+                vec_copy(i).start()
+
+        start(loads)
+        start(hidden_load(0))
+        work = {k: [] for k in range(INPUT_TICK, total)}
+        for c in range(ROW_CHUNKS):
+            work[INPUT_TICK + c].append(part(piece, c))
+            work[TOKEN_TICK + c].append(part(first, c))
+            work[TOKEN_TICK + c + 1].append(part(second, c))
+        work[INPUT_TICK + ROW_CHUNKS].append(part(pass_on, ROW_CHUNKS - 1, True))
+        for i in range(len(vec_peer_ids) + 1):
+            work[INPUT_TICK + 2 + i].append(part(vec_step, i))
+        work[first_heads + 1].append(lambda: at_load(3).start())
+        work[first_heads + 2].append(lambda: at_load(3).wait())
+        run_ticks(INPUT_TICK, total, {k: fns for k, fns in work.items() if fns})
+        finish(stores(ROW_CHUNKS - 1))
 
     vec[...] = jnp.zeros(vec.shape, F32)
     vec[0:1, :] = gain_mlp_part[...]
@@ -894,33 +1063,28 @@
     at_load(1).start()
     for k in range(3):
         b_load(jnp.int32(k), lambda copy: copy.start())
-    at_load(0).wait()
-    pair_send(jnp.int32(0))
-    pair_send(jnp.int32(1))
-    feed_back()
+    both = 2 * chunk
+    rows_of = (full, head_cols)
+    pl.run_scoped(
+        feed_phase, pltpu.VMEM(wd_hbm.shape, BF16), pltpu.VMEM((both, width), BF16),
+        pltpu.VMEM((both, hidden), F32), pltpu.VMEM((both, hidden), F32),
+        pltpu.VMEM((both, hidden), BF16), pltpu.VMEM((both, hidden), BF16))
     at_load(1).wait()
-
-    work = {0: hidden_partial, 8: attention_back, 9: turn_tokens, 10: input_partial, 11: gains_sum}
-    for c in range(ROW_CHUNKS):
-        work[3 + c] = functools.partial(branch_back, c)
-        work[13 + c] = functools.partial(token_grads, c)
-
-    def body(k, carry):
-        tick(k)
-        for when, fn in work.items():
-            @pl.when(k == when)
-            def _(fn=fn):
-                fn()
-
-        @pl.when(k == first_heads + 1)
-        def _():
-            at_load(3).start()
-
-        @pl.when(k == first_heads + 2)
-        def _():
-            at_load(3).wait()
-        return carry
-    lax.fori_loop(0, total, body, 0)
+    pl.run_scoped(
+        hidden_phase, pltpu.VMEM((2,) + wg_hbm.shape, BF16), pltpu.VMEM((both, hidden), BF16),
+        pltpu.VMEM((both, hidden), BF16))
+    pl.run_scoped(
+        branch_phase, pltpu.VMEM((chunk, width), F32), pltpu.VMEM((chunk, width), BF16),
+        pltpu.VMEM((2, both, width), BF16), pltpu.VMEM((2, width, both), BF16),
+        pltpu.VMEM(w_out_hbm.shape, BF16), pltpu.VMEM((2, both, head_cols), BF16),
+        pltpu.VMEM((full // ROW_CHUNKS, width), BF16))
+    pl.run_scoped(
+        attention_phase, pltpu.VMEM(rows_of, BF16), pltpu.VMEM(rows_of, BF16), pltpu.VMEM(rows_of, BF16),
+        pltpu.VMEM(rows_of, BF16), pltpu.VMEM(rows_of, F32), pltpu.VMEM(rows_of, F32),
+        pltpu.VMEM((full, HEAD), F32), pltpu.VMEM(rows_of, F32), pltpu.VMEM((full, full), F32))
+    pl.run_scoped(
+        input_phase, pltpu.VMEM((3,) + wq_hbm.shape, BF16), pltpu.VMEM((full, 3 * head_cols), BF16),
+        pltpu.VMEM((chunk, width), F32), pltpu.VMEM((2, chunk, width), BF16))
     finish_chunk(jnp.int32(total - 1), jnp.int32(passes - 1))
     out_act(jnp.int32(total - 1), lambda copy: copy.wait())
     gains_out[...] = vec[...]
@@ -984,7 +1148,8 @@
             DMA,
         ]
         + [per_chunk] * 12
-        + [DMA((2,)), DMA((2,)), DMA((steps + 1,)), DMA((steps + 1,)), DMA((4,)), REG, REG, REG],
+        + [DMA((2,)), DMA((2,)), DMA((steps + 1,)), DMA((steps + 1,)), DMA((4,)), DMA((6,)), DMA((8,)), DMA((1,)), DMA((1,)),
+           REG, REG, REG],
         compiler_params=pltpu.CompilerParams(
             collective_id=2, has_side_effects=True, vmem_limit_bytes=VMEM_LIMIT),
     )(*hbm, *vmem_args)

time: 1180 us -> 987 us (0.84)
  Pallas kernels: 1080 us -> 886 us
    pallas_call x1, Pallas kernels: 883 us -> 690 us  [backward_layer(): pl.pallas_call(functools.partial(backward_kernel, dp_size, counts), out_s...]
where the time goes in v3:
time: 987 us; the launch traced here: 980 us
  Pallas kernels  886 us (90%)
  local copies, waits for them, and re-layouts  36.8 us (4%)
  matrix products  27 us (3%)
  other arithmetic  26.1 us (3%)
    pallas_call x1, Pallas kernels, backward_layer(): pl.pallas_call(functools.partial(backward_kernel, dp_size, counts), out_s...  690 us
    pallas_call x1, Pallas kernels, forward_layer(): pl.pallas_call(forward_kernel, out_shape=(shape(row_count, hidden), shape...  196 us
  transfers between devices with their start and end apart: 2, of which 0 were waited for; matrix products, arithmetic and copies ran while one was open for 3% of the time, Pallas kernels for 0%

profile of v3, /device:TPU:0, one launch (start us, length us, event | category | flops | bytes accessed | tf_op | source)
XLA Modules:
  0.0 980.2 jit_solution(16715983197601142664)
XLA Ops:
  0.7 6.7 multiply_reduce_fusion.1
  7.4 2.4 multiply_reduce_fusion
  10.4 6.2 convolution_convert_fusion.value_hbm
  17.3 3.4 fusion.20
  20.7 4.9 dynamic-slice_select_fusion
  25.7 1.7 fusion.10
  28.0 2.6 collective-permute-start.1
  30.6 1.3 pad_maximum_fusion.2
  32.0 1.2 copy.64
  33.2 1.9 copy.63
  35.1 2.3 copy.88
  38.6 2.9 copy.75.query_raw_hbm
  41.5 1.8 copy.76.key_raw_hbm
  45.4 1.9 multiply_multiply_fusion.1
  47.8 1.1 pad_maximum_fusion
  49.5 1.9 fusion
  51.4 1.9 fusion.1
  53.4 4.7 fusion.2
  58.1 4.4 fusion.12
  62.5 3.5 fusion.13
  66.2 1.3 copy.87
  67.5 1.3 copy.73.query_hbm
  68.8 1.3 copy.74.key_hbm
  72.2 1.7 fusion.15
  75.6 195.8 %shard_map.246 = (f32[1024,2048]{1,0:T(8,128)}, f32[1024,2048]{1,0:T(8,128)}, bf16[1024,2048]{1,0:T(8,128)(2,1)}, bf16[2048,1024]{1,0:T(8,128)(2,1)}, bf16[1024,...) custom-call(bf16[1024,512]{1,0:T(8,128)(2,1)} %pad_maximum_fusion.1., ...), custom_call_target="tpu_custom_call" | custom-call | tf_op jit(solution)/shard_map/pallas_call | solution.py:298
  271.4 690.2 %shard_map.247 = (f32[2560,256]{1,0:T(8,128)}, f32[256,5632]{1,0:T(8,128)}, bf16[1024,2048]{1,0:T(8,128)(2,1)}, f32[8,2048]{1,0:T(8,128)}, bf16[1024,2048]{1,0:T...) custom-call(bf16[2048,1024]{1,0:T(8,128)(2,1)} %get-tuple-element.27, ...), custom_call_target="tpu_custom_call" | custom-call | tf_op jit(solution)/shard_map/pallas_call | solution.py:1109
  963.3 2.5 fusion.31
  965.8 4.9 fusion.30
  971.5 1.5 slice.92
  974.3 2.1 copy.91
  976.4 1.6 copy-done.4
  978.0 2.0 copy.92
  (69 shorter events, 14.0 us)
Async XLA Ops:
  0.6 6.7 copy-start
  0.7 6.7 copy-start.8
  9.8 18.2 %collective-permute-start = (f32[2,1024]{1,0:T(2,128)S(1)}, f32[2,1024]{1,0:T(2,128)S(1)}, u32[]{:S(2)}, u32[]{:S(2)}) collective-permute-start(f32[2,1024]{1,0:T(2,128)S(1)} %pad_maximum_fusion.5), channel_id=1, source_target_pairs={{0,1},{1,0},{2,3},{3,2},{4,5},{5,4},{6,7},{7,6},{8,9},{9,8},{10,11... | collective-permute-start | bytes 24584 | tf_op jit(solution)/shard_map/ppermute | solution.py:1232
  10.4 6.3 copy-start.11
  10.4 6.3 copy-start.12
  10.4 6.3 copy-start.15
  20.7 6.7 copy-start.16
  20.7 9.9 %copy-start.1 = (f32[1024,64]{1,0:T(8,128)S(1)}, f32[1024,64]{1,0:T(8,128)}, u32[]{:S(2)}) copy-start(f32[1024,64]{1,0:T(8,128)} %get-tuple-element.68) | copy-start | bytes 786436
  20.7 9.9 %copy-start.2 = (f32[1024,64]{1,0:T(8,128)S(1)}, f32[1024,64]{1,0:T(8,128)}, u32[]{:S(2)}) copy-start(f32[1024,64]{1,0:T(8,128)} %get-tuple-element.67) | copy-start | bytes 786436
  20.7 9.9 %copy-start.9 = (f32[1024,64]{1,0:T(8,128)S(1)}, f32[1024,64]{1,0:T(8,128)}, u32[]{:S(2)}) copy-start(f32[1024,64]{1,0:T(8,128)} %get-tuple-element.66) | copy-start | bytes 786436
  25.7 11.7 %copy-start.13 = (bf16[2048]{0:T(1024)(128)(2,1)S(1)}, bf16[2048]{0:T(1024)(128)(2,1)}, u32[]{:S(2)}) copy-start(bf16[2048]{0:T(1024)(128)(2,1)} %param.24) | copy-start | bytes 12292
  25.7 12.3 %copy-start.14 = (bf16[2048]{0:T(1024)(128)(2,1)S(1)}, bf16[2048]{0:T(1024)(128)(2,1)}, u32[]{:S(2)}) copy-start(bf16[2048]{0:T(1024)(128)(2,1)} %param.28) | copy-start | bytes 12292
  28.0 17.3 %collective-permute-start.1 = (f32[2,1024]{1,0:T(2,128)S(1)}, f32[2,1024]{1,0:T(2,128)S(1)}, u32[]{:S(2)}, u32[]{:S(2)}) collective-permute-start(f32[2,1024]{1,0:T(2,128)S(1)} %fusion.29), channel_id=1, source_target_pairs={{0,2},{1,3},{2,0},{3,1},{4,6},{5,7},{6,4},{7,5},{8,10},{9,11},{10,... | collective-permute-start | bytes 24584 | tf_op jit(solution)/shard_map/ppermute | solution.py:1236
  45.4 1.9 copy-start.7
  53.4 4.7 copy-start.10
  62.5 5.0 copy-start.5
  965.8 4.9 copy-start.6
  970.7 3.6 copy-start.3
  974.3 3.7 copy-start.4

commit v4 on v3

--- a/solution.py
+++ b/solution.py
@@ -27,7 +27,7 @@
 INPUT_TICK = 21
 TOKEN_TICK = 26
 HBM_NAMES = (
-    "gdrt", "hlt", "tokens", "inner", "mixed", "gdr", "gate", "up", "branch", "seed",
+    "gdrt", "hlt", "tokens", "inner", "mixed", "gdr", "gate", "up", "branch", "cotangent",
     "query", "key", "value", "query_raw", "key_raw",
     "w_out", "w_gate", "w_up", "w_down", "w_query", "w_key", "w_value",
 )
@@ -57,33 +57,47 @@
 
 
 def forward_kernel(
-    mixed, w_out, attn_gain, mlp_gain, tok_hbm, seed_hbm, wg_hbm, wu_hbm, wd_hbm,
-    gate_out, up_out, inner_out, hlt_out, gdr_out, gdrt_out, branch_out, out_out, gain_out,
-    wg, wu, wd, cs, crecv, xs, xr, xr2, ag, gate_buf, up_buf, inner_buf, low_buf, hlt_buf,
-    out_buf, tok, seed,
-    w_sem, t_sem, s_sem, cs_sem, cr_sem, xs_sem, xr_sem, as_sem, ar_sem, cs2_sem, cr2_sem, xs2_sem, xr2_sem,
+    tok_hbm, cot_hbm, wq_hbm, wk_hbm, wv_hbm, wo_hbm, wg_hbm, wu_hbm, wd_hbm, cos_hbm, sin_hbm,
+    seg_live, seg_row, query_gain, key_gain, attn_gain, mlp_gain,
+    gate_out, up_out, inner_out, hlt_out, gdr_out, gdrt_out, branch_out, out_out,
+    query_out, key_out, value_out, query_raw_out, key_raw_out, mixed_out,
+    gain_out, inverse_out, log_out,
+    wg, wu, cs, crecv, xs, xr, xr2, ag, squares, squares_in,
+    w_sem, t_sem, s_sem, a_sem, r_sem, m_sem, sq_s_sem, sq_r_sem, sx_s_sem, sx_r_sem,
+    cs_sem, cr_sem, xs_sem, xr_sem, as_sem, ar_sem, cs2_sem, cr2_sem, xs2_sem, xr2_sem,
     gs_sem, gr_sem, os_sem, or_sem, g_sem, h_sem, b_sem, d_sem, o_sem,
 ):
     core, sibling, across = tensor_peers()
     chunk = xs.shape[1]
     half = chunk * ROW_CHUNKS
-    tiles = wg.shape[1] // TILE
-    wide_tiles = wd.shape[1] // TILE
-    loads = [
+    full = 2 * half
+    both = 2 * chunk
+    width, hidden = xs.shape[2], wg.shape[1]
+    head_cols = wq_hbm.shape[1]
+    heads = head_cols // HEAD
+    tiles = hidden // TILE
+    wide_tiles = width // TILE
+    last = ROW_CHUNKS - 1
+    nt = (((1,), (1,)), ((), ()))
+
+    def start(copies):
+        for copy in copies:
+            copy.start()
+
+    def finish(copies):
+        for copy in copies:
+            copy.wait()
+
+    def own_rows(s, c):
+        return pl.ds(pl.multiple_of(c * both + jnp.where(core == s, 0, chunk), chunk), chunk)
+
+    def row_load(c, src, dst, sem):
+        return pltpu.make_async_copy(src.at[own_rows(0, c)], dst.at[c % 2], sem.at[c % 2])
+
+    wide_loads = [
         pltpu.make_async_copy(src, dst, w_sem.at[i])
-        for i, (src, dst) in enumerate(((wg_hbm, wg), (wu_hbm, wu), (wd_hbm, wd)))
+        for i, (src, dst) in enumerate(((wg_hbm, wg), (wu_hbm, wu)))
     ]
-    for load in loads:
-        load.start()
-
-    def row_load(c, src, dst, sem):
-        return pltpu.make_async_copy(
-            src.at[pl.ds(c * chunk, chunk)], dst.at[c % 2], sem.at[c % 2])
-
-    for c in range(2):
-        row_load(c, tok_hbm, tok, t_sem).start()
-        row_load(c, seed_hbm, seed, s_sem).start()
-    greet({"tensor": sibling}, {"tensor": across})
 
     def remote(src, dst, send_sem, recv_sem, peer):
         return pltpu.make_async_remote_copy(
@@ -128,22 +142,190 @@
             for s in range(2)
         ]
 
-    for c in range(ROW_CHUNKS):
+    def square_copy(c):
+        return remote(
+            squares.at[c], squares_in.at[0, c], sq_s_sem.at[c], sq_r_sem.at[c], sibling)
+
+    def square_x_copy(c):
+        return remote(
+            squares.at[c], squares_in.at[1, c], sx_s_sem.at[c], sx_r_sem.at[c], across)
+
+    def square_pass_on(c):
+        square_copy(c).wait()
+        squares[c] += squares_in[0, c]
+        square_x_copy(c).start()
+
+    def projections(weights, tok, query_raw, key_raw, value, value_turned):
+        def tok_load(c):
+            return pltpu.make_async_copy(
+                tok_hbm.at[pl.ds(c * both, both)], tok.at[c % 2], t_sem.at[c % 2])
+
+        loads = [
+            pltpu.make_async_copy(w, weights.at[i], a_sem.at[i])
+            for i, w in enumerate((wq_hbm, wk_hbm, wv_hbm))
+        ]
+        tok_load(0).start()
+        start(loads)
+        tok_load(1).start()
+        greet({"tensor": sibling}, {"tensor": across})
+        lanes = lax.broadcasted_iota(jnp.int32, (both, HEAD), 1)
+        for c in range(ROW_CHUNKS):
+            at = slice(c * both, (c + 1) * both)
+            tok_load(c).wait()
+            if c == 0:
+                loads[0].wait()
+            query_raw[at, :] = jnp.dot(tok[c % 2], weights[0], preferred_element_type=F32)
+            if c == 0:
+                loads[1].wait()
+            key_raw[at, :] = jnp.dot(tok[c % 2], weights[1], preferred_element_type=F32)
+            query_square = jnp.sum(query_raw[at, :] * query_raw[at, :], axis=1, keepdims=True)
+            key_square = jnp.sum(key_raw[at, :] * key_raw[at, :], axis=1, keepdims=True)
+            squares[c] = jnp.where(lanes == 0, query_square, key_square)
+            square_copy(c).start()
+            if c == 0:
+                loads[2].wait()
+                start(wide_loads)
+            value[at, :] = jnp.dot(tok[c % 2], weights[2], preferred_element_type=F32).astype(BF16)
+            value_turned[:, at] = value[at, :].T
+            if c + 2 < ROW_CHUNKS:
+                tok_load(c + 2).start()
+            if c >= 1:
+                square_pass_on(c - 1)
+        square_pass_on(last)
+
+    def attend(c, query_raw, key_raw, query, key, value_turned, cosine, sine, w_out, mixed, bias):
+        first, keys = c * both, (c + 1) * both
+        at = slice(first, keys)
+        square_x_copy(c).wait()
+        squares[c] += squares_in[1, c]
+        inverse = lax.rsqrt(squares[c] / width + EPSILON)
+        inverse_out[at, :] = inverse
+        for raw, gain, lane, dst in (
+            (query_raw, query_gain, 0, query), (key_raw, key_gain, 1, key)):
+            gains = gain[...].astype(F32)
+            for h in range(heads):
+                cols = slice(h * HEAD, (h + 1) * HEAD)
+                normed = raw[at, cols] * inverse[:, lane : lane + 1] * gains[h : h + 1, :]
+                turned = normed * cosine[at, :] + pltpu.roll(normed, HEAD // 2, 1) * sine[at, :]
+                dst[at, cols] = turned.astype(BF16)
+        key_at = lax.broadcasted_iota(jnp.int32, (keys, both), 0)
+        query_at = lax.broadcasted_iota(jnp.int32, (keys, both), 1) + first
+        allowed = (
+            (seg_live[0:keys, 0:1] == seg_row[:, at])
+            & (key_at <= query_at)
+            & ((seg_live[0:keys, 1:2] > 0) | (key_at == query_at)))
+        bias[0:keys, :] = jnp.where(allowed, 0.0, NEG_FILL)
+
+        def head(h, carry):
+            cols = pl.ds(pl.multiple_of(h * HEAD, HEAD), HEAD)
+            scores = lax.dot_general(
+                key[0:keys, cols], query[at, cols], nt, preferred_element_type=F32) * HEAD ** (-0.5)
+            scores = scores + bias[0:keys, :]
+            top = jnp.max(scores, axis=0, keepdims=True)
+            powers = jnp.exp(scores - top)
+            total = jnp.sum(powers, axis=0, keepdims=True)
+            prob = (powers / total).astype(BF16)
+            log_out[pl.ds(h, 1), at] = top + jnp.log(total)
+            turned = jnp.dot(value_turned[cols, 0:keys], prob, preferred_element_type=F32)
+            mixed[c % 2, :, cols] = turned.T.astype(BF16)
+            return carry
+        lax.fori_loop(0, heads, head, 0)
+
+        def mixed_rows(s):
+            return pl.ds(pl.multiple_of(jnp.where(core == s, 0, chunk), chunk), chunk)
         if c >= 2:
             core_copy(c - 2).wait_send()
-        cs[c % 2] = jnp.dot(mixed[rows(half + c * chunk), :], w_out[...], preferred_element_type=F32)
+        cs[c % 2] = jnp.dot(mixed[c % 2, mixed_rows(1), :], w_out[...], preferred_element_type=F32)
         core_copy(c).start()
-        xs[c] = jnp.dot(mixed[rows(c * chunk), :], w_out[...], preferred_element_type=F32)
+        xs[c] = jnp.dot(mixed[c % 2, mixed_rows(0), :], w_out[...], preferred_element_type=F32)
+        start(mixed_copies(c, mixed))
         if c >= 1:
-            core_copy(c - 1).wait_recv()
-            xs[c - 1] += crecv[c - 1]
-            x_copy(c - 1).start()
+            pass_on(c - 1)
+
+    def mixed_copies(c, mixed):
+        return [
+            pltpu.make_async_copy(
+                mixed.at[c % 2, pl.ds(pl.multiple_of(jnp.where(core == s, 0, chunk), chunk), chunk)],
+                mixed_out.at[rows(s * half + c * chunk)], m_sem.at[c % 2, s])
+            for s in range(2)
+        ]
+
+    def pass_on(c):
+        core_copy(c).wait_recv()
+        xs[c] += crecv[c]
+        x_copy(c).start()
+
+    def attention(query_raw, key_raw, query, key, value, value_turned, cosine, sine, w_out):
+        tables = [
+            pltpu.make_async_copy(src, dst, r_sem.at[i])
+            for i, (src, dst) in enumerate(((cos_hbm, cosine), (sin_hbm, sine), (wo_hbm, w_out)))
+        ]
+        start(tables)
+        pl.run_scoped(
+            functools.partial(
+                projections, query_raw=query_raw, key_raw=key_raw, value=value,
+                value_turned=value_turned),
+            pltpu.VMEM((3,) + wq_hbm.shape, BF16), pltpu.VMEM((2, both, width), BF16))
+        finish(tables)
+        results = [
+            pltpu.make_async_copy(src, dst, a_sem.at[i])
+            for i, (src, dst) in enumerate((
+                (value, value_out), (query_raw, query_raw_out), (key_raw, key_raw_out),
+                (query, query_out), (key, key_out)))
+        ]
+        start(results[:3])
+
+        def chunks(mixed, bias):
+            for c in range(ROW_CHUNKS):
+                if c >= 2:
+                    finish(mixed_copies(c - 2, mixed))
+                attend(
+                    c, query_raw, key_raw, query, key, value_turned, cosine, sine, w_out, mixed, bias)
+            start(results[3:])
+            pass_on(last)
+            for c in range(last - 1, ROW_CHUNKS):
+                core_copy(c).wait_send()
+                finish(mixed_copies(c, mixed))
+            finish(results)
+        pl.run_scoped(
+            chunks, pltpu.VMEM((2, both, head_cols), BF16), pltpu.VMEM((full, both), F32))
+
+    rows_of = (full, head_cols)
+    pl.run_scoped(
+        attention, pltpu.VMEM(rows_of, F32), pltpu.VMEM(rows_of, F32), pltpu.VMEM(rows_of, BF16),
+        pltpu.VMEM(rows_of, BF16), pltpu.VMEM(rows_of, BF16), pltpu.VMEM((head_cols, full), BF16),
+        pltpu.VMEM((full, HEAD), F32), pltpu.VMEM((full, HEAD), F32), pltpu.VMEM(wo_hbm.shape, BF16))
+    pl.run_scoped(
+        functools.partial(
+            feed_forward, core, chunk, own_rows, row_load, rows, side_copies, turned_copies,
+            (x_copy, hidden_copy, core2_copy, x2_copy, grad_copy, out_copy), wide_loads, seg_live,
+            (tok_hbm, cot_hbm, wd_hbm, attn_gain, mlp_gain, wg, wu),
+            (gate_out, up_out, inner_out, hlt_out, gdr_out, gdrt_out, branch_out, out_out, gain_out),
+            (cs, crecv, xs, xr, xr2, ag),
+            (w_sem, t_sem, s_sem, g_sem, h_sem, b_sem, d_sem, o_sem)),
+        pltpu.VMEM(wd_hbm.shape, BF16), pltpu.VMEM((both, hidden), F32), pltpu.VMEM((both, hidden), F32),
+        pltpu.VMEM((both, hidden), BF16), pltpu.VMEM((both, width), BF16), pltpu.VMEM((width, both), BF16),
+        pltpu.VMEM((both, width), BF16), pltpu.VMEM((2, chunk, width), BF16),
+        pltpu.VMEM((2, chunk, width), BF16))
+
+
+def feed_forward(
+    core, chunk, own_rows, row_load, rows, side_copies, turned_copies, remote_copies, wide_loads, seg_live,
+    operands, results, buffers, sems,
+    wd, gate_buf, up_buf, inner_buf, low_buf, hlt_buf, out_buf, tok, seed,
+):
+    x_copy, hidden_copy, core2_copy, x2_copy, grad_copy, out_copy = remote_copies
+    tok_hbm, cot_hbm, wd_hbm, attn_gain, mlp_gain, wg, wu = operands
+    gate_out, up_out, inner_out, hlt_out, gdr_out, gdrt_out, branch_out, out_out, gain_out = results
+    cs, crecv, xs, xr, xr2, ag = buffers
+    w_sem, t_sem, s_sem, g_sem, h_sem, b_sem, d_sem, o_sem = sems
     last = ROW_CHUNKS - 1
-    core_copy(last).wait_recv()
-    xs[last] += crecv[last]
-    x_copy(last).start()
-    core_copy(last - 1).wait_send()
-    core_copy(last).wait_send()
+    tiles, wide_tiles = wg.shape[1] // TILE, wd.shape[1] // TILE
+    loads = wide_loads + [pltpu.make_async_copy(wd_hbm, wd, w_sem.at[2])]
+    loads[2].start()
+    for c in range(2):
+        row_load(c, tok_hbm, tok, t_sem).start()
+        row_load(c, cot_hbm, seed, s_sem).start()
 
     def feed(c):
         x_copy(c).wait()
@@ -208,10 +390,10 @@
         x2_copy(c).wait()
         down = xs[c] + xr2[c]
         inv = mean_inverse(down)
-        row_load(c, seed_hbm, seed, s_sem).wait()
-        seed_rows = seed[c % 2].astype(F32)
+        row_load(c, cot_hbm, seed, s_sem).wait()
+        seed_rows = seed[c % 2].astype(F32) * seg_live[own_rows(0, c), 1:2].astype(F32)
         if c + 2 < ROW_CHUNKS:
-            row_load(c + 2, seed_hbm, seed, s_sem).start()
+            row_load(c + 2, cot_hbm, seed, s_sem).start()
         normed = down * inv
         gain_total = gain_total + column_sum(seed_rows * normed)
         scaled = seed_rows * mlp_gain[...]
@@ -244,9 +426,8 @@
     def out_copies(c):
         return [
             pltpu.make_async_copy(
-                out_buf.at[pl.ds(s * chunk, chunk)],
-                out_out.at[pl.ds(pl.multiple_of(at * half + c * chunk, chunk), chunk)], o_sem.at[s])
-            for s, at in ((0, core), (1, 1 - core))
+                out_buf.at[pl.ds(s * chunk, chunk)], out_out.at[own_rows(s, c)], o_sem.at[s])
+            for s in range(2)
         ]
 
     def place(c):
@@ -284,9 +465,10 @@
         out_copy(c).wait_send()
 
 
-def forward_layer(mixed, w_out, attn_gain, mlp_gain, tok, seed, w_gate, w_up, w_down):
-    row_count, width = mixed.shape[0], w_out.shape[1]
-    hidden = w_gate.shape[1]
+def forward_layer(hbm, vmem_args):
+    tokens, w_query, w_gate = hbm[0], hbm[2], hbm[6]
+    row_count, width = tokens.shape
+    hidden, head_cols = w_gate.shape[1], w_query.shape[1]
     chunk = row_count // 2 // ROW_CHUNKS
     DMA = pltpu.SemaphoreType.DMA
     vmem, any_space = pl.BlockSpec(memory_space=pltpu.VMEM), pl.BlockSpec(memory_space=pl.ANY)
@@ -306,45 +488,49 @@
             shape(width, row_count, kind=BF16),
             shape(row_count // 2, width),
             shape(row_count, width, kind=BF16),
+            shape(row_count, head_cols, kind=BF16),
+            shape(row_count, head_cols, kind=BF16),
+            shape(row_count, head_cols, kind=BF16),
+            shape(row_count, head_cols),
+            shape(row_count, head_cols),
+            shape(row_count, head_cols, kind=BF16),
             shape(1, width),
+            shape(row_count, HEAD),
+            shape(head_cols // HEAD, row_count),
         ),
-        in_specs=[vmem] * 4 + [any_space] * 5,
-        out_specs=(any_space,) * 8 + (vmem,),
+        in_specs=[any_space] * len(hbm) + [vmem] * len(vmem_args),
+        out_specs=(any_space,) * 14 + (vmem,) * 3,
         scratch_shapes=[
             pltpu.VMEM(w_gate.shape, BF16),
-            pltpu.VMEM(w_up.shape, BF16),
-            pltpu.VMEM(w_down.shape, BF16),
+            pltpu.VMEM(w_gate.shape, BF16),
             pltpu.VMEM((2, chunk, width), F32),
             pltpu.VMEM((ROW_CHUNKS, chunk, width), F32),
             pltpu.VMEM((ROW_CHUNKS, chunk, width), F32),
             pltpu.VMEM((ROW_CHUNKS, chunk, width), F32),
             pltpu.VMEM((ROW_CHUNKS, chunk, width), F32),
             pltpu.VMEM((2, chunk, width), F32),
-            pltpu.VMEM((2 * chunk, hidden), F32),
-            pltpu.VMEM((2 * chunk, hidden), F32),
-            pltpu.VMEM((2 * chunk, hidden), BF16),
-            pltpu.VMEM((2 * chunk, width), BF16),
-            pltpu.VMEM((width, 2 * chunk), BF16),
-            pltpu.VMEM((2 * chunk, width), BF16),
-            pltpu.VMEM((2, chunk, width), BF16),
-            pltpu.VMEM((2, chunk, width), BF16),
+            pltpu.VMEM((ROW_CHUNKS, 2 * chunk, HEAD), F32),
+            pltpu.VMEM((2, ROW_CHUNKS, 2 * chunk, HEAD), F32),
             DMA((3,)),
             DMA((2,)),
             DMA((2,)),
+            DMA((5,)),
+            DMA((3,)),
+            DMA((2, 2)),
         ]
-        + [per_chunk] * 14
+        + [per_chunk] * 18
         + [DMA((3, 2)), DMA((2,)), DMA, DMA((2, 2)), DMA((2,))],
         compiler_params=pltpu.CompilerParams(
             collective_id=1, has_side_effects=True, vmem_limit_bytes=VMEM_LIMIT),
-    )(mixed, w_out, attn_gain, mlp_gain, tok, seed, w_gate, w_up, w_down)
+    )(*hbm, *vmem_args)
 
 
 def backward_kernel(
     dp_size, counts,
-    gdrt_hbm, hlt_hbm, tok_hbm, inner_hbm, mixed_hbm, gdr_hbm, gate_hbm, up_hbm, branch_hbm, seed_hbm,
+    gdrt_hbm, hlt_hbm, tok_hbm, inner_hbm, mixed_hbm, gdr_hbm, gate_hbm, up_hbm, branch_hbm, cot_hbm,
     query_hbm, key_hbm, value_hbm, query_raw_hbm, key_raw_hbm,
     w_out_hbm, wg_hbm, wu_hbm, wd_hbm, wq_hbm, wk_hbm, wv_hbm,
-    query_inv, key_inv, log_totals, seg_col, seg_row, live_col, cosine, sine,
+    inverses, log_totals, seg_live, seg_row, cosine, sine,
     query_gain, key_gain, attn_gain, gain_mlp_part,
     turned_out, straight_out, token_out, gains_out,
     ggr_hbm, gur_hbm, gbt_hbm, gh_hbm, gqkv_hbm,
@@ -665,7 +851,7 @@
         return [(b, a) for a, b in pairs] if out else pairs
 
     def sequence_rows(s, c):
-        return pl.ds(pl.multiple_of(jnp.where(core == s, 0, half) + c * chunk, chunk), chunk)
+        return pl.ds(pl.multiple_of(2 * c * chunk + jnp.where(core == s, 0, chunk), chunk), chunk)
 
     def core_copy(c, again):
         ss, rs = (cs2_sem, cr2_sem) if again else (cs_sem, cr_sem)
@@ -764,7 +950,8 @@
 
         def loads(c):
             rows = pl.ds(c * chunk, chunk)
-            return copies_of(pre_sem, (branch_hbm.at[rows], branch), (seed_hbm.at[rows], seed))
+            return copies_of(
+                pre_sem, (branch_hbm.at[rows], branch), (cot_hbm.at[sequence_rows(0, c)], seed))
 
         def stores(c):
             i = c % 2
@@ -787,7 +974,8 @@
             i = c % 2
             finish(loads(c))
             x_copy(c, False).wait()
-            grad_hidden = xs[c] + xr[c] + seed[...].astype(F32)
+            live = seg_live[sequence_rows(0, c), 1:2].astype(F32)
+            grad_hidden = xs[c] + xr[c] + seed[...].astype(F32) * live
             xs[c] = grad_hidden
             start(hidden_store(c))
             values = branch[...]
@@ -854,9 +1042,9 @@
                 key_at = lax.broadcasted_iota(jnp.int32, (keys, q_rows), 0)
                 query_at = lax.broadcasted_iota(jnp.int32, (keys, q_rows), 1) + i * q_rows
                 allowed = (
-                    (seg_col[0:keys, :] == seg_row[:, rows])
+                    (seg_live[0:keys, 0:1] == seg_row[:, rows])
                     & (key_at <= query_at)
-                    & ((live_col[0:keys, :] > 0) | (key_at == query_at)))
+                    & ((seg_live[0:keys, 1:2] > 0) | (key_at == query_at)))
                 bias[0:keys, rows] = jnp.where(allowed, 0.0, NEG_FILL)
             finish(loads)
 
@@ -880,14 +1068,15 @@
             mixed_grad[:, cols] = dv[...].astype(BF16)
 
         store_value = copies_of(st_sem, (mixed_grad, gqkv_hbm.at[:, value_cols]))
-        sides = ((dq, query_raw_hbm, query_inv, query_gain), (dk, key_raw_hbm, key_inv, key_gain))
+        sides = ((dq, query_raw_hbm, query_gain), (dk, key_raw_hbm, key_gain))
 
         def load_raw(which):
             return copies_of(pre_sem, (sides[which][1], raw))
 
         def back(which):
-            grads, _, inv, gain = sides[which]
+            grads, _, gain = sides[which]
             finish(load_raw(which))
+            gains = gain[...].astype(F32)
             lanes = lax.broadcasted_iota(jnp.int32, (q_rows, HEAD), 1)
 
             def block_back(i, carry):
@@ -896,11 +1085,12 @@
                 for h in range(heads):
                     cols = slice(h * HEAD, (h + 1) * HEAD)
                     grad = grads[rows, cols]
-                    grad = grad * cosine[rows, :] + pltpu.roll(grad, HEAD // 2, 1) * sine[rows, :]
+                    grad = grad * cosine[rows, :] - pltpu.roll(grad, HEAD // 2, 1) * sine[rows, :]
                     raw_rows = raw[rows, cols]
                     gain_cols = slice(which * head_cols + h * HEAD, which * head_cols + (h + 1) * HEAD)
-                    vec[2:3, gain_cols] += column_sum(grad * raw_rows * inv[rows, :])
-                    scaled = grad * gain[:, cols]
+                    vec[2:3, gain_cols] += column_sum(
+                        grad * raw_rows * inverses[rows, which : which + 1])
+                    scaled = grad * gains[h : h + 1, :]
                     grads[rows, cols] = scaled
                     dot = dot + jnp.sum(scaled * raw_rows, axis=1, keepdims=True)
                 if which == 0:
@@ -919,10 +1109,10 @@
             dots[...] += dots_in[i]
 
         def combine(which):
-            grads, _, inv, _ = sides[which]
+            grads = sides[which][0]
             for i in range(full // q_rows):
                 rows = slice(i * q_rows, (i + 1) * q_rows)
-                inv_rows = inv[rows, :]
+                inv_rows = inverses[rows, which : which + 1]
                 dot = dots[rows, which : which + 1]
                 mixed_grad[rows, :] = (
                     inv_rows * grads[rows, :]
@@ -1156,88 +1346,15 @@
     return results[:4]
 
 
-def times(left, right):
-    return jnp.dot(left, right, preferred_element_type=F32)
-
-
 def rope_tables():
     half_size = HEAD // 2
     freq_row = ROPE_BASE ** (-(jnp.arange(half_size, dtype=F32) * 2.0) / HEAD)
     angle = jnp.arange(LENGTH, dtype=F32)[:, None] * freq_row[None, :]
-    return (jnp.cos(angle), jnp.sin(angle))
-
-
-def rotate(values, cosine, sine_part, direction):
-    row_count, col_count = values.shape
-    half_size = HEAD // 2
-    split = values.reshape(row_count // LENGTH, LENGTH, col_count // HEAD, 2, half_size)
-    first = split[:, :, :, 0]
-    second = split[:, :, :, 1]
-    cos_b = cosine[None, :, None, :]
-    sin_b = direction * sine_part[None, :, None, :]
-    turned = jnp.stack((first * cos_b - second * sin_b, second * cos_b + first * sin_b), axis=3)
-    return turned.reshape(row_count, col_count)
-
-
-def visible_keys(begin_at, block_rows, segment_ids, live_rows):
-    seq_length = segment_ids.shape[0]
-    key_index = jnp.arange(seq_length)
-    query_index = begin_at + jnp.arange(block_rows)
-    query_segs = segment_ids[begin_at : begin_at + block_rows]
-    same_doc = query_segs[:, None] == segment_ids[None, :]
-    causal = key_index[None, :] <= query_index[:, None]
-    kept_key = (live_rows[None, :] > 0) | (key_index[None, :] == query_index[:, None])
-    return same_doc & causal & kept_key
-
-
-def block_scores(query_seq, key_heads, begin_at, block_rows, segment_ids, live_rows):
-    local_heads = key_heads.shape[1]
-    query_heads = query_seq[begin_at : begin_at + block_rows].reshape(block_rows, local_heads, HEAD)
-    scores = jnp.einsum(
-        "ihd,jhd->hij", query_heads, key_heads, preferred_element_type=F32
-    ) * HEAD ** (-0.5)
-    allowed = visible_keys(begin_at, block_rows, segment_ids, live_rows)
-    return (query_heads, jnp.where(allowed[None], scores, NEG_FILL))
-
-
-def attend_forward(query_seq, key_seq, value_seq, segment_ids, live_rows):
-    seq_length = query_seq.shape[0]
-    local_heads = query_seq.shape[1] // HEAD
-    block_rows = min(512, seq_length)
-    key_heads = key_seq.reshape(seq_length, local_heads, HEAD)
-    value_heads = value_seq.reshape(seq_length, local_heads, HEAD)
-    mixed_parts = []
-    lse_parts = []
-    for begin_at in range(0, seq_length, block_rows):
-        query_heads, scores = block_scores(
-            query_seq, key_heads, begin_at, block_rows, segment_ids, live_rows
-        )
-        row_max = jnp.max(scores, axis=-1, keepdims=True)
-        exp_scores = jnp.exp(scores - row_max)
-        row_total = jnp.sum(exp_scores, axis=-1, keepdims=True)
-        attn_prob = (exp_scores / row_total).astype(BF16)
-        mixed_block = jnp.einsum(
-            "hij,jhd->ihd", attn_prob, value_heads, preferred_element_type=F32
-        )
-        mixed_parts.append(mixed_block.reshape(block_rows, -1).astype(BF16))
-        lse_parts.append((row_max + jnp.log(row_total))[..., 0])
-    return (jnp.concatenate(mixed_parts, 0), jnp.concatenate(lse_parts, 1))
-
-
-def make_shards(dp_size, tensor_size):
-    core_pairs = [(i, i ^ 1) for i in range(tensor_size)]
-    tensor_bits = [1 << b for b in range(1, tensor_size.bit_length() - 1)]
-
-    def to_core(values):
-        return lax.ppermute(values, "tensor", core_pairs)
-
-    def wide_sum(values):
-        for bit in tensor_bits:
-            values = values + lax.ppermute(
-                values, "tensor", [(i, i ^ bit) for i in range(tensor_size)]
-            )
-        return values
-
+    cosine, sine = jnp.cos(angle), jnp.sin(angle)
+    return jnp.concatenate((cosine, cosine), 1), jnp.concatenate((-sine, sine), 1)
+
+
+def make_shards(dp_size):
     def shards(
         tokens,
         segments,
@@ -1255,40 +1372,12 @@
         gain_mlp,
         cotangent,
     ):
-        row_count, model_width = tokens.shape
-        half_rows = row_count // 2
-        block = model_width // dp_size
-        core_at = lax.axis_index("tensor") % 2
-        cosine, sine_part = rope_tables()
-
-        def split_rows(values):
-            own = lax.dynamic_slice_in_dim(values, core_at * half_rows, half_rows, 0)
-            other = lax.dynamic_slice_in_dim(values, (1 - core_at) * half_rows, half_rows, 0)
-            return own, other
-
-        query_raw = times(tokens, w_query)
-        key_raw = times(tokens, w_key)
-        value_rows = times(tokens, w_value).astype(BF16)
-        squares = jnp.stack(
-            (jnp.sum(query_raw * query_raw, axis=1), jnp.sum(key_raw * key_raw, axis=1))
-        )
-        squares = wide_sum(squares + to_core(squares))
-        query_inv = lax.rsqrt(squares[0] / model_width + EPSILON)[:, None]
-        key_inv = lax.rsqrt(squares[1] / model_width + EPSILON)[:, None]
-        query_gain = gain_query.reshape(-1).astype(F32)
-        key_gain = gain_key.reshape(-1).astype(F32)
-        query_norm = rotate(query_raw * query_inv * query_gain, cosine, sine_part, 1.0).astype(BF16)
-        key_norm = rotate(key_raw * key_inv * key_gain, cosine, sine_part, 1.0).astype(BF16)
-        mixed, log_totals = attend_forward(query_norm, key_norm, value_rows, segments, pad_mask)
-        mixed_own, mixed_other = split_rows(mixed)
-        mixed_rows = jnp.concatenate((mixed_own, mixed_other), 0)
-        tokens_own, tokens_other = split_rows(tokens)
-        cot_own, _ = split_rows(cotangent)
-        live_own, _ = split_rows(pad_mask[:, None])
-        attn_gain = gain_attn.astype(F32)
-        mlp_gain = gain_mlp.astype(F32)
-        seed = jnp.where(live_own > 0, cot_own, jnp.zeros_like(cot_own))
-
+        block = tokens.shape[1] // dp_size
+        cosine, sine = rope_tables()
+        seg_live = jnp.stack((segments, pad_mask), 1)
+        seg_row = segments[None, :]
+        attn_gain = gain_attn.astype(F32)[None, :]
+        mlp_gain = gain_mlp.astype(F32)[None, :]
         (
             gate_rows,
             up_rows,
@@ -1298,31 +1387,32 @@
             grad_down_turned,
             branch_rows,
             output,
+            query_norm,
+            key_norm,
+            value_rows,
+            query_raw,
+            key_raw,
+            mixed_rows,
             gain_mlp_part,
+            inverses,
+            log_totals,
         ) = forward_layer(
-            mixed_rows,
-            w_out,
-            attn_gain[None, :],
-            mlp_gain[None, :],
-            tokens_own,
-            seed,
-            w_gate,
-            w_up,
-            w_down,
+            (
+                tokens, cotangent, w_query, w_key, w_value, w_out, w_gate, w_up, w_down, cosine, sine,
+            ),
+            (seg_live, seg_row, gain_query, gain_key, attn_gain, mlp_gain),
         )
         turned, straight, grad_tokens, gains = backward_layer(
             dp_size,
             (
                 grad_down_turned, hidden_turned, tokens, inner_rows, mixed_rows, grad_down_rows,
-                gate_rows, up_rows, branch_rows, seed,
+                gate_rows, up_rows, branch_rows, cotangent,
                 query_norm, key_norm, value_rows, query_raw, key_raw,
                 w_out, w_gate, w_up, w_down, w_query, w_key, w_value,
             ),
             (
-                query_inv, key_inv, log_totals, segments[:, None], segments[None, :],
-                pad_mask[:, None], jnp.concatenate((cosine, cosine), 1),
-                jnp.concatenate((sine_part, -sine_part), 1),
-                query_gain[None, :], key_gain[None, :], attn_gain[None, :], gain_mlp_part,
+                inverses, log_totals, seg_live, seg_row, cosine, sine,
+                gain_query, gain_key, attn_gain, gain_mlp_part,
             ),
         )
         hidden, head_cols = w_gate.shape[1], w_query.shape[1]
@@ -1387,5 +1477,5 @@
         P("tensor", "dp"),
         P("dp"),
     )
-    shards = make_shards(mesh.shape["dp"], mesh.shape["tensor"])
+    shards = make_shards(mesh.shape["dp"])
     return jax.shard_map(shards, mesh=mesh, in_specs=in_specs, out_specs=out_specs, check_vma=False)

time: 987 us -> 945 us (0.957)
  matrix products: 27 us -> 0 us
  Pallas kernels: 886 us -> 910 us
  other arithmetic: 26.1 us -> 4.49 us
  local copies, waits for them, and re-layouts: 36.8 us -> 21.9 us
    dot_general x7 -> x0, matrix products: 27 us -> none  [the longest x3 15.4 us: times(): return jnp.dot(left, right, preferred_element_type=F32)]
    pallas_call x1, Pallas kernels: 196 us -> 217 us  [forward_layer(): pl.pallas_call(forward_kernel, out_shape=(shape(row_count, hidden), shape...]
  transfers between devices with their start and end apart: 2 -> 0, of which waited for: 0 -> 0; matrix products, arithmetic and copies ran while one was open for 3% -> 0% of each run, Pallas kernels for 0% -> 0%
where the time goes in v4:
time: 945 us; the launch traced here: 937 us
  Pallas kernels  910 us (96%)
  local copies, waits for them, and re-layouts  21.9 us (2%)
    pallas_call x1, Pallas kernels, backward_layer(): pl.pallas_call(functools.partial(backward_kernel, dp_size, counts), out_s...  693 us
    pallas_call x1, Pallas kernels, forward_layer(): pl.pallas_call(forward_kernel, out_shape=(shape(row_count, hidden), shape...  217 us

profile of v4, /device:TPU:0, one launch (start us, length us, event | category | flops | bytes accessed | tf_op | source)
XLA Modules:
  0.0 937.3 jit_solution(10820671211766885896)
XLA Ops:
  0.6 0.0 copy-start.6
  0.7 0.0 copy-start.3
  0.7 0.0 copy-start.4
  0.7 0.0 copy-start.5
  0.7 2.0 fusion.2
  2.7 1.3 pad_maximum_fusion
  4.0 0.0 copy-done.6
  4.0 0.0 copy-done.3
  4.0 1.0 copy.30.seg_live
  5.0 0.0 copy-done.4
  5.0 0.6 broadcast_in_dim.20
  5.6 0.0 copy-done.5
  5.6 0.6 broadcast_in_dim.21
  6.2 216.6 %shard_map.246 = (f32[1024,2048]{1,0:T(8,128)}, f32[1024,2048]{1,0:T(8,128)}, bf16[1024,2048]{1,0:T(8,128)(2,1)}, bf16[2048,1024]{1,0:T(8,128)(2,1)}, bf16[1024,...) custom-call(bf16[1024,2048]{1,0:T(8,128)(2,1)} %tok_hbm.3, ...), custom_call_target="tpu_custom_call" | custom-call | tf_op jit(solution)/shard_map/pallas_call | solution.py:480
  222.8 693.4 %shard_map.247 = (f32[2560,256]{1,0:T(8,128)}, f32[256,5632]{1,0:T(8,128)}, bf16[1024,2048]{1,0:T(8,128)(2,1)}, f32[8,2048]{1,0:T(8,128)}, bf16[1024,2048]{1,0:T...) custom-call(bf16[2048,1024]{1,0:T(8,128)(2,1)} %get-tuple-element.35, ...), custom_call_target="tpu_custom_call" | custom-call | tf_op jit(solution)/shard_map/pallas_call | solution.py:1299
  916.2 2.5 fusion.4
  918.7 1.9 slice.42
  920.6 0.8 slice.43
  921.3 0.1 constant_dynamic-slice_fusion.1
  921.4 0.6 fusion.5
  922.0 0.8 slice.46
  922.8 0.6 constant_dynamic-slice_fusion
  923.5 0.0 copy-start.2
  923.5 4.9 fusion.3
  928.4 0.0 copy-start
  928.4 0.0 copy-done.2
  928.4 1.5 slice.50
  929.8 1.5 copy-done
  931.3 0.0 copy-start.1
  931.3 2.1 copy.34
  933.4 1.6 copy-done.1
  935.0 2.0 copy.35
  (2 shorter events, 0.0 us)
Async XLA Ops:
  0.6 3.3 copy-start.6
  0.7 3.3 copy-start.3
  0.7 4.4 copy-start.4
  0.7 5.0 copy-start.5
  923.5 4.9 copy-start.2
  928.4 2.9 copy-start
  931.3 3.7 copy-start.1

commit v5 on v4

--- a/solution.py
+++ b/solution.py
@@ -18,21 +18,22 @@
 
 
 COLS = 256
-SPAN = 6
+LINE_FIRST = (1, 23)
 Y_SLOTS = 3
-B_SLOTS = 5
+B_SLOTS = 3
 FEED_TICK = 3
 HIDDEN_TICK = 7
 BRANCH_TICK = 12
-INPUT_TICK = 21
-TOKEN_TICK = 26
+INPUT_TICK = 20
+TOKEN_TICK = 25
 HBM_NAMES = (
     "gdrt", "hlt", "tokens", "inner", "mixed", "gdr", "gate", "up", "branch", "cotangent",
-    "query", "key", "value", "query_raw", "key_raw",
+    "query", "key", "value", "query_raw", "key_raw", "partner",
+    "inverses", "seg_live", "cosine", "sine",
     "w_out", "w_gate", "w_up", "w_down", "w_query", "w_key", "w_value",
 )
 TILE = 512
-VMEM_LIMIT = 63 * 1024 * 1024
+VMEM_LIMIT = 65400 * 1024
 MESH = pl.DeviceIdType.MESH
 
 def column_sum(values):
@@ -60,14 +61,16 @@
     tok_hbm, cot_hbm, wq_hbm, wk_hbm, wv_hbm, wo_hbm, wg_hbm, wu_hbm, wd_hbm, cos_hbm, sin_hbm,
     seg_live, seg_row, query_gain, key_gain, attn_gain, mlp_gain,
     gate_out, up_out, inner_out, hlt_out, gdr_out, gdrt_out, branch_out, out_out,
-    query_out, key_out, value_out, query_raw_out, key_raw_out, mixed_out,
+    query_out, key_out, value_out, query_raw_out, key_raw_out, mixed_out, partner_out,
     gain_out, inverse_out, log_out,
     wg, wu, cs, crecv, xs, xr, xr2, ag, squares, squares_in,
     w_sem, t_sem, s_sem, a_sem, r_sem, m_sem, sq_s_sem, sq_r_sem, sx_s_sem, sx_r_sem,
     cs_sem, cr_sem, xs_sem, xr_sem, as_sem, ar_sem, cs2_sem, cr2_sem, xs2_sem, xr2_sem,
-    gs_sem, gr_sem, os_sem, or_sem, g_sem, h_sem, b_sem, d_sem, o_sem,
+    gs_sem, gr_sem, os_sem, or_sem, hs_sem, hr_sem, fs_sem, fr_sem, g_sem, h_sem, b_sem, d_sem, o_sem,
 ):
     core, sibling, across = tensor_peers()
+    dp_at = lax.axis_index("dp")
+    partner = dp_at + 1 - 2 * lax.rem(dp_at, 2)
     chunk = xs.shape[1]
     half = chunk * ROW_CHUNKS
     full = 2 * half
@@ -104,6 +107,16 @@
             src_ref=src, dst_ref=dst, send_sem=send_sem, recv_sem=recv_sem,
             device_id={"tensor": peer}, device_id_type=MESH)
 
+    def partner_copy(c):
+        return pltpu.make_async_remote_copy(
+            src_ref=xr.at[c], dst_ref=partner_out.at[rows(c * chunk)], send_sem=hs_sem.at[c],
+            recv_sem=hr_sem.at[c], device_id={"dp": partner}, device_id_type=MESH)
+
+    def hand_copy(c):
+        return remote(
+            partner_out.at[rows(c * chunk)], partner_out.at[rows(half + c * chunk)],
+            fs_sem.at[c], fr_sem.at[c], sibling)
+
     def core_copy(c):
         return remote(cs.at[c % 2], crecv.at[c], cs_sem.at[c], cr_sem.at[c], sibling)
 
@@ -167,7 +180,7 @@
         tok_load(0).start()
         start(loads)
         tok_load(1).start()
-        greet({"tensor": sibling}, {"tensor": across})
+        greet({"tensor": sibling}, {"tensor": across}, {"dp": partner})
         lanes = lax.broadcasted_iota(jnp.int32, (both, HEAD), 1)
         for c in range(ROW_CHUNKS):
             at = slice(c * both, (c + 1) * both)
@@ -298,7 +311,7 @@
     pl.run_scoped(
         functools.partial(
             feed_forward, core, chunk, own_rows, row_load, rows, side_copies, turned_copies,
-            (x_copy, hidden_copy, core2_copy, x2_copy, grad_copy, out_copy), wide_loads, seg_live,
+            (x_copy, hidden_copy, core2_copy, x2_copy, grad_copy, out_copy, partner_copy, hand_copy), wide_loads, seg_live,
             (tok_hbm, cot_hbm, wd_hbm, attn_gain, mlp_gain, wg, wu),
             (gate_out, up_out, inner_out, hlt_out, gdr_out, gdrt_out, branch_out, out_out, gain_out),
             (cs, crecv, xs, xr, xr2, ag),
@@ -314,7 +327,7 @@
     operands, results, buffers, sems,
     wd, gate_buf, up_buf, inner_buf, low_buf, hlt_buf, out_buf, tok, seed,
 ):
-    x_copy, hidden_copy, core2_copy, x2_copy, grad_copy, out_copy = remote_copies
+    x_copy, hidden_copy, core2_copy, x2_copy, grad_copy, out_copy, partner_copy, hand_copy = remote_copies
     tok_hbm, cot_hbm, wd_hbm, attn_gain, mlp_gain, wg, wu = operands
     gate_out, up_out, inner_out, hlt_out, gdr_out, gdrt_out, branch_out, out_out, gain_out = results
     cs, crecv, xs, xr, xr2, ag = buffers
@@ -326,6 +339,10 @@
     for c in range(2):
         row_load(c, tok_hbm, tok, t_sem).start()
         row_load(c, cot_hbm, seed, s_sem).start()
+
+    def hand_on(c):
+        partner_copy(c).wait_recv()
+        hand_copy(c).start()
 
     def feed(c):
         x_copy(c).wait()
@@ -339,6 +356,7 @@
             row_load(c + 2, tok_hbm, tok, t_sem).start()
         xr[c] = hidden
         hidden_copy(c).start()
+        partner_copy(c).start()
         low_buf[0:chunk, :] = hidden.astype(BF16)
         if c >= 1:
             for copy in turned_copies(hlt_buf, hlt_out, h_sem, c - 1):
@@ -385,6 +403,8 @@
         core2_copy(c).wait_recv()
         xs[c] += crecv[c]
         x2_copy(c).start()
+        if c >= 1:
+            hand_on(c - 1)
 
     def finish(c, gain_total):
         x2_copy(c).wait()
@@ -400,6 +420,7 @@
         dot = jnp.sum(scaled * down, axis=1, keepdims=True)
         grad = inv * scaled - down * (inv * inv * inv * dot / down.shape[1])
         hidden_copy(c).wait_send()
+        partner_copy(c).wait_send()
         xr2[c] = grad
         grad_copy(c).start()
         xr[c] = xr[c] + normed * mlp_gain[...]
@@ -447,6 +468,8 @@
         gain_total = finish(c, gain_total)
         if c >= 1:
             place(c - 1)
+        if c == 1:
+            hand_on(last)
     place(last)
     gain_out[...] = gain_total
     for buf, dst, i in ((gate_buf, gate_out, 0), (up_buf, up_out, 1), (inner_buf, inner_out, 2)):
@@ -463,6 +486,7 @@
     for c in range(ROW_CHUNKS):
         grad_copy(c).wait_send()
         out_copy(c).wait_send()
+        hand_copy(c).wait()
 
 
 def forward_layer(hbm, vmem_args):
@@ -494,12 +518,13 @@
             shape(row_count, head_cols),
             shape(row_count, head_cols),
             shape(row_count, head_cols, kind=BF16),
+            shape(row_count, width),
             shape(1, width),
             shape(row_count, HEAD),
             shape(head_cols // HEAD, row_count),
         ),
         in_specs=[any_space] * len(hbm) + [vmem] * len(vmem_args),
-        out_specs=(any_space,) * 14 + (vmem,) * 3,
+        out_specs=(any_space,) * 15 + (vmem,) * 3,
         scratch_shapes=[
             pltpu.VMEM(w_gate.shape, BF16),
             pltpu.VMEM(w_gate.shape, BF16),
@@ -518,7 +543,7 @@
             DMA((3,)),
             DMA((2, 2)),
         ]
-        + [per_chunk] * 18
+        + [per_chunk] * 22
         + [DMA((3, 2)), DMA((2,)), DMA, DMA((2, 2)), DMA((2,))],
         compiler_params=pltpu.CompilerParams(
             collective_id=1, has_side_effects=True, vmem_limit_bytes=VMEM_LIMIT),
@@ -528,21 +553,22 @@
 def backward_kernel(
     dp_size, counts,
     gdrt_hbm, hlt_hbm, tok_hbm, inner_hbm, mixed_hbm, gdr_hbm, gate_hbm, up_hbm, branch_hbm, cot_hbm,
-    query_hbm, key_hbm, value_hbm, query_raw_hbm, key_raw_hbm,
+    query_hbm, key_hbm, value_hbm, query_raw_hbm, key_raw_hbm, partner_hbm,
+    inverses_hbm, seg_live_hbm, cos_hbm, sin_hbm,
     w_out_hbm, wg_hbm, wu_hbm, wd_hbm, wq_hbm, wk_hbm, wv_hbm,
-    inverses, log_totals, seg_live, seg_row, cosine, sine,
+    log_totals, seg_row,
     query_gain, key_gain, attn_gain, gain_mlp_part,
-    turned_out, straight_out, token_out, gains_out,
+    down_out, out_out, gate_out, up_out, query_out, key_out, value_out, token_out, gains_out,
     ggr_hbm, gur_hbm, gbt_hbm, gh_hbm, gqkv_hbm,
-    at, bbuf, ysend, yrecv, zsend, zrecv, stage, stage_t, cs, crecv, xs, xr, ag, dots, dots_in,
+    at, bbuf, bsend, bpar, own, ysend, yrecv, fsend, frecv, zsend, zrecv, stage, stage_t, cs, crecv, xs, xr, ag, dots, dots_in,
     vec, vec_in,
-    at_sem, b_sem, ys_sem, yr_sem, zs_sem, zr_sem, out_sem,
+    at_sem, b_sem, bs_sem, ys_sem, yr_sem, fs_sem, fr_sem, zs_sem, zr_sem, out_sem, far_sem,
     cs_sem, cr_sem, xs_sem, xr_sem, as_sem, ar_sem, cs2_sem, cr2_sem, xs2_sem, xr2_sem, as2_sem,
-    ar2_sem, ds_sem, dr_sem, vs_sem, vr_sem, w_sem, pre_sem, st_sem, gh_sem, tok_sem,
+    ar2_sem, ds_sem, dr_sem, vs_sem, vr_sem, w_sem, pre_sem, st_sem, gh_sem, tok_sem, live_sem,
     y_credit, up_credit, down_credit,
 ):
-    n_down, n_hidden, n_heads, n_out = counts
-    first_heads = n_down + n_hidden
+    n_down, n_pairs, n_heads, n_out = counts
+    first_heads = n_down + n_pairs
     first_out = first_heads + n_heads
     total = first_out + n_out
     line = dp_size // 2
@@ -552,7 +578,7 @@
     half = chunk * ROW_CHUNKS
     full = 2 * half
     head_cols = query_hbm.shape[1]
-    passes = total + total // SPAN
+    passes = total + n_pairs + len(LINE_FIRST)
     dp_at = lax.axis_index("dp")
     z, y = dp_at // 2, dp_at % 2
     partner = dp_at + 1 - 2 * y
@@ -568,23 +594,6 @@
     def at_tensor(i):
         return {"tensor": i}
 
-    barrier = pltpu.get_barrier_semaphore()
-
-    def greet_one(peer):
-        pl.semaphore_signal(barrier, inc=1, device_id=peer, device_id_type=MESH)
-
-    other_z = z - 1 + 2 * lax.rem(z, 2)
-    has_other = (other_z >= 0) & (other_z < line)
-    for peer in vec_peers:
-        greet_one(at_dp(peer))
-    greet_one(at_tensor(sibling))
-    greet_one(at_tensor(across))
-
-    @pl.when(has_other)
-    def _():
-        greet_one(at_dp(2 * other_z + y))
-    pl.semaphore_wait(barrier, len(steps) + 2 + has_other.astype(jnp.int32))
-
     def remote(src, dst, send_sem, recv_sem, peer):
         return pltpu.make_async_remote_copy(
             src_ref=src, dst_ref=dst, send_sem=send_sem, recv_sem=recv_sem,
@@ -596,50 +605,59 @@
     def z_copy(p, b, slot, target):
         return remote(zsend.at[p, b], zrecv.at[p, slot], zs_sem.at[p, b], zr_sem.at[p, slot], at_dp(target))
 
-    def group_of(k):
-        return (
-            (k >= n_down).astype(jnp.int32)
-            + (k >= first_heads).astype(jnp.int32)
-            + (k >= first_out).astype(jnp.int32))
+    def final_copy(p):
+        return remote(fsend.at[p], frecv.at[p], fs_sem.at[p], fr_sem.at[p], at_dp(partner))
+
+    def is_pair(k):
+        return (k >= n_down) & (k < first_heads)
+
+    def slot_of(k):
+        return lax.rem(
+            (k >= n_down).astype(jnp.int32) + (k >= first_heads).astype(jnp.int32)
+            + (k >= first_out).astype(jnp.int32), 2)
+
+    def row_block(rows_at):
+        return pl.ds(pl.multiple_of(rows_at * block, block), block)
 
     def product(k, rows_at):
         return jnp.dot(
-            at[lax.rem(group_of(k), 2), pl.ds(pl.multiple_of(rows_at * block, block), block), :],
-            bbuf[lax.rem(k, B_SLOTS)], preferred_element_type=F32)
+            at[slot_of(k), row_block(rows_at), :], bbuf[lax.rem(k, B_SLOTS)],
+            preferred_element_type=F32)
+
+    def pair_product(k, rows_at):
+        return product(k, rows_at) + jnp.dot(
+            at[2, row_block(rows_at), :], bpar[...], preferred_element_type=F32)
 
     def at_load(i):
         src = (gdrt_hbm, hlt_hbm, None, gbt_hbm)[i]
         return pltpu.make_async_copy(src, at.at[i % 2], at_sem.at[i % 2])
 
     def b_load(k, act):
-        def columns(src, at_chunk):
+        def columns(src, at_chunk, dst, sem):
             act(pltpu.make_async_copy(
-                src.at[:, pl.ds(pl.multiple_of(at_chunk * COLS, COLS), COLS)],
-                bbuf.at[lax.rem(k, B_SLOTS)], b_sem.at[lax.rem(k, B_SLOTS)]))
-        per = n_hidden // 2
+                src.at[:, pl.ds(pl.multiple_of(at_chunk * COLS, COLS), COLS)], dst, sem))
+        own_dst, own_sem = bbuf.at[lax.rem(k, B_SLOTS)], b_sem.at[lax.rem(k, B_SLOTS)]
 
         @pl.when(k < n_down)
         def _():
-            columns(inner_hbm, k)
-
-        @pl.when((k >= n_down) & (k < n_down + per))
-        def _():
-            columns(ggr_hbm, k - n_down)
-
-        @pl.when((k >= n_down + per) & (k < first_heads))
-        def _():
-            columns(gur_hbm, k - n_down - per)
+            columns(inner_hbm, k, own_dst, own_sem)
+
+        for first, src in ((n_down, ggr_hbm), (n_down + n_pairs // 2, gur_hbm)):
+            @pl.when((k >= first) & (k < first + n_pairs // 2))
+            def _(first=first, src=src):
+                columns(src, 2 * (k - first) + y, own_dst, own_sem)
+                columns(src, 2 * (k - first) + 1 - y, bsend, bs_sem)
 
         @pl.when((k >= first_heads) & (k < first_out))
         def _():
-            columns(gqkv_hbm, k - first_heads)
+            columns(gqkv_hbm, k - first_heads, own_dst, own_sem)
 
         @pl.when((k >= first_out) & (k < total))
         def _():
-            columns(mixed_hbm, k - first_out)
+            columns(mixed_hbm, k - first_out, own_dst, own_sem)
 
     def line_first(k):
-        return lax.rem(k, SPAN) == SPAN - 1
+        return functools.reduce(jnp.logical_or, [k == at_chunk for at_chunk in LINE_FIRST])
 
     def walk(fn):
         def body(i, carry):
@@ -661,13 +679,21 @@
             pl.semaphore_wait(y_credit, 1)
         b_load(k, lambda copy: copy.wait())
 
-        @pl.when(jnp.logical_not(line_first(k)))
+        @pl.when(jnp.logical_not(line_first(k) | is_pair(k)))
         def _():
             def one(b, up=None):
                 ysend[p, b] = product(k, 2 * b + 1 - y)
                 y_copy(p, b).start()
             walk(one)
             one(z)
+
+        @pl.when(is_pair(k))
+        def _():
+            def rows_out(b, carry):
+                ysend[p, b] = bsend[row_block(b), :].astype(F32)
+                y_copy(p, b).start()
+                return carry
+            lax.fori_loop(0, line, rows_out, 0)
 
     def line_send(q, k, source):
         p = lax.rem(q, 2)
@@ -732,17 +758,41 @@
     def is_turned(k):
         return (k < n_down) | (k >= first_out)
 
+    per_head = n_heads // 3
+    results = (
+        (0, n_down, down_out, True),
+        (first_heads, per_head, query_out, False),
+        (first_heads + per_head, per_head, key_out, False),
+        (first_heads + 2 * per_head, per_head, value_out, False),
+        (first_out, n_out, out_out, True),
+    )
+    pair_results = ((n_down, gate_out), (n_down + n_pairs // 2, up_out))
+
     def out_act(k, act):
-        @pl.when(is_turned(k))
-        def _():
-            first = jnp.where(k < n_down, k, k - first_out + n_down) * COLS
-            act(pltpu.make_async_copy(
-                stage_t, turned_out.at[pl.ds(pl.multiple_of(first, COLS), COLS)], out_sem))
-
-        @pl.when(jnp.logical_not(is_turned(k)))
-        def _():
-            cols = pl.ds(pl.multiple_of((k - n_down) * COLS, COLS), COLS)
-            act(pltpu.make_async_copy(stage, straight_out.at[:, cols], out_sem))
+        def place(at_chunk):
+            return pl.ds(pl.multiple_of(at_chunk * COLS, COLS), COLS)
+
+        for first, count, dst, turned in results:
+            @pl.when((k >= first) & (k < first + count))
+            def _(first=first, dst=dst, turned=turned):
+                if turned:
+                    act(pltpu.make_async_copy(stage_t, dst.at[place(k - first)], out_sem))
+                else:
+                    act(pltpu.make_async_copy(stage, dst.at[:, place(k - first)], out_sem))
+
+        for first, dst in pair_results:
+            @pl.when((k >= first) & (k < first + n_pairs // 2))
+            def _(first=first, dst=dst):
+                act(pltpu.make_async_copy(stage, dst.at[:, place(2 * (k - first) + y)], out_sem))
+
+    def far_out(k):
+        for first, dst in pair_results:
+            @pl.when((k >= first) & (k < first + n_pairs // 2))
+            def _(first=first, dst=dst):
+                cols = pl.ds(pl.multiple_of((2 * (k - first) + 1 - y) * COLS, COLS), COLS)
+                copy = pltpu.make_async_copy(frecv.at[lax.rem(k, Y_SLOTS)], dst.at[:, cols], far_sem)
+                copy.start()
+                copy.wait()
 
     def finish_chunk(k, q):
         p = lax.rem(k, Y_SLOTS)
@@ -750,12 +800,15 @@
         @pl.when(k >= 1)
         def _():
             out_act(k - 1, lambda copy: copy.wait())
-        stage[...] = product(k, 2 * z + y)
-        y_copy(p, z).wait_recv()
-        stage[...] += yrecv[p, z]
+        stage[...] = own[...]
+
+        @pl.when(jnp.logical_not(is_pair(k)))
+        def _():
+            y_copy(p, z).wait_recv()
+            stage[...] += yrecv[p, z]
         line_own(q, stage)
 
-        @pl.when(is_turned(k))
+        @pl.when((k < n_down) | (k >= first_out))
         def _():
             stage_t[...] = stage[...].T
         out_act(k, lambda copy: copy.start())
@@ -769,14 +822,35 @@
             for b in range(line):
                 y_copy(p, b).wait_send()
 
+        @pl.when(is_pair(k))
+        def _():
+            final_copy(p).wait()
+            far_out(k)
+
         @pl.when(k < total - Y_SLOTS)
         def _():
             pl.semaphore_signal(y_credit, inc=1, device_id=at_dp(partner), device_id_type=MESH)
+
+    def pass_of(k):
+        return (
+            k + jnp.clip(k - n_down, 0, n_pairs)
+            + sum((k > at_chunk).astype(jnp.int32) for at_chunk in LINE_FIRST))
+
+    def prefetch(k):
+        @pl.when(k + 2 < total)
+        def _():
+            b_load(k + 2, lambda copy: copy.start())
+
+    def send_ahead(k):
+        @pl.when(k + 2 < total)
+        def _():
+            pair_send(k + 2)
 
     def tick(k):
         p = lax.rem(k, Y_SLOTS)
-        q = k + k // SPAN
+        q = pass_of(k)
         is_line_first = line_first(k)
+        prefetch(k)
 
         @pl.when(jnp.logical_not(is_line_first))
         def _():
@@ -793,6 +867,7 @@
         @pl.when(k >= 1)
         def _():
             finish_chunk(k - 1, q - 1)
+        own[...] = product(k, 2 * z + y)
 
         @pl.when(is_line_first)
         def _():
@@ -800,14 +875,27 @@
             ysend[p, z] = product(k, 2 * z + 1 - y)
             line_own(q, ysend.at[p, z])
             y_copy(p, z).start()
-
-        @pl.when(k + 2 < total)
-        def _():
-            pair_send(k + 2)
-
-        @pl.when(k + 3 < total)
-        def _():
-            b_load(k + 3, lambda copy: copy.start())
+        send_ahead(k)
+
+    def pair_tick(k, work):
+        p = lax.rem(k, Y_SLOTS)
+        q = pass_of(k)
+        prefetch(k)
+
+        def rows_in(b, carry):
+            y_copy(p, b).wait_recv()
+            bpar[row_block(b), :] = yrecv[p, b].astype(BF16)
+            return carry
+        lax.fori_loop(0, line, rows_in, 0)
+        line_send(q, k, lambda b: pair_product(k, 2 * b + 1 - y))
+        finish_chunk(k - 1, q - 1)
+        work(q)
+        line_send(q + 1, k, lambda b: pair_product(k, 2 * b + y))
+        own[...] = pair_product(k, 2 * z + y)
+        fsend[p] = pair_product(k, 2 * z + 1 - y)
+        line_own(q, fsend.at[p])
+        final_copy(p).start()
+        send_ahead(k)
 
     nt = (((1,), (1,)), ((), ()))
 
@@ -822,23 +910,41 @@
         for copy in copies:
             copy.wait()
 
+    first_pair, last_pair = n_down, n_down + 2 * n_pairs
+
     def run_ticks(first, last, work):
-        def body(k, carry):
-            tick(k)
+        def do_work(at_half):
             for when, fn in work.items():
                 low, high = when if isinstance(when, tuple) else (when, when + 1)
 
-                @pl.when((k >= low) & (k < high))
-                def _(fn=fn, low=low):
+                @pl.when((at_half >= low) & (at_half < high))
+                def _(fn=fn, low=low, high=high):
                     if isinstance(fn, list):
                         for one in fn:
                             one()
                     elif low + 1 == high:
                         fn()
                     else:
-                        fn(k - low)
+                        fn(at_half - low)
+
+        def single(at_half, carry):
+            k = jnp.where(at_half < first_pair, at_half, at_half - n_pairs)
+            tick(k)
+            do_work(at_half)
             return carry
-        lax.fori_loop(first, last, body, 0)
+
+        def double(m, carry):
+            at_half = first_pair + 2 * m
+            pair_tick(first_pair + m, lambda q: do_work(at_half))
+            do_work(at_half + 1)
+            return carry
+        if first < first_pair:
+            lax.fori_loop(first, min(last, first_pair), single, 0)
+        low, high = max(first, first_pair), min(last, last_pair)
+        if low < high:
+            lax.fori_loop((low - first_pair) // 2, (high - first_pair) // 2, double, 0)
+        if last > last_pair:
+            lax.fori_loop(max(first, last_pair), last, single, 0)
 
     def part(fn, *args):
         return functools.partial(fn, *args)
@@ -855,7 +961,7 @@
 
     def core_copy(c, again):
         ss, rs = (cs2_sem, cr2_sem) if again else (cs_sem, cr_sem)
-        return remote(cs.at[c % 2], crecv.at[c], ss.at[c], rs.at[c], at_tensor(sibling))
+        return remote(cs, crecv.at[c], ss.at[c], rs.at[c], at_tensor(sibling))
 
     def x_copy(c, again):
         ss, rs = (xs2_sem, xr2_sem) if again else (xs_sem, xr_sem)
@@ -873,7 +979,19 @@
 
     hidden = wd_hbm.shape[0]
 
-    def feed_phase(wd, grads, gates, ups, ggr, gur):
+    def feed_phase(wd, grads, gates, ups, ggr, gur, far_rows):
+        far_piece = full // ROW_CHUNKS
+
+        def far_load(c):
+            return copies_of(
+                tok_sem, (partner_hbm.at[pl.ds(c * far_piece, far_piece)], far_rows))
+
+        def far_turn(c):
+            finish(far_load(c))
+            at[2, :, pl.ds(c * far_piece, far_piece)] = far_rows[...].astype(BF16).T
+            if c + 1 < ROW_CHUNKS:
+                start(far_load(c + 1))
+
         def loads(c):
             return copies_of(
                 pre_sem, *both_sides(gdr_hbm, grads, c), *both_sides(gate_hbm, gates, c),
@@ -905,12 +1023,15 @@
         load_weight = copies_of(w_sem, (wd_hbm, wd))
         start(load_weight)
         start(loads(0))
+        start(far_load(0))
         at_load(0).wait()
         pair_send(jnp.int32(0))
         pair_send(jnp.int32(1))
         finish(load_weight)
         piece(0)
-        run_ticks(0, FEED_TICK, {c - 1: part(piece, c) for c in range(1, ROW_CHUNKS)})
+        far_turn(0)
+        run_ticks(0, FEED_TICK, {
+            c - 1: [part(piece, c), part(far_turn, c)] for c in range(1, ROW_CHUNKS)})
         finish(stores(ROW_CHUNKS - 1))
 
     def hidden_phase(weights, ggr, gur):
@@ -932,7 +1053,7 @@
                 total_part = total_part + lax.dot_general(
                     gur[...], weights[1, rows, :], nt, preferred_element_type=F32)
                 xs[c, :, rows] = total_part[0:chunk]
-                cs[c % 2, :, rows] = total_part[chunk : 2 * chunk]
+                cs[:, rows] = total_part[chunk : 2 * chunk]
                 return carry
             lax.fori_loop(0, width // TILE, tile, 0)
             core_copy(c, False).start()
@@ -944,8 +1065,9 @@
         run_ticks(
             FEED_TICK, HIDDEN_TICK, {FEED_TICK + c: part(piece, c) for c in range(ROW_CHUNKS)})
 
-    def branch_phase(branch, seed, low, turned, w_out, mixed_grad, token_rows):
+    def branch_phase(branch, seed, low, turned, w_out, mixed_grad, token_rows, seg_live):
         load_weight = copies_of(w_sem, (w_out_hbm, w_out))
+        load_live = copies_of(live_sem, (seg_live_hbm, seg_live))
         token_piece = full // ROW_CHUNKS
 
         def loads(c):
@@ -973,6 +1095,8 @@
         def first(c):
             i = c % 2
             finish(loads(c))
+            if c == 0:
+                finish(load_live)
             x_copy(c, False).wait()
             live = seg_live[sequence_rows(0, c), 1:2].astype(F32)
             grad_hidden = xs[c] + xr[c] + seed[...].astype(F32) * live
@@ -1014,6 +1138,7 @@
                 start(token_load(c + 1))
 
         start(load_weight)
+        start(load_live)
         start(loads(0))
         start(token_load(0))
         work = {HIDDEN_TICK + c: [] for c in range(ROW_CHUNKS + 1)}
@@ -1027,7 +1152,9 @@
         for c in range(ROW_CHUNKS - 2, ROW_CHUNKS):
             finish(stores(c))
 
-    def attention_phase(query, key, value, mixed_grad, dq, dk, dv, raw, bias):
+    def attention_phase(
+        query, key, value, mixed_grad, dq, dk, dv, raw, bias, inverses, seg_live, cosine, sine,
+    ):
         heads = head_cols // HEAD
         q_rows = min(256, full)
         scale = HEAD ** (-0.5)
@@ -1035,8 +1162,11 @@
         loads = copies_of(
             pre_sem, (query_hbm, query), (key_hbm, key), (value_hbm, value),
             (gqkv_hbm.at[:, value_cols], mixed_grad))
+        load_tables = copies_of(
+            w_sem, (inverses_hbm, inverses), (seg_live_hbm, seg_live), (cos_hbm, cosine), (sin_hbm, sine))
 
         def masks():
+            finish(load_tables)
             for i in range(full // q_rows):
                 rows, keys = slice(i * q_rows, (i + 1) * q_rows), (i + 1) * q_rows
                 key_at = lax.broadcasted_iota(jnp.int32, (keys, q_rows), 0)
@@ -1045,7 +1175,7 @@
                     (seg_live[0:keys, 0:1] == seg_row[:, rows])
                     & (key_at <= query_at)
                     & ((seg_live[0:keys, 1:2] > 0) | (key_at == query_at)))
-                bias[0:keys, rows] = jnp.where(allowed, 0.0, NEG_FILL)
+                bias[0:keys, rows] = jnp.where(allowed, 0.0, NEG_FILL).astype(BF16)
             finish(loads)
 
         def head(h):
@@ -1057,7 +1187,7 @@
                 q_block, grad_block = query[rows, cols], mixed_grad[rows, cols]
                 key_block, value_block = key[0:keys, cols], value[0:keys, cols]
                 scores = lax.dot_general(key_block, q_block, nt, preferred_element_type=F32) * scale
-                prob = jnp.exp(scores + bias[0:keys, rows] - log_totals[pl.ds(h, 1), rows])
+                prob = jnp.exp(scores + bias[0:keys, rows].astype(F32) - log_totals[pl.ds(h, 1), rows])
                 grad_prob = lax.dot_general(value_block, grad_block, nt, preferred_element_type=F32)
                 row_dot = jnp.sum(prob * grad_prob, axis=0, keepdims=True)
                 grad_scores = (prob * (grad_prob - row_dot)).astype(BF16)
@@ -1153,15 +1283,16 @@
             start(store_grads(0))
 
         start(loads)
+        start(load_tables)
         t = BRANCH_TICK
         run_ticks(t, INPUT_TICK, {
             t: masks,
-            (t + 1, t + 1 + heads): head,
-            t + heads: after_heads,
-            t + heads + 1: back_query,
-            t + heads + 2: back_key,
-            t + heads + 3: first_sum,
-            t + heads + 4: [second_sum, last_part],
+            (t, t + heads): head,
+            t + heads - 1: after_heads,
+            t + heads: back_query,
+            t + heads + 1: back_key,
+            t + heads + 2: first_sum,
+            t + heads + 3: [second_sum, last_part],
         })
         finish(store_grads(0))
 
@@ -1188,7 +1319,7 @@
                     if s == 0:
                         xs[c, :, cols] = total_part
                     else:
-                        cs[c % 2, :, cols] = total_part
+                        cs[:, cols] = total_part
                     return carry
                 lax.fori_loop(0, width // TILE, tile, 0)
             core_copy(c, True).start()
@@ -1234,7 +1365,8 @@
 
         start(loads)
         start(hidden_load(0))
-        work = {k: [] for k in range(INPUT_TICK, total)}
+        halves = total + n_pairs
+        work = {k: [] for k in range(INPUT_TICK, halves)}
         for c in range(ROW_CHUNKS):
             work[INPUT_TICK + c].append(part(piece, c))
             work[TOKEN_TICK + c].append(part(first, c))
@@ -1242,23 +1374,41 @@
         work[INPUT_TICK + ROW_CHUNKS].append(part(pass_on, ROW_CHUNKS - 1, True))
         for i in range(len(vec_peer_ids) + 1):
             work[INPUT_TICK + 2 + i].append(part(vec_step, i))
-        work[first_heads + 1].append(lambda: at_load(3).start())
-        work[first_heads + 2].append(lambda: at_load(3).wait())
-        run_ticks(INPUT_TICK, total, {k: fns for k, fns in work.items() if fns})
+        work[last_pair + 1].append(lambda: at_load(3).start())
+        work[last_pair + 2].append(lambda: at_load(3).wait())
+        run_ticks(INPUT_TICK, halves, {k: fns for k, fns in work.items() if fns})
         finish(stores(ROW_CHUNKS - 1))
 
     vec[...] = jnp.zeros(vec.shape, F32)
     vec[0:1, :] = gain_mlp_part[...]
     at_load(0).start()
     at_load(1).start()
-    for k in range(3):
+    for k in range(2):
         b_load(jnp.int32(k), lambda copy: copy.start())
+    barrier = pltpu.get_barrier_semaphore()
+
+    def greet_one(peer):
+        pl.semaphore_signal(barrier, inc=1, device_id=peer, device_id_type=MESH)
+
+    other_z = z - 1 + 2 * lax.rem(z, 2)
+    has_other = (other_z >= 0) & (other_z < line)
+    for peer in vec_peers:
+        greet_one(at_dp(peer))
+    greet_one(at_tensor(sibling))
+    greet_one(at_tensor(across))
+
+    @pl.when(has_other)
+    def _():
+        greet_one(at_dp(2 * other_z + y))
+    pl.semaphore_wait(barrier, len(steps) + 2 + has_other.astype(jnp.int32))
+
     both = 2 * chunk
     rows_of = (full, head_cols)
     pl.run_scoped(
         feed_phase, pltpu.VMEM(wd_hbm.shape, BF16), pltpu.VMEM((both, width), BF16),
         pltpu.VMEM((both, hidden), F32), pltpu.VMEM((both, hidden), F32),
-        pltpu.VMEM((both, hidden), BF16), pltpu.VMEM((both, hidden), BF16))
+        pltpu.VMEM((both, hidden), BF16), pltpu.VMEM((both, hidden), BF16),
+        pltpu.VMEM((full // ROW_CHUNKS, width), F32))
     at_load(1).wait()
     pl.run_scoped(
         hidden_phase, pltpu.VMEM((2,) + wg_hbm.shape, BF16), pltpu.VMEM((both, hidden), BF16),
@@ -1267,17 +1417,22 @@
         branch_phase, pltpu.VMEM((chunk, width), F32), pltpu.VMEM((chunk, width), BF16),
         pltpu.VMEM((2, both, width), BF16), pltpu.VMEM((2, width, both), BF16),
         pltpu.VMEM(w_out_hbm.shape, BF16), pltpu.VMEM((2, both, head_cols), BF16),
-        pltpu.VMEM((full // ROW_CHUNKS, width), BF16))
+        pltpu.VMEM((full // ROW_CHUNKS, width), BF16), pltpu.VMEM(seg_live_hbm.shape, jnp.int32))
     pl.run_scoped(
         attention_phase, pltpu.VMEM(rows_of, BF16), pltpu.VMEM(rows_of, BF16), pltpu.VMEM(rows_of, BF16),
         pltpu.VMEM(rows_of, BF16), pltpu.VMEM(rows_of, F32), pltpu.VMEM(rows_of, F32),
-        pltpu.VMEM((full, HEAD), F32), pltpu.VMEM(rows_of, F32), pltpu.VMEM((full, full), F32))
+        pltpu.VMEM((full, HEAD), F32), pltpu.VMEM(rows_of, F32), pltpu.VMEM((full, full), BF16),
+        pltpu.VMEM((full, HEAD), F32), pltpu.VMEM(seg_live_hbm.shape, jnp.int32),
+        pltpu.VMEM((full, HEAD), F32), pltpu.VMEM((full, HEAD), F32))
     pl.run_scoped(
         input_phase, pltpu.VMEM((3,) + wq_hbm.shape, BF16), pltpu.VMEM((full, 3 * head_cols), BF16),
         pltpu.VMEM((chunk, width), F32), pltpu.VMEM((2, chunk, width), BF16))
     finish_chunk(jnp.int32(total - 1), jnp.int32(passes - 1))
     out_act(jnp.int32(total - 1), lambda copy: copy.wait())
-    gains_out[...] = vec[...]
+    gains_out[...] = jnp.zeros(gains_out.shape, F32)
+    gains_out[0:8, :] = vec[...]
+    for h in range(2 * head_cols // HEAD):
+        gains_out[8 + h : 9 + h, 0:HEAD] = vec[2:3, h * HEAD : (h + 1) * HEAD]
 
 
 def backward_layer(dp_size, hbm, vmem_args):
@@ -1286,7 +1441,7 @@
     hidden, head_cols = names["inner"].shape[1], names["query"].shape[1]
     line, block = dp_size // 2, width // dp_size
     chunk = row_count // 2 // ROW_CHUNKS
-    counts = (hidden // COLS, 2 * hidden // COLS, 3 * head_cols // COLS, head_cols // COLS)
+    counts = (hidden // COLS, hidden // COLS, 3 * head_cols // COLS, head_cols // COLS)
     DMA, REG = pltpu.SemaphoreType.DMA, pltpu.SemaphoreType.REGULAR
     vmem, any_space = pl.BlockSpec(memory_space=pltpu.VMEM), pl.BlockSpec(memory_space=pl.ANY)
 
@@ -1299,10 +1454,15 @@
     results = pl.pallas_call(
         functools.partial(backward_kernel, dp_size, counts),
         out_shape=(
-            shape((counts[0] + counts[3]) * COLS, block),
-            shape(block, (counts[1] + counts[2]) * COLS),
+            shape(hidden, block),
+            shape(head_cols, block),
+            shape(block, hidden),
+            shape(block, hidden),
+            shape(block, head_cols),
+            shape(block, head_cols),
+            shape(block, head_cols),
             shape(row_count, width, kind=BF16),
-            shape(8, width),
+            shape(8 + 2 * head_cols // HEAD, width),
             shape(row_count, hidden, kind=BF16),
             shape(row_count, hidden, kind=BF16),
             shape(width, row_count, kind=BF16),
@@ -1310,17 +1470,22 @@
             shape(row_count, 3 * head_cols, kind=BF16),
         ),
         in_specs=[any_space] * len(hbm) + [vmem] * len(vmem_args),
-        out_specs=(any_space,) * 3 + (vmem,) + (any_space,) * 5,
+        out_specs=(any_space,) * 8 + (vmem,) + (any_space,) * 5,
         scratch_shapes=[
-            pltpu.VMEM((2, width, row_count), BF16),
+            pltpu.VMEM((3, width, row_count), BF16),
             pltpu.VMEM((B_SLOTS, row_count, COLS), BF16),
+            pltpu.VMEM((row_count, COLS), BF16),
+            pltpu.VMEM((row_count, COLS), BF16),
+            pltpu.VMEM(slot, F32),
             pltpu.VMEM((Y_SLOTS, line) + slot, F32),
             pltpu.VMEM((Y_SLOTS, line) + slot, F32),
+            pltpu.VMEM((Y_SLOTS,) + slot, F32),
+            pltpu.VMEM((Y_SLOTS,) + slot, F32),
             pltpu.VMEM((2, line) + slot, F32),
             pltpu.VMEM((2, line + 1) + slot, F32),
             pltpu.VMEM(slot, F32),
             pltpu.VMEM((COLS, block), F32),
-            pltpu.VMEM((2, chunk, width), F32),
+            pltpu.VMEM((chunk, width), F32),
             pltpu.VMEM((ROW_CHUNKS, chunk, width), F32),
             pltpu.VMEM((ROW_CHUNKS, chunk, width), F32),
             pltpu.VMEM((ROW_CHUNKS, chunk, width), F32),
@@ -1331,19 +1496,23 @@
             pltpu.VMEM((steps + 1, 8, width), F32),
             DMA((2,)),
             DMA((B_SLOTS,)),
+            DMA,
             DMA((Y_SLOTS, line)),
             DMA((Y_SLOTS, line)),
+            DMA((Y_SLOTS,)),
+            DMA((Y_SLOTS,)),
             DMA((2, line)),
             DMA((2, line + 1)),
             DMA,
+            DMA,
         ]
         + [per_chunk] * 12
-        + [DMA((2,)), DMA((2,)), DMA((steps + 1,)), DMA((steps + 1,)), DMA((4,)), DMA((6,)), DMA((8,)), DMA((1,)), DMA((1,)),
+        + [DMA((2,)), DMA((2,)), DMA((steps + 1,)), DMA((steps + 1,)), DMA((4,)), DMA((6,)), DMA((8,)), DMA((1,)), DMA((1,)), DMA((1,)),
            REG, REG, REG],
         compiler_params=pltpu.CompilerParams(
             collective_id=2, has_side_effects=True, vmem_limit_bytes=VMEM_LIMIT),
     )(*hbm, *vmem_args)
-    return results[:4]
+    return results[:9]
 
 
 def rope_tables():
@@ -1393,6 +1562,7 @@
             query_raw,
             key_raw,
             mixed_rows,
+            partner_rows,
             gain_mlp_part,
             inverses,
             log_totals,
@@ -1402,42 +1572,46 @@
             ),
             (seg_live, seg_row, gain_query, gain_key, attn_gain, mlp_gain),
         )
-        turned, straight, grad_tokens, gains = backward_layer(
+        (
+            grad_down,
+            grad_out,
+            grad_gate,
+            grad_up,
+            grad_query,
+            grad_key,
+            grad_value,
+            grad_tokens,
+            gains,
+        ) = backward_layer(
             dp_size,
             (
                 grad_down_turned, hidden_turned, tokens, inner_rows, mixed_rows, grad_down_rows,
                 gate_rows, up_rows, branch_rows, cotangent,
-                query_norm, key_norm, value_rows, query_raw, key_raw,
+                query_norm, key_norm, value_rows, query_raw, key_raw, partner_rows,
+                inverses, seg_live, cosine, sine,
                 w_out, w_gate, w_up, w_down, w_query, w_key, w_value,
             ),
             (
-                inverses, log_totals, seg_live, seg_row, cosine, sine,
-                gain_query, gain_key, attn_gain, gain_mlp_part,
+                log_totals, seg_row, gain_query, gain_key, attn_gain, gain_mlp_part,
             ),
         )
-        hidden, head_cols = w_gate.shape[1], w_query.shape[1]
-        grad_gate, grad_up = straight[:, :hidden], straight[:, hidden : 2 * hidden]
-        grad_query, grad_key, grad_value = (
-            straight[:, 2 * hidden + i * head_cols : 2 * hidden + (i + 1) * head_cols]
-            for i in range(3)
-        )
+        heads, head_block = gain_query.shape[0], HEAD // dp_size
         dp_at = lax.axis_index("dp")
-        wide = lax.dynamic_slice_in_dim(gains[:2], dp_at * block, block, 1)
-        head_gains = gains[2, : 2 * head_cols].reshape(2 * gain_query.shape[0], HEAD)
-        head_gains = lax.dynamic_slice_in_dim(head_gains, dp_at * (HEAD // dp_size), HEAD // dp_size, 1)
+        wide = lax.dynamic_slice(gains, (0, dp_at * block), (2, block))
+        head_gains = lax.dynamic_slice(gains, (8, dp_at * head_block), (2 * heads, head_block))
         return (
             output,
             grad_tokens,
             grad_query,
             grad_key,
             grad_value,
-            turned[hidden:],
-            head_gains[: gain_query.shape[0]],
-            head_gains[gain_query.shape[0] :],
+            grad_out,
+            head_gains[:heads],
+            head_gains[heads:],
             wide[1],
             grad_gate,
             grad_up,
-            turned[:hidden],
+            grad_down,
             wide[0],
         )
 

time: 945 us -> 884 us (0.935)
  Pallas kernels: 910 us -> 854 us
    pallas_call x1, Pallas kernels: 693 us -> 637 us  [backward_layer(): pl.pallas_call(functools.partial(backward_kernel, dp_size, counts), out_s...]
    slice x7 -> x1, local copies, waits for them, and re-layouts: 12.9 us -> 0.59 us  [shards(): head_gains[heads:]]
where the time goes in v5:
time: 884 us; the launch traced here: 878 us
  Pallas kernels  854 us (97%)
  local copies, waits for them, and re-layouts  18 us (2%)
    pallas_call x1, Pallas kernels, backward_layer(): pl.pallas_call(functools.partial(backward_kernel, dp_size, counts), out_s...  637 us
    pallas_call x1, Pallas kernels, forward_layer(): pl.pallas_call(forward_kernel, out_shape=(shape(row_count, hidden), shape...  217 us

profile of v5, /device:TPU:0, one launch (start us, length us, event | category | flops | bytes accessed | tf_op | source)
XLA Modules:
  0.0 877.9 jit_solution(14395596640243005816)
XLA Ops:
  0.6 0.0 copy-start.11
  0.7 0.0 copy-start.8
  0.7 0.0 copy-start.9
  0.7 0.0 copy-start.10
  0.7 2.0 fusion.2
  2.7 1.3 pad_maximum_fusion
  4.0 0.0 copy-done.11
  4.0 0.0 copy-done.8
  4.0 1.0 copy.30.seg_live.seg_live_hbm
  5.0 0.0 copy-done.9
  5.0 0.6 broadcast_in_dim.20
  5.6 0.0 copy-done.10
  5.6 0.6 broadcast_in_dim.21
  6.2 216.8 %shard_map.246 = (f32[1024,2048]{1,0:T(8,128)}, f32[1024,2048]{1,0:T(8,128)}, bf16[1024,2048]{1,0:T(8,128)(2,1)}, bf16[2048,1024]{1,0:T(8,128)(2,1)}, bf16[1024,...) custom-call(bf16[1024,2048]{1,0:T(8,128)(2,1)} %tok_hbm.3, ...), custom_call_target="tpu_custom_call" | custom-call | tf_op jit(solution)/shard_map/pallas_call | solution.py:504
  223.1 637.3 %shard_map.247 = (f32[2048,256]{1,0:T(8,128)}, f32[512,256]{1,0:T(8,128)}, f32[256,2048]{1,0:T(8,128)}, f32[256,2048]{1,0:T(8,128)}, f32[256,512]{1,0:T(8,128)},...) custom-call(bf16[2048,1024]{1,0:T(8,128)(2,1)} %get-tuple-element.41, ...), custom_call_target="tpu_custom_call" | custom-call | tf_op jit(solution)/shard_map/pallas_call | solution.py:1454
  860.4 0.8 constant_dynamic-slice_fusion
  861.2 0.6 fusion.3
  861.8 1.4 constant_dynamic-slice_fusion.1
  863.2 4.9 copy.41
  868.1 0.0 copy-done
  868.1 0.0 copy-start.4
  868.1 0.0 copy-start.3
  868.1 2.1 copy.42
  870.3 0.8 copy.43
  871.1 0.8 copy.44
  871.9 0.8 copy.45
  872.7 0.8 copy.46
  873.5 0.0 copy-done.3
  873.5 1.3 copy.47
  874.8 1.3 copy.48
  876.1 0.0 copy-done.1
  876.1 1.3 copy.49
  (13 shorter events, 0.0 us)
Async XLA Ops:
  0.6 3.3 copy-start.11
  0.7 3.3 copy-start.8
  0.7 4.4 copy-start.9
  0.7 5.0 copy-start.10
  863.2 4.9 copy-start
  868.1 2.2 copy-start.7
  868.1 3.0 copy-start.6
  868.1 3.8 copy-start.5
  868.1 4.6 copy-start.4
  868.1 5.3 copy-start.3
  870.3 4.5 copy-start.2
  873.5 2.6 copy-start.1

commit v6 on v5

--- a/solution.py
+++ b/solution.py
@@ -2,6 +2,7 @@
 
 import jax
 import jax.numpy as jnp
+import numpy as np
 from jax import lax
 from jax.experimental import pallas as pl
 from jax.experimental.pallas import tpu as pltpu
@@ -18,7 +19,7 @@
 
 
 COLS = 256
-LINE_FIRST = (1, 23)
+LINE_FIRST = (1, 5, 23)
 Y_SLOTS = 3
 B_SLOTS = 3
 FEED_TICK = 3
@@ -63,7 +64,7 @@
     gate_out, up_out, inner_out, hlt_out, gdr_out, gdrt_out, branch_out, out_out,
     query_out, key_out, value_out, query_raw_out, key_raw_out, mixed_out, partner_out,
     gain_out, inverse_out, log_out,
-    wg, wu, cs, crecv, xs, xr, xr2, ag, squares, squares_in,
+    wg, cs, crecv, xs, xr, xr2, ag, squares, squares_in,
     w_sem, t_sem, s_sem, a_sem, r_sem, m_sem, sq_s_sem, sq_r_sem, sx_s_sem, sx_r_sem,
     cs_sem, cr_sem, xs_sem, xr_sem, as_sem, ar_sem, cs2_sem, cr2_sem, xs2_sem, xr2_sem,
     gs_sem, gr_sem, os_sem, or_sem, hs_sem, hr_sem, fs_sem, fr_sem, g_sem, h_sem, b_sem, d_sem, o_sem,
@@ -97,10 +98,7 @@
     def row_load(c, src, dst, sem):
         return pltpu.make_async_copy(src.at[own_rows(0, c)], dst.at[c % 2], sem.at[c % 2])
 
-    wide_loads = [
-        pltpu.make_async_copy(src, dst, w_sem.at[i])
-        for i, (src, dst) in enumerate(((wg_hbm, wg), (wu_hbm, wu)))
-    ]
+    wide_loads = [pltpu.make_async_copy(wg_hbm, wg, w_sem.at[0])]
 
     def remote(src, dst, send_sem, recv_sem, peer):
         return pltpu.make_async_remote_copy(
@@ -168,43 +166,29 @@
         squares[c] += squares_in[0, c]
         square_x_copy(c).start()
 
-    def projections(weights, tok, query_raw, key_raw, value, value_turned):
-        def tok_load(c):
-            return pltpu.make_async_copy(
-                tok_hbm.at[pl.ds(c * both, both)], tok.at[c % 2], t_sem.at[c % 2])
-
-        loads = [
-            pltpu.make_async_copy(w, weights.at[i], a_sem.at[i])
-            for i, w in enumerate((wq_hbm, wk_hbm, wv_hbm))
-        ]
-        tok_load(0).start()
-        start(loads)
-        tok_load(1).start()
-        greet({"tensor": sibling}, {"tensor": across}, {"dp": partner})
+    def project(c, weights, loads, tok, tok_load, query_raw, key_raw, value, value_turned):
+        at = slice(c * both, (c + 1) * both)
         lanes = lax.broadcasted_iota(jnp.int32, (both, HEAD), 1)
-        for c in range(ROW_CHUNKS):
-            at = slice(c * both, (c + 1) * both)
-            tok_load(c).wait()
-            if c == 0:
-                loads[0].wait()
-            query_raw[at, :] = jnp.dot(tok[c % 2], weights[0], preferred_element_type=F32)
-            if c == 0:
-                loads[1].wait()
-            key_raw[at, :] = jnp.dot(tok[c % 2], weights[1], preferred_element_type=F32)
-            query_square = jnp.sum(query_raw[at, :] * query_raw[at, :], axis=1, keepdims=True)
-            key_square = jnp.sum(key_raw[at, :] * key_raw[at, :], axis=1, keepdims=True)
-            squares[c] = jnp.where(lanes == 0, query_square, key_square)
-            square_copy(c).start()
-            if c == 0:
-                loads[2].wait()
-                start(wide_loads)
-            value[at, :] = jnp.dot(tok[c % 2], weights[2], preferred_element_type=F32).astype(BF16)
-            value_turned[:, at] = value[at, :].T
-            if c + 2 < ROW_CHUNKS:
-                tok_load(c + 2).start()
-            if c >= 1:
-                square_pass_on(c - 1)
-        square_pass_on(last)
+        tok_load(c).wait()
+        if c == 0:
+            loads[0].wait()
+        query_raw[at, :] = jnp.dot(tok[c % 2], weights[0], preferred_element_type=F32)
+        if c == 0:
+            loads[1].wait()
+        key_raw[at, :] = jnp.dot(tok[c % 2], weights[1], preferred_element_type=F32)
+        query_square = jnp.sum(query_raw[at, :] * query_raw[at, :], axis=1, keepdims=True)
+        key_square = jnp.sum(key_raw[at, :] * key_raw[at, :], axis=1, keepdims=True)
+        squares[c] = jnp.where(lanes == 0, query_square, key_square)
+        square_copy(c).start()
+        if c == 0:
+            loads[2].wait()
+            start(wide_loads)
+        if c == 1:
+            square_pass_on(0)
+        value[at, :] = jnp.dot(tok[c % 2], weights[2], preferred_element_type=F32).astype(BF16)
+        value_turned[:, at] = value[at, :].T
+        if c + 2 < ROW_CHUNKS:
+            tok_load(c + 2).start()
 
     def attend(c, query_raw, key_raw, query, key, value_turned, cosine, sine, w_out, mixed, bias):
         first, keys = c * both, (c + 1) * both
@@ -246,14 +230,15 @@
 
         def mixed_rows(s):
             return pl.ds(pl.multiple_of(jnp.where(core == s, 0, chunk), chunk), chunk)
+        if c + 1 < ROW_CHUNKS:
+            square_pass_on(c + 1)
         if c >= 2:
             core_copy(c - 2).wait_send()
         cs[c % 2] = jnp.dot(mixed[c % 2, mixed_rows(1), :], w_out[...], preferred_element_type=F32)
         core_copy(c).start()
         xs[c] = jnp.dot(mixed[c % 2, mixed_rows(0), :], w_out[...], preferred_element_type=F32)
         start(mixed_copies(c, mixed))
-        if c >= 1:
-            pass_on(c - 1)
+        pass_on(c)
 
     def mixed_copies(c, mixed):
         return [
@@ -268,55 +253,67 @@
         xs[c] += crecv[c]
         x_copy(c).start()
 
-    def attention(query_raw, key_raw, query, key, value, value_turned, cosine, sine, w_out):
+    def attention(
+        query_raw, key_raw, query, key, value, value_turned, cosine, sine, w_out, weights, tok, mixed, bias,
+    ):
+        def tok_load(c):
+            return pltpu.make_async_copy(
+                tok_hbm.at[pl.ds(c * both, both)], tok.at[c % 2], t_sem.at[c % 2])
+
+        loads = [
+            pltpu.make_async_copy(w, weights.at[i], a_sem.at[i])
+            for i, w in enumerate((wq_hbm, wk_hbm, wv_hbm))
+        ]
         tables = [
             pltpu.make_async_copy(src, dst, r_sem.at[i])
             for i, (src, dst) in enumerate(((cos_hbm, cosine), (sin_hbm, sine), (wo_hbm, w_out)))
         ]
+        tok_load(0).start()
+        start(loads)
+        tok_load(1).start()
         start(tables)
-        pl.run_scoped(
-            functools.partial(
-                projections, query_raw=query_raw, key_raw=key_raw, value=value,
-                value_turned=value_turned),
-            pltpu.VMEM((3,) + wq_hbm.shape, BF16), pltpu.VMEM((2, both, width), BF16))
-        finish(tables)
+        greet({"tensor": sibling}, {"tensor": across}, {"dp": partner})
         results = [
             pltpu.make_async_copy(src, dst, a_sem.at[i])
             for i, (src, dst) in enumerate((
                 (value, value_out), (query_raw, query_raw_out), (key_raw, key_raw_out),
                 (query, query_out), (key, key_out)))
         ]
-        start(results[:3])
-
-        def chunks(mixed, bias):
-            for c in range(ROW_CHUNKS):
-                if c >= 2:
-                    finish(mixed_copies(c - 2, mixed))
+        for c in range(ROW_CHUNKS + 1):
+            if c < ROW_CHUNKS:
+                project(c, weights, loads, tok, tok_load, query_raw, key_raw, value, value_turned)
+            if c == 1:
+                finish(tables)
+            if c == last:
+                start(results[:3])
+            if c >= 1:
+                if c >= 3:
+                    finish(mixed_copies(c - 3, mixed))
                 attend(
-                    c, query_raw, key_raw, query, key, value_turned, cosine, sine, w_out, mixed, bias)
-            start(results[3:])
-            pass_on(last)
-            for c in range(last - 1, ROW_CHUNKS):
-                core_copy(c).wait_send()
-                finish(mixed_copies(c, mixed))
-            finish(results)
-        pl.run_scoped(
-            chunks, pltpu.VMEM((2, both, head_cols), BF16), pltpu.VMEM((full, both), F32))
+                    c - 1, query_raw, key_raw, query, key, value_turned, cosine, sine, w_out, mixed, bias)
+        start(results[3:])
+        for c in range(last - 1, ROW_CHUNKS):
+            core_copy(c).wait_send()
+            finish(mixed_copies(c, mixed))
+        finish(results)
 
     rows_of = (full, head_cols)
     pl.run_scoped(
         attention, pltpu.VMEM(rows_of, F32), pltpu.VMEM(rows_of, F32), pltpu.VMEM(rows_of, BF16),
         pltpu.VMEM(rows_of, BF16), pltpu.VMEM(rows_of, BF16), pltpu.VMEM((head_cols, full), BF16),
-        pltpu.VMEM((full, HEAD), F32), pltpu.VMEM((full, HEAD), F32), pltpu.VMEM(wo_hbm.shape, BF16))
+        pltpu.VMEM((full, HEAD), F32), pltpu.VMEM((full, HEAD), F32), pltpu.VMEM(wo_hbm.shape, BF16),
+        pltpu.VMEM((3,) + wq_hbm.shape, BF16), pltpu.VMEM((2, both, width), BF16),
+        pltpu.VMEM((2, both, head_cols), BF16), pltpu.VMEM((full, both), F32))
     pl.run_scoped(
         functools.partial(
             feed_forward, core, chunk, own_rows, row_load, rows, side_copies, turned_copies,
             (x_copy, hidden_copy, core2_copy, x2_copy, grad_copy, out_copy, partner_copy, hand_copy), wide_loads, seg_live,
-            (tok_hbm, cot_hbm, wd_hbm, attn_gain, mlp_gain, wg, wu),
+            (tok_hbm, cot_hbm, wu_hbm, wd_hbm, attn_gain, mlp_gain, wg),
             (gate_out, up_out, inner_out, hlt_out, gdr_out, gdrt_out, branch_out, out_out, gain_out),
             (cs, crecv, xs, xr, xr2, ag),
             (w_sem, t_sem, s_sem, g_sem, h_sem, b_sem, d_sem, o_sem)),
-        pltpu.VMEM(wd_hbm.shape, BF16), pltpu.VMEM((both, hidden), F32), pltpu.VMEM((both, hidden), F32),
+        pltpu.VMEM(wu_hbm.shape, BF16), pltpu.VMEM(wd_hbm.shape, BF16),
+        pltpu.VMEM((both, hidden), F32), pltpu.VMEM((both, hidden), F32),
         pltpu.VMEM((both, hidden), BF16), pltpu.VMEM((both, width), BF16), pltpu.VMEM((width, both), BF16),
         pltpu.VMEM((both, width), BF16), pltpu.VMEM((2, chunk, width), BF16),
         pltpu.VMEM((2, chunk, width), BF16))
@@ -325,16 +322,20 @@
 def feed_forward(
     core, chunk, own_rows, row_load, rows, side_copies, turned_copies, remote_copies, wide_loads, seg_live,
     operands, results, buffers, sems,
-    wd, gate_buf, up_buf, inner_buf, low_buf, hlt_buf, out_buf, tok, seed,
+    wu, wd, gate_buf, up_buf, inner_buf, low_buf, hlt_buf, out_buf, tok, seed,
 ):
     x_copy, hidden_copy, core2_copy, x2_copy, grad_copy, out_copy, partner_copy, hand_copy = remote_copies
-    tok_hbm, cot_hbm, wd_hbm, attn_gain, mlp_gain, wg, wu = operands
+    tok_hbm, cot_hbm, wu_hbm, wd_hbm, attn_gain, mlp_gain, wg = operands
     gate_out, up_out, inner_out, hlt_out, gdr_out, gdrt_out, branch_out, out_out, gain_out = results
     cs, crecv, xs, xr, xr2, ag = buffers
     w_sem, t_sem, s_sem, g_sem, h_sem, b_sem, d_sem, o_sem = sems
     last = ROW_CHUNKS - 1
     tiles, wide_tiles = wg.shape[1] // TILE, wd.shape[1] // TILE
-    loads = wide_loads + [pltpu.make_async_copy(wd_hbm, wd, w_sem.at[2])]
+    loads = wide_loads + [
+        pltpu.make_async_copy(wu_hbm, wu, w_sem.at[1]),
+        pltpu.make_async_copy(wd_hbm, wd, w_sem.at[2]),
+    ]
+    loads[1].start()
     loads[2].start()
     for c in range(2):
         row_load(c, tok_hbm, tok, t_sem).start()
@@ -527,7 +528,6 @@
         out_specs=(any_space,) * 15 + (vmem,) * 3,
         scratch_shapes=[
             pltpu.VMEM(w_gate.shape, BF16),
-            pltpu.VMEM(w_gate.shape, BF16),
             pltpu.VMEM((2, chunk, width), F32),
             pltpu.VMEM((ROW_CHUNKS, chunk, width), F32),
             pltpu.VMEM((ROW_CHUNKS, chunk, width), F32),
@@ -867,6 +867,7 @@
         @pl.when(k >= 1)
         def _():
             finish_chunk(k - 1, q - 1)
+        send_ahead(k)
         own[...] = product(k, 2 * z + y)
 
         @pl.when(is_line_first)
@@ -875,7 +876,6 @@
             ysend[p, z] = product(k, 2 * z + 1 - y)
             line_own(q, ysend.at[p, z])
             y_copy(p, z).start()
-        send_ahead(k)
 
     def pair_tick(k, work):
         p = lax.rem(k, Y_SLOTS)
@@ -889,13 +889,13 @@
         lax.fori_loop(0, line, rows_in, 0)
         line_send(q, k, lambda b: pair_product(k, 2 * b + 1 - y))
         finish_chunk(k - 1, q - 1)
+        send_ahead(k)
         work(q)
         line_send(q + 1, k, lambda b: pair_product(k, 2 * b + y))
         own[...] = pair_product(k, 2 * z + y)
         fsend[p] = pair_product(k, 2 * z + 1 - y)
         line_own(q, fsend.at[p])
         final_copy(p).start()
-        send_ahead(k)
 
     nt = (((1,), (1,)), ((), ()))
 
@@ -1517,10 +1517,10 @@
 
 def rope_tables():
     half_size = HEAD // 2
-    freq_row = ROPE_BASE ** (-(jnp.arange(half_size, dtype=F32) * 2.0) / HEAD)
-    angle = jnp.arange(LENGTH, dtype=F32)[:, None] * freq_row[None, :]
-    cosine, sine = jnp.cos(angle), jnp.sin(angle)
-    return jnp.concatenate((cosine, cosine), 1), jnp.concatenate((-sine, sine), 1)
+    freq_row = ROPE_BASE ** (-(np.arange(half_size, dtype=np.float64) * 2.0) / HEAD)
+    angle = (np.arange(LENGTH, dtype=np.float64)[:, None] * freq_row[None, :]).astype(np.float32)
+    cosine, sine = np.cos(angle), np.sin(angle)
+    return np.concatenate((cosine, cosine), 1), np.concatenate((-sine, sine), 1)
 
 
 def make_shards(dp_size):
@@ -1542,7 +1542,7 @@
         cotangent,
     ):
         block = tokens.shape[1] // dp_size
-        cosine, sine = rope_tables()
+        cosine, sine = (jnp.asarray(table, F32) for table in rope_tables())
         seg_live = jnp.stack((segments, pad_mask), 1)
         seg_row = segments[None, :]
         attn_gain = gain_attn.astype(F32)[None, :]

time: 884 us -> 863 us (0.976)
  Pallas kernels: 854 us -> 838 us
    pallas_call x1, Pallas kernels: 637 us -> 625 us  [backward_layer(): pl.pallas_call(functools.partial(backward_kernel, dp_size, counts), out_s...]
where the time goes in v6:
time: 863 us; the launch traced here: 860 us
  Pallas kernels  838 us (97%)
  local copies, waits for them, and re-layouts  18 us (2%)
    pallas_call x1, Pallas kernels, backward_layer(): pl.pallas_call(functools.partial(backward_kernel, dp_size, counts), out_s...  625 us
    pallas_call x1, Pallas kernels, forward_layer(): pl.pallas_call(forward_kernel, out_shape=(shape(row_count, hidden), shape...  213 us

profile of v6, /device:TPU:0, one launch (start us, length us, event | category | flops | bytes accessed | tf_op | source)
XLA Modules:
  0.0 859.9 jit_solution(13761110703888459217)
XLA Ops:
  0.6 0.7 pad_add_fusion
  1.4 1.0 copy.32.seg_live.seg_live_hbm
  2.4 1.3 broadcast_in_dim.18
  3.7 1.3 broadcast_in_dim.19
  5.0 212.6 %shard_map.264 = (f32[1024,2048]{1,0:T(8,128)}, f32[1024,2048]{1,0:T(8,128)}, bf16[1024,2048]{1,0:T(8,128)(2,1)}, bf16[2048,1024]{1,0:T(8,128)(2,1)}, bf16[1024,...) custom-call(bf16[1024,2048]{1,0:T(8,128)(2,1)} %tok_hbm.3, ...), custom_call_target="tpu_custom_call" | custom-call | tf_op jit(solution)/shard_map/pallas_call | solution.py:505
  217.6 625.0 %shard_map.265 = (f32[2048,256]{1,0:T(8,128)}, f32[512,256]{1,0:T(8,128)}, f32[256,2048]{1,0:T(8,128)}, f32[256,2048]{1,0:T(8,128)}, f32[256,512]{1,0:T(8,128)},...) custom-call(bf16[2048,1024]{1,0:T(8,128)(2,1)} %get-tuple-element.41, ...), custom_call_target="tpu_custom_call" | custom-call | tf_op jit(solution)/shard_map/pallas_call | solution.py:1454
  842.6 0.7 constant_dynamic-slice_fusion
  843.3 0.6 fusion
  843.9 1.4 constant_dynamic-slice_fusion.1
  845.3 0.0 copy-start
  845.3 4.9 copy.43
  850.3 0.0 copy-done
  850.3 0.0 copy-start.7
  850.3 0.0 copy-start.6
  850.3 0.0 copy-start.5
  850.3 0.0 copy-start.4
  850.3 0.0 copy-start.3
  850.3 2.1 copy.44
  852.4 0.0 copy-done.7
  852.4 0.8 copy.45
  853.2 0.0 copy-done.6
  853.2 0.8 copy.46
  854.0 0.0 copy-done.5
  854.0 0.8 copy.47
  854.8 0.0 copy-done.4
  854.8 0.8 copy.48
  855.6 0.0 copy-done.3
  855.6 1.3 copy.49
  856.9 0.0 copy-done.2
  856.9 1.3 copy.50
  858.3 0.0 copy-done.1
  858.3 1.3 copy.51
  (2 shorter events, 0.0 us)
Async XLA Ops:
  845.3 4.9 copy-start
  850.3 2.2 copy-start.7
  850.3 3.0 copy-start.6
  850.3 3.8 copy-start.5
  850.3 4.6 copy-start.4
  850.3 5.3 copy-start.3
  852.4 4.5 copy-start.2
  855.6 2.6 copy-start.1

commit v7 on v6

--- a/solution.py
+++ b/solution.py
@@ -19,7 +19,7 @@
 
 
 COLS = 256
-LINE_FIRST = (1, 5, 23)
+LINE_FIRST = (0, 4)
 Y_SLOTS = 3
 B_SLOTS = 3
 FEED_TICK = 3

time: 863 us -> 848 us (0.983)
  Pallas kernels: 838 us -> 822 us
    pallas_call x1, Pallas kernels: 625 us -> 609 us  [backward_layer(): pl.pallas_call(functools.partial(backward_kernel, dp_size, counts), out_s...]
where the time goes in v7:
time: 848 us; the launch traced here: 844 us
  Pallas kernels  822 us (97%)
  local copies, waits for them, and re-layouts  18 us (2%)
    pallas_call x1, Pallas kernels, backward_layer(): pl.pallas_call(functools.partial(backward_kernel, dp_size, counts), out_s...  609 us
    pallas_call x1, Pallas kernels, forward_layer(): pl.pallas_call(forward_kernel, out_shape=(shape(row_count, hidden), shape...  213 us

profile of v7, /device:TPU:0, one launch (start us, length us, event | category | flops | bytes accessed | tf_op | source)
XLA Modules:
  0.0 844.1 jit_solution(5460134315259953026)
XLA Ops:
  0.6 0.7 pad_add_fusion
  1.4 1.0 copy.32.seg_live.seg_live_hbm
  2.4 1.3 broadcast_in_dim.18
  3.7 1.3 broadcast_in_dim.19
  5.0 212.6 %shard_map.264 = (f32[1024,2048]{1,0:T(8,128)}, f32[1024,2048]{1,0:T(8,128)}, bf16[1024,2048]{1,0:T(8,128)(2,1)}, bf16[2048,1024]{1,0:T(8,128)(2,1)}, bf16[1024,...) custom-call(bf16[1024,2048]{1,0:T(8,128)(2,1)} %tok_hbm.3, ...), custom_call_target="tpu_custom_call" | custom-call | tf_op jit(solution)/shard_map/pallas_call | solution.py:505
  217.6 609.2 %shard_map.265 = (f32[2048,256]{1,0:T(8,128)}, f32[512,256]{1,0:T(8,128)}, f32[256,2048]{1,0:T(8,128)}, f32[256,2048]{1,0:T(8,128)}, f32[256,512]{1,0:T(8,128)},...) custom-call(bf16[2048,1024]{1,0:T(8,128)(2,1)} %get-tuple-element.41, ...), custom_call_target="tpu_custom_call" | custom-call | tf_op jit(solution)/shard_map/pallas_call | solution.py:1454
  826.8 0.7 constant_dynamic-slice_fusion
  827.6 0.6 fusion
  828.2 1.4 constant_dynamic-slice_fusion.1
  829.6 0.0 copy-start
  829.6 4.9 copy.43
  834.5 0.0 copy-done
  834.5 0.0 copy-start.7
  834.5 0.0 copy-start.6
  834.5 0.0 copy-start.5
  834.5 0.0 copy-start.4
  834.5 0.0 copy-start.3
  834.5 2.1 copy.44
  836.7 0.0 copy-done.7
  836.7 0.8 copy.45
  837.5 0.0 copy-done.6
  837.5 0.8 copy.46
  838.3 0.0 copy-done.5
  838.3 0.8 copy.47
  839.1 0.0 copy-done.4
  839.1 0.8 copy.48
  839.9 0.0 copy-done.3
  839.9 1.3 copy.49
  841.2 0.0 copy-done.2
  841.2 1.3 copy.50
  842.5 0.0 copy-done.1
  842.5 1.3 copy.51
  (2 shorter events, 0.0 us)
Async XLA Ops:
  829.6 4.9 copy-start
  834.5 2.2 copy-start.7
  834.5 3.0 copy-start.6
  834.5 3.8 copy-start.5
  834.5 4.6 copy-start.4
  834.5 5.3 copy-start.3
  836.7 4.5 copy-start.2
  839.9 2.6 copy-start.1

commit v8 on v7

--- a/solution.py
+++ b/solution.py
@@ -1003,6 +1003,8 @@
 
         def piece(c):
             finish(loads(c))
+            if c == 0:
+                finish(load_weight)
             if c >= 1:
                 finish(stores(c - 1))
 
@@ -1027,11 +1029,9 @@
         at_load(0).wait()
         pair_send(jnp.int32(0))
         pair_send(jnp.int32(1))
-        finish(load_weight)
-        piece(0)
-        far_turn(0)
-        run_ticks(0, FEED_TICK, {
-            c - 1: [part(piece, c), part(far_turn, c)] for c in range(1, ROW_CHUNKS)})
+        parts = [part(one, c) for c in range(ROW_CHUNKS) for one in (piece, far_turn)]
+        cuts = [0, 3, 5, len(parts)]
+        run_ticks(0, FEED_TICK, {k: parts[cuts[k] : cuts[k + 1]] for k in range(FEED_TICK)})
         finish(stores(ROW_CHUNKS - 1))
 
     def hidden_phase(weights, ggr, gur):

time: 848 us -> 847 us (level)
  no operation moved by 1% of the time
where the time goes in v8:
time: 847 us; the launch traced here: 844 us
  Pallas kernels  822 us (97%)
  local copies, waits for them, and re-layouts  18 us (2%)
    pallas_call x1, Pallas kernels, backward_layer(): pl.pallas_call(functools.partial(backward_kernel, dp_size, counts), out_s...  609 us
    pallas_call x1, Pallas kernels, forward_layer(): pl.pallas_call(forward_kernel, out_shape=(shape(row_count, hidden), shape...  213 us

profile of v8, /device:TPU:0, one launch (start us, length us, event | category | flops | bytes accessed | tf_op | source)
XLA Modules:
  0.0 844.0 jit_solution(4823447342958013230)
XLA Ops:
  0.6 0.7 pad_add_fusion
  1.4 1.0 copy.32.seg_live.seg_live_hbm
  2.4 1.3 broadcast_in_dim.18
  3.7 1.3 broadcast_in_dim.19
  5.0 212.6 %shard_map.264 = (f32[1024,2048]{1,0:T(8,128)}, f32[1024,2048]{1,0:T(8,128)}, bf16[1024,2048]{1,0:T(8,128)(2,1)}, bf16[2048,1024]{1,0:T(8,128)(2,1)}, bf16[1024,...) custom-call(bf16[1024,2048]{1,0:T(8,128)(2,1)} %tok_hbm.3, ...), custom_call_target="tpu_custom_call" | custom-call | tf_op jit(solution)/shard_map/pallas_call | solution.py:505
  217.6 609.1 %shard_map.265 = (f32[2048,256]{1,0:T(8,128)}, f32[512,256]{1,0:T(8,128)}, f32[256,2048]{1,0:T(8,128)}, f32[256,2048]{1,0:T(8,128)}, f32[256,512]{1,0:T(8,128)},...) custom-call(bf16[2048,1024]{1,0:T(8,128)(2,1)} %get-tuple-element.41, ...), custom_call_target="tpu_custom_call" | custom-call | tf_op jit(solution)/shard_map/pallas_call | solution.py:1454
  826.7 0.7 constant_dynamic-slice_fusion
  827.5 0.6 fusion
  828.0 1.4 constant_dynamic-slice_fusion.1
  829.5 0.0 copy-start
  829.5 4.9 copy.43
  834.4 0.0 copy-done
  834.4 0.0 copy-start.7
  834.4 0.0 copy-start.6
  834.4 0.0 copy-start.5
  834.4 0.0 copy-start.4
  834.4 0.0 copy-start.3
  834.4 2.1 copy.44
  836.6 0.0 copy-done.7
  836.6 0.8 copy.45
  837.4 0.0 copy-done.6
  837.4 0.8 copy.46
  838.2 0.0 copy-done.5
  838.2 0.8 copy.47
  839.0 0.0 copy-done.4
  839.0 0.8 copy.48
  839.8 0.0 copy-done.3
  839.8 1.3 copy.49
  841.1 0.0 copy-done.2
  841.1 1.3 copy.50
  842.4 0.0 copy-done.1
  842.4 1.3 copy.51
  (2 shorter events, 0.0 us)
Async XLA Ops:
  829.5 4.9 copy-start
  834.4 2.2 copy-start.7
  834.4 3.0 copy-start.6
  834.4 3.8 copy-start.5
  834.4 4.6 copy-start.4
  834.4 5.3 copy-start.3
  836.6 4.5 copy-start.2
  839.8 2.6 copy-start.1
